TPU v7x, 256 devices: a whole 4x4x8 slice. The times are simulated.
256 devices in a mesh: blk: 64 (over z, y, core), grp: 4 (over x).
Axes of the slice: x: 4, y: 4, z: 8, core: 2. Of those that a mesh axis runs over, the one named last changes fastest.
Arguments:
- source_points: bfloat16 [524288, 64], P(('blk', 'grp')), may hold values from -6 to 6
- target_points: bfloat16 [524288, 64], P('blk'), may hold values from -6 to 6
- source_logw: float32 [524288], P(('blk', 'grp')), may hold values from -1 to 1
- target_logw: float32 [524288], P('blk'), may hold values from -1 to 1
- source_feats: bfloat16 [524288, 128], P(('blk', 'grp')), may hold values from -4 to 4
- target_feats: bfloat16 [524288, 128], P('blk'), may hold values from -4 to 4
- pair_owner: int32 [2048, 7], P(('blk', 'grp')), may hold values from 0 to 63, all different within a row; in each aligned block of 8 rows (0 to 7, 8 to 15, ...) at most 2 rows name the same one
- pair_slot: int32 [2048, 7], P(('blk', 'grp')), may hold values from 0 to 31
Outputs:
- moved_source: bfloat16 [524288, 128], P(('blk', 'grp'))
- moved_target: bfloat16 [524288, 128], P(('blk', 'grp'))
Inputs may be any that keep to these rules, and one draw needn't show every extreme that they name: `pair_owner`: each row names 7 different owners. Within the rows of one device no owner is named more than 2 times, a bound that some block reaches.
All inputs are finite; a program needn't handle non-finite values.
Results may differ from a plain program's by a relative error of at most 0.0057.
Values may be sent and summed in bfloat16 or wider, within the bound.
A program may use at most 128 MiB of HBM per device.

v0:
```python
import jax
import jax.numpy as jnp
from jax import lax
from jax.sharding import PartitionSpec as P

ROUNDS = 2


smoothing = 0.05
lowest = -1e30


def combined_all(part, axis, combine):
    gathered = jax.tree.map(lambda a: lax.all_gather(a, axis), part)

    def take(source):
        return jax.tree.map(lambda a: lax.dynamic_index_in_dim(a, source, 0, False), gathered)

    return lax.fori_loop(
        1, lax.axis_size(axis), lambda source, state: combine(state, take(source)), take(0)
    )


def block_cost(points, squares, targets, target_squares, width):
    inner = jnp.einsum("id,kjd->kij", points, targets, preferred_element_type=jnp.float32)
    return (squares[None, :, None] + target_squares[:, None, :] - 2.0 * inner) * (0.5 / width)


def squares_of(values):
    widened = values.astype(jnp.float32)
    return jnp.sum(widened * widened, axis=-1)


def combine(first, second):
    upper = jnp.maximum(first[0], second[0])
    return (upper, first[1] * jnp.exp(first[0] - upper) + second[1] * jnp.exp(second[0] - upper))


def shards(
    source_points,
    target_points,
    source_logw,
    target_logw,
    source_feats,
    target_feats,
    pair_owner,
    pair_slot,
):
    owners_count = lax.axis_size("blk")
    group_index = lax.axis_index("grp")
    dev_blocks, neighbours = pair_owner.shape
    block = source_points.shape[0] // dev_blocks
    width = source_points.shape[1]
    features = source_feats.shape[1]
    owner_blocks = target_points.shape[0] // block
    capacity = max(2, (dev_blocks * neighbours + owners_count - 1) // owners_count)
    slots = owners_count * capacity
    pairs = dev_blocks * neighbours
    own_start = group_index * dev_blocks
    owners = pair_owner.reshape(pairs)
    wanted = pair_slot.reshape(pairs)
    marks = (owners[:, None] == jnp.arange(owners_count, dtype=jnp.int32)[None, :]).astype(
        jnp.int32
    )
    earlier = jnp.cumsum(marks, axis=0) - marks
    position = owners * capacity + jnp.sum(earlier * marks, axis=1)
    request = (
        jnp.zeros((slots,), jnp.int32).at[position].set(wanted).reshape(owners_count, capacity)
    )
    owned_points = target_points.reshape(owner_blocks, block, width)
    owned_feats = target_feats.reshape(owner_blocks, block, features)
    owned_weights = target_logw.reshape(owner_blocks, block)
    asked_here = lax.all_to_all(request, "blk", split_axis=0, concat_axis=0, tiled=True)
    sent_points = lax.all_to_all(
        owned_points[asked_here], "blk", split_axis=0, concat_axis=0, tiled=True
    )
    fetched = (sent_points, asked_here)
    fetched_points, asked = fetched

    def per_pair(received, tail):
        flat = received.reshape((slots,) + tail)
        return flat[position].reshape((dev_blocks, neighbours) + tail)

    def with_own(own_rows, remote):
        diagonal = lax.dynamic_slice_in_dim(own_rows, own_start, dev_blocks, 0)
        return jnp.concatenate([diagonal[:, None], remote], axis=1)

    def spread(values, fill, dtype):
        remote = values[:, 1:].reshape((pairs,) + values.shape[2:])
        buffer = (
            jnp.full((slots,) + values.shape[2:], fill, dtype)
            .at[position]
            .set(remote.astype(dtype))
        )
        return buffer.reshape((owners_count, capacity) + values.shape[2:])

    def place_own(values, fill):
        base = jnp.full((owner_blocks,) + values.shape[1:], fill, values.dtype)
        return lax.dynamic_update_slice_in_dim(base, values, own_start, 0)

    target_sets = with_own(owned_points, per_pair(fetched_points, (block, width)))
    target_squares = squares_of(target_sets)
    source_blocks = source_points.reshape(dev_blocks, block, width)
    source_squares = squares_of(source_blocks)
    source_weights = source_logw.reshape(dev_blocks, block)
    asked_flat = asked.reshape(slots)
    matches = asked_flat[None, :] == jnp.arange(owner_blocks, dtype=jnp.int32)[:, None]

    def row_pass(inputs):
        points, squares, targets, target_sq, potential, weights = inputs
        cost = block_cost(points, squares, targets, target_sq, width)
        scores = (potential[:, None, :] - cost) / smoothing
        peak = jnp.max(scores, axis=(0, 2))
        total = jnp.sum(jnp.exp(scores - peak[None, :, None]), axis=(0, 2))
        return smoothing * (weights - peak - jnp.log(total))

    def column_pass(inputs):
        points, squares, targets, target_sq, potential_row = inputs
        cost = block_cost(points, squares, targets, target_sq, width)
        scores = (potential_row[None, :, None] - cost) / smoothing
        peak = jnp.max(scores, axis=1)
        total = jnp.sum(jnp.exp(scores - peak[:, None, :]), axis=1)
        return (peak, total)

    potential_pairs = jnp.zeros((dev_blocks, neighbours + 1, block), jnp.float32)
    lse_pairs = jnp.zeros((dev_blocks, neighbours + 1, block), jnp.float32)
    source_pot = jnp.zeros((dev_blocks, block), jnp.float32)
    for sweep in range(ROUNDS):
        source_pot = lax.map(
            row_pass,
            (
                source_blocks,
                source_squares,
                target_sets,
                target_squares,
                potential_pairs,
                source_weights,
            ),
        )
        peaks, totals = lax.map(
            column_pass, (source_blocks, source_squares, target_sets, target_squares, source_pot)
        )
        got_peaks, got_totals = (
            lax.all_to_all(
                spread(peaks, lowest, jnp.float32), "blk", split_axis=0, concat_axis=0, tiled=True
            ),
            lax.all_to_all(
                spread(totals, 0.0, jnp.float32), "blk", split_axis=0, concat_axis=0, tiled=True
            ),
        )
        got_peaks = got_peaks.reshape(slots, block)
        got_totals = got_totals.reshape(slots, block)
        own_peaks = place_own(peaks[:, 0], lowest)
        own_totals = place_own(totals[:, 0], 0.0)
        upper = jnp.max(jnp.where(matches[:, :, None], got_peaks[None], lowest), axis=1)
        upper = jnp.maximum(upper, own_peaks)
        scaled = got_totals[None] * jnp.exp(got_peaks[None] - upper[:, None, :])
        summed = jnp.sum(jnp.where(matches[:, :, None], scaled, 0.0), axis=1)
        summed = summed + own_totals * jnp.exp(own_peaks - upper)
        upper, summed = combined_all((upper, summed), "grp", combine)
        column_lse = upper + jnp.log(summed)
        owner_pot = smoothing * (owned_weights - column_lse)
        back_pot, back_lse = (
            lax.all_to_all(owner_pot[asked], "blk", split_axis=0, concat_axis=0, tiled=True),
            lax.all_to_all(column_lse[asked], "blk", split_axis=0, concat_axis=0, tiled=True),
        )
        potential_pairs = with_own(owner_pot, per_pair(back_pot, (block,)))
        lse_pairs = with_own(column_lse, per_pair(back_lse, (block,)))
    fetched_feats = lax.all_to_all(
        owned_feats[asked], "blk", split_axis=0, concat_axis=0, tiled=True
    )
    feature_sets = with_own(owned_feats, per_pair(fetched_feats, (block, features)))
    source_feat_blocks = source_feats.reshape(dev_blocks, block, features)

    def transport(inputs):
        (
            points,
            squares,
            targets,
            target_sq,
            potential,
            lse_row,
            potential_row,
            target_feat_set,
            own_feats,
        ) = inputs
        cost = block_cost(points, squares, targets, target_sq, width)
        scores = (potential[:, None, :] - cost) / smoothing
        peak = jnp.max(scores, axis=(0, 2))
        expo = jnp.exp(scores - peak[None, :, None])
        denom = jnp.sum(expo, axis=(0, 2))
        mixed = jnp.einsum(
            "kij,kjf->if",
            expo.astype(jnp.bfloat16),
            target_feat_set,
            preferred_element_type=jnp.float32,
        )
        moved_row = (mixed / denom[:, None]).astype(jnp.bfloat16)
        column_weights = jnp.exp(
            (potential_row[None, :, None] - cost) / smoothing - lse_row[:, None, :]
        ).astype(jnp.bfloat16)
        parts = jnp.einsum(
            "kij,if->kjf", column_weights, own_feats, preferred_element_type=jnp.float32
        ).astype(jnp.bfloat16)
        return (moved_row, parts)

    moved_rows, parts = lax.map(
        transport,
        (
            source_blocks,
            source_squares,
            target_sets,
            target_squares,
            potential_pairs,
            lse_pairs,
            source_pot,
            feature_sets,
            source_feat_blocks,
        ),
    )
    moved_source = moved_rows.reshape(dev_blocks * block, features)
    got_parts = lax.all_to_all(
        spread(parts, 0.0, jnp.bfloat16), "blk", split_axis=0, concat_axis=0, tiled=True
    )
    collected = jnp.dot(
        matches.astype(jnp.bfloat16),
        got_parts.reshape(slots, block * features),
        preferred_element_type=jnp.float32,
    )
    own_parts = place_own(
        parts[:, 0].astype(jnp.float32).reshape(dev_blocks, block * features), 0.0
    )
    totals_all = (collected + own_parts).reshape(owner_blocks * block, features)
    moved_target = lax.psum_scatter(totals_all, "grp", scatter_dimension=0, tiled=True).astype(
        jnp.bfloat16
    )
    return (moved_source, moved_target)


def solution(mesh):
    return jax.shard_map(
        shards,
        mesh=mesh,
        in_specs=(
            P(("blk", "grp"), None),
            P("blk", None),
            P(("blk", "grp")),
            P("blk"),
            P(("blk", "grp"), None),
            P("blk", None),
            P(("blk", "grp"), None),
            P(("blk", "grp"), None),
        ),
        out_specs=(P(("blk", "grp"), None), P(("blk", "grp"), None)),
        check_vma=False,
    )
```

profile of v0, /device:TPU:1, one launch (start us, length us, event | category | flops | bytes accessed | tf_op | source)
XLA Modules:
  0.0 923.6 jit_solution(3731902167799342196)
XLA Ops:
  11.5 13.2 %all-to-all-start = ((s32[64,1,2]{2,1,0:T(1,128)}), s32[64,1,2]{2,1,0:T(1,128)S(1)}, u32[]{:S(2)}, u32[]{:S(2)}) async-start(s32[64,1,2]{2,1,0:T(1,128)} %bitcast.56), calls=%async_computation | async-start | bytes 65536 | tf_op jit(solution)/shard_map/all_to_all | solution.py:73
  26.0 8.0 all-to-all-done
  47.5 90.1 %all-to-all-done.1 = bf16[64,2,256,64]{2,3,1,0:T(8,128)(2,1)} async-done(((bf16[64,2,256,64]{2,3,1,0:T(8,128)(2,1)}), bf16[64,2,256,64]{2,3,1,0:T(8,128)(2,1)}, u32[]{:S(2)}, u32[]{:S(2)}) %all-to-all-start.1) | async-done | bytes 4194336 | tf_op jit(solution)/shard_map/all_to_all | solution.py:74
  145.6 17.0 %while.90 = (s32[]{:T(128)}, f32[8,256]{1,0:T(8,128)S(1)}, f32[8,256]{1,0:T(8,128)S(1)}, f32[8,256]{1,0:T(8,128)S(1)}, f32[8,8,256]{2,1,0:T(8,128)S(1)}, /*index...) while((s32[]{:T(128)}, f32[8,256]{1,0:T(8,128)S(1)}, ...), condition=%wide.region_8.9_spmd, body=%wide.region_5.8_spmd.sunk | while | flops 71827712 | bytes 4529269 | solution.py:129
  162.7 16.4 %while.91 = (s32[]{:T(128)}, f32[8,8,256]{2,1,0:T(8,128)S(1)}, f32[8,8,256]{2,1,0:T(8,128)S(1)}, f32[8,256]{1,0:T(8,128)S(1)}, f32[8,256]{1,0:T(8,128)S(1)}, /*i...) while((s32[]{:T(128)}, f32[8,8,256]{2,1,0:T(8,128)S(1)}, ...), condition=%wide.region_12.13_spmd, body=%wide.region_9.12_spmd.sunk | while | flops 71823360 | bytes 4578421 | solution.py:140
  189.3 9.4 %all-to-all-done.2 = f32[64,2,256]{2,1,0:T(2,128)S(1)} async-done(((f32[64,2,256]{2,1,0:T(2,128)}), f32[64,2,256]{2,1,0:T(2,128)S(1)}, u32[]{:S(2)}, u32[]{:S(2)}) %all-to-all-start.2) | async-done | bytes 131104 | tf_op jit(solution)/shard_map/all_to_all | solution.py:144
  204.4 10.2 %all-gather = f32[128,256]{1,0:T(8,128)S(1)} all-gather(f32[32,256]{1,0:T(8,128)S(1)} %max.26), channel_id=2, replica_groups=mesh['blk'=64,'grp'=4] {'grp'}, dimensions={0}, use_global_device_ids=true | all-gather | bytes 163840 | tf_op jit(solution)/shard_map/all_gather | solution.py:14
  216.0 9.4 %all-gather.1 = f32[128,256]{1,0:T(8,128)S(1)} all-gather(f32[32,256]{1,0:T(8,128)S(1)} %multiply_add_fusion.1), channel_id=3, replica_groups=mesh['blk'=64,'grp'=4] {'grp'}, dimensions={0}, use_global_device_ids=true | all-gather | bytes 163840 | tf_op jit(solution)/shard_map/all_gather | solution.py:14
  227.1 15.6 %all-to-all-start.4 = ((f32[64,2,256]{2,1,0:T(2,128)}), f32[64,2,256]{2,1,0:T(2,128)S(1)}, u32[]{:S(2)}, u32[]{:S(2)}) async-start(f32[64,2,256]{2,1,0:T(2,128)} %reshape.293), calls=%async_computation.4 | async-start | bytes 262144 | tf_op jit(solution)/shard_map/all_to_all | solution.py:164
  242.8 11.1 %all-to-all-done.4 = f32[64,2,256]{2,1,0:T(2,128)S(1)} async-done(((f32[64,2,256]{2,1,0:T(2,128)}), f32[64,2,256]{2,1,0:T(2,128)S(1)}, u32[]{:S(2)}, u32[]{:S(2)}) %all-to-all-start.4) | async-done | bytes 131104 | tf_op jit(solution)/shard_map/all_to_all | solution.py:164
  254.6 18.5 %while.93 = (s32[]{:T(128)}, f32[8,256]{1,0:T(8,128)S(1)}, f32[8,256]{1,0:T(8,128)S(1)}, f32[8,8,256]{2,1,0:T(8,128)S(1)}, f32[8,256]{1,0:T(8,128)S(1)}, /*index...) while((s32[]{:T(128)}, f32[8,256]{1,0:T(8,128)S(1)}, ...), condition=%wide.region_22.23_spmd, body=%wide.region_19.22_spmd.sunk | while | flops 71827712 | bytes 4553853 | solution.py:129
  273.2 16.4 %while.94 = (s32[]{:T(128)}, f32[8,8,256]{2,1,0:T(8,128)S(1)}, f32[8,8,256]{2,1,0:T(8,128)S(1)}, f32[8,256]{1,0:T(8,128)S(1)}, f32[8,256]{1,0:T(8,128)S(1)}, /*i...) while((s32[]{:T(128)}, f32[8,8,256]{2,1,0:T(8,128)S(1)}, ...), condition=%wide.region_26.27_spmd, body=%wide.region_23.26_spmd.sunk | while | flops 71823360 | bytes 4578421 | solution.py:140
  297.3 9.7 %all-to-all-done.5 = f32[64,2,256]{2,1,0:T(2,128)S(1)} async-done(((f32[64,2,256]{2,1,0:T(2,128)}), f32[64,2,256]{2,1,0:T(2,128)S(1)}, u32[]{:S(2)}, u32[]{:S(2)}) %all-to-all-start.5) | async-done | bytes 131104 | tf_op jit(solution)/shard_map/all_to_all | solution.py:144
  312.6 10.0 %all-gather.2 = f32[128,256]{1,0:T(8,128)S(1)} all-gather(f32[32,256]{1,0:T(8,128)S(1)} %max.27), channel_id=4, replica_groups=mesh['blk'=64,'grp'=4] {'grp'}, dimensions={0}, use_global_device_ids=true | all-gather | bytes 163840 | tf_op jit(solution)/shard_map/all_gather | solution.py:14
  324.2 9.1 all-gather.3
  335.0 15.1 %all-to-all-start.7 = ((f32[64,2,256]{2,1,0:T(2,128)}), f32[64,2,256]{2,1,0:T(2,128)S(1)}, u32[]{:S(2)}, u32[]{:S(2)}) async-start(f32[64,2,256]{2,1,0:T(2,128)} %reshape.309), calls=%async_computation.7 | async-start | bytes 262144 | tf_op jit(solution)/shard_map/all_to_all | solution.py:164
  351.6 9.6 %all-to-all-done.7 = f32[64,2,256]{2,1,0:T(2,128)S(1)} async-done(((f32[64,2,256]{2,1,0:T(2,128)}), f32[64,2,256]{2,1,0:T(2,128)S(1)}, u32[]{:S(2)}, u32[]{:S(2)}) %all-to-all-start.7) | async-done | bytes 131104 | tf_op jit(solution)/shard_map/all_to_all | solution.py:164
  384.6 180.7 %all-to-all-done.8 = bf16[64,2,256,128]{3,2,1,0:T(8,128)(2,1)} async-done(((bf16[64,2,256,128]{3,2,1,0:T(8,128)(2,1)}), bf16[64,2,256,128]{3,2,1,0:T(8,128)(2,1)}, u32[]{:S(2)}, u32[]{:S(2)}) %all-to-all-start.8) | async-done | bytes 8388640 | tf_op jit(solution)/shard_map/all_to_all | solution.py:169
  575.9 56.9 %while.96 = (s32[]{:T(128)}, bf16[8,256,128]{2,1,0:T(8,128)(2,1)}, bf16[8,8,256,128]{3,2,1,0:T(8,128)(2,1)}, f32[8,8,256]{2,1,0:T(8,128)S(1)}, f32[8,256]{1,0:T(...) while((s32[]{:T(128)}, bf16[8,256,128]{2,1,0:T(8,128)(2,1)}, ...), condition=%wide.region_36.37_spmd, body=%wide.region_33.36_spmd.sunk | while | flops 345832960 | bytes 9967761 | solution.py:207
  642.4 11.7 %scatter_fusion = bf16[128,256,128]{2,1,0:T(8,128)(2,1)} fusion(bf16[128,256,128]{2,1,0:T(8,128)(2,1)} %broadcast_in_dim.161, s32[56]{0:T(128)S(1)} %fusion.88, bf16[56,256,128]{2,1,0:T(8,128)(2,1)} %bitcast.335), kind=kCustom, calls=%fused_computation.15 | custom fusion | bytes 11010272 | tf_op jit(solution)/shard_map/scatter | solution.py:93
  654.0 10.2 %all-to-all-start.10 = ((bf16[64,2,256,128]{3,2,1,0:T(8,128)(2,1)}), bf16[64,2,256,128]{3,2,1,0:T(8,128)(2,1)}, u32[]{:S(2)}, u32[]{:S(2)}) async-start(bf16[64,2,256,128]{3,2,1,0:T(8,128)(2,1)} %bitcast.330), calls=%async_computation.10 | async-start | bytes 16777216 | tf_op jit(solution)/shard_map/all_to_all | solution.py:222
  665.7 181.0 %all-to-all-done.10 = bf16[64,2,256,128]{3,2,1,0:T(8,128)(2,1)} async-done(((bf16[64,2,256,128]{3,2,1,0:T(8,128)(2,1)}), bf16[64,2,256,128]{3,2,1,0:T(8,128)(2,1)}, u32[]{:S(2)}, u32[]{:S(2)}) %all-to-all-start.10) | async-done | bytes 8388640 | tf_op jit(solution)/shard_map/all_to_all | solution.py:222
  846.7 10.4 %fusion.71 = f32[32,32768]{1,0:T(8,128)} fusion(bf16[16,8,256,128]{3,2,1,0:T(8,128)(2,1)} %bitcast.89, s32[128]{0:T(128)S(1)} %eq.38), kind=kOutput, calls=%fused_computation.128 | convolution fusion | flops 268439552 | bytes 12583424 | tf_op jit(solution)/shard_map/dot_general | solution.py:225
  864.8 49.6 %reduce-scatter.2.cloned.1.call-done = f32[2048,128]{1,0:T(8,128)} async-done(((f32[8192,128]{1,0:T(8,128)}), f32[2048,128]{1,0:T(8,128)}) %reduce-scatter.2.cloned.1.call-update) | async-done | bytes 1048592 | tf_op jit(solution)/shard_map/reduce_scatter | solution.py:234
  (420 shorter events, 242.8 us)
Async XLA Ops:
  7.2 358.5 %copy-start = (bf16[8192,128]{1,0:T(8,128)(2,1)S(1)}, bf16[8192,128]{1,0:T(8,128)(2,1)}, u32[]{:S(2)}) copy-start(bf16[8192,128]{1,0:T(8,128)(2,1)} %param.27) | copy-start | bytes 6291460
  11.5 22.5 %all-to-all-start = ((s32[64,1,2]{2,1,0:T(1,128)}), s32[64,1,2]{2,1,0:T(1,128)S(1)}, u32[]{:S(2)}, u32[]{:S(2)}) async-start(s32[64,1,2]{2,1,0:T(1,128)} %bitcast.56), calls=%async_computation | async-start | bytes 65536 | tf_op jit(solution)/shard_map/all_to_all | solution.py:73
  37.1 5.9 copy-start.7
  37.1 5.9 copy-start.4
  37.1 6.0 copy-start.6
  37.1 6.7 copy-start.3
  37.1 100.5 %all-to-all-start.1 = ((bf16[64,2,256,64]{2,3,1,0:T(8,128)(2,1)}), bf16[64,2,256,64]{2,3,1,0:T(8,128)(2,1)}, u32[]{:S(2)}, u32[]{:S(2)}) async-start(bf16[64,2,256,64]{2,3,1,0:T(8,128)(2,1)} %bitcast.331), calls=%async_computation.1 | async-start | bytes 8388608 | tf_op jit(solution)/shard_map/all_to_all | solution.py:74
  141.8 2.3 copy-start.2
  144.1 1.5 copy-start.5
  180.7 18.1 %all-to-all-start.2 = ((f32[64,2,256]{2,1,0:T(2,128)}), f32[64,2,256]{2,1,0:T(2,128)S(1)}, u32[]{:S(2)}, u32[]{:S(2)}) async-start(f32[64,2,256]{2,1,0:T(2,128)} %reshape.253), calls=%async_computation.2 | async-start | bytes 262144 | tf_op jit(solution)/shard_map/all_to_all | solution.py:144
  198.8 15.8 %all-to-all-start.3 = ((f32[64,2,256]{2,1,0:T(2,128)}), f32[64,2,256]{2,1,0:T(2,128)S(1)}, u32[]{:S(2)}, u32[]{:S(2)}) async-start(f32[64,2,256]{2,1,0:T(2,128)} %reshape.255), calls=%async_computation.3 | async-start | bytes 262144 | tf_op jit(solution)/shard_map/all_to_all | solution.py:147
  227.1 26.7 %all-to-all-start.4 = ((f32[64,2,256]{2,1,0:T(2,128)}), f32[64,2,256]{2,1,0:T(2,128)S(1)}, u32[]{:S(2)}, u32[]{:S(2)}) async-start(f32[64,2,256]{2,1,0:T(2,128)} %reshape.293), calls=%async_computation.4 | async-start | bytes 262144 | tf_op jit(solution)/shard_map/all_to_all | solution.py:164
  291.2 15.8 %all-to-all-start.5 = ((f32[64,2,256]{2,1,0:T(2,128)}), f32[64,2,256]{2,1,0:T(2,128)S(1)}, u32[]{:S(2)}, u32[]{:S(2)}) async-start(f32[64,2,256]{2,1,0:T(2,128)} %reshape.259), calls=%async_computation.5 | async-start | bytes 262144 | tf_op jit(solution)/shard_map/all_to_all | solution.py:144
  307.0 15.8 %all-to-all-start.6 = ((f32[64,2,256]{2,1,0:T(2,128)}), f32[64,2,256]{2,1,0:T(2,128)S(1)}, u32[]{:S(2)}, u32[]{:S(2)}) async-start(f32[64,2,256]{2,1,0:T(2,128)} %reshape.261), calls=%async_computation.6 | async-start | bytes 262144 | tf_op jit(solution)/shard_map/all_to_all | solution.py:147
  335.0 26.3 %all-to-all-start.7 = ((f32[64,2,256]{2,1,0:T(2,128)}), f32[64,2,256]{2,1,0:T(2,128)S(1)}, u32[]{:S(2)}, u32[]{:S(2)}) async-start(f32[64,2,256]{2,1,0:T(2,128)} %reshape.309), calls=%async_computation.7 | async-start | bytes 262144 | tf_op jit(solution)/shard_map/all_to_all | solution.py:164
  361.2 15.8 %all-to-all-start.9 = ((f32[64,2,256]{2,1,0:T(2,128)}), f32[64,2,256]{2,1,0:T(2,128)S(1)}, u32[]{:S(2)}, u32[]{:S(2)}) async-start(f32[64,2,256]{2,1,0:T(2,128)} %reshape.341), calls=%async_computation.9 | async-start | bytes 262144 | tf_op jit(solution)/shard_map/all_to_all | solution.py:165
  377.0 188.2 %all-to-all-start.8 = ((bf16[64,2,256,128]{3,2,1,0:T(8,128)(2,1)}), bf16[64,2,256,128]{3,2,1,0:T(8,128)(2,1)}, u32[]{:S(2)}, u32[]{:S(2)}) async-start(bf16[64,2,256,128]{3,2,1,0:T(8,128)(2,1)} %bitcast.332), calls=%async_computation.8 | async-start | bytes 16777216 | tf_op jit(solution)/shard_map/all_to_all | solution.py:169
  654.0 192.6 %all-to-all-start.10 = ((bf16[64,2,256,128]{3,2,1,0:T(8,128)(2,1)}), bf16[64,2,256,128]{3,2,1,0:T(8,128)(2,1)}, u32[]{:S(2)}, u32[]{:S(2)}) async-start(bf16[64,2,256,128]{3,2,1,0:T(8,128)(2,1)} %bitcast.330), calls=%async_computation.10 | async-start | bytes 16777216 | tf_op jit(solution)/shard_map/all_to_all | solution.py:222
  664.3 250.2 %reduce-scatter.2.cloned.1.call-start = ((), (), s32[]{:S(2)}) async-start(), calls=%async_computation.12 | async-start | bytes 5242880 | tf_op jit(solution)/shard_map/reduce_scatter | solution.py:234
  864.8 51.7 %copy-start.1 = (bf16[8192,128]{1,0:T(8,128)(2,1)S(1)}, bf16[8192,128]{1,0:T(8,128)(2,1)}, u32[]{:S(2)}) copy-start(bf16[8192,128]{1,0:T(8,128)(2,1)} %param.27) | copy-start | bytes 6291460
Sparse Core Ops, SparseCore 0:
  865.0 49.4 reduce-scatter.1
where the time goes:
time: 935 us; the launch traced here: 924 us
  waiting for transfers between devices  554 us (59%)
  matrix products  117 us (13%)
  starting transfers between devices  90.8 us (10%)
  local copies, waits for them, and re-layouts  69.8 us (7%)
  blocking collectives  38.7 us (4%)
  other arithmetic  35.7 us (4%)
  between operations  15.1 us (2%)
    all_to_all x1, waiting for transfers between devices, shards(): lax.all_to_all(spread(parts, 0.0, jnp.bfloat16), 'blk', split_axis=0, con...  181 us
    all_to_all x1, waiting for transfers between devices, shards(): lax.all_to_all(owned_feats[asked], 'blk', split_axis=0, concat_axis=0, ti...  181 us
    all_to_all x1, waiting for transfers between devices, shards(): lax.all_to_all(owned_points[asked_here], 'blk', split_axis=0, concat_axis...  90.1 us
    dot_general x40, matrix products, block_cost(): jnp.einsum('id,kjd->kij', points, targets, preferred_element_type=jnp.flo...  68.9 us
    reduce_scatter x1, waiting for transfers between devices, shards(): lax.psum_scatter(totals_all, 'grp', scatter_dimension=0, tiled=True)  49.6 us
    all_gather x4, blocking collectives, combined_all(): gathered = jax.tree.map(lambda a: lax.all_gather(a, axis), part)  38.7 us
    all_to_all x2, starting transfers between devices, shards(): lax.all_to_all(owner_pot[asked], 'blk', split_axis=0, concat_axis=0, tile...  30.7 us
    all_to_all x2, waiting for transfers between devices, shards(): lax.all_to_all(owner_pot[asked], 'blk', split_axis=0, concat_axis=0, tile...  20.7 us
  transfers between devices with their start and end apart: 12, of which 11 were waited for; matrix products, arithmetic and copies ran while one was open for 2% of the time, Pallas kernels for 0%

commit v1 on v0

v1 whole, which is shorter than its diff:
```python
import functools
import jax
import jax.numpy as jnp
from jax import lax
from jax.experimental import pallas as pl
from jax.experimental.pallas import tpu as pltpu
from jax.sharding import PartitionSpec as P

ROUNDS = 2
LOWEST = -1e30
CROSS = 0.3125
SQUARE = 0.15625
MESH = pl.DeviceIdType.MESH
MIB = 2**20
f32 = jnp.float32
bf16 = jnp.bfloat16


def params(cid=None, vmem=48):
    if cid is None:
        return pltpu.CompilerParams(vmem_limit_bytes=vmem * MIB)
    return pltpu.CompilerParams(
        collective_id=cid, has_side_effects=True, vmem_limit_bytes=vmem * MIB
    )


def nt(a, b):
    return lax.dot_general(a, b, (((1,), (1,)), ((), ())), preferred_element_type=f32)


def tn(a, b):
    return lax.dot_general(a, b, (((0,), (0,)), ((), ())), preferred_element_type=f32)


def nn(a, b):
    return jnp.dot(a, b, preferred_element_type=f32)


def greet(axes):
    bar = pltpu.get_barrier_semaphore()
    total = 0
    for name in axes:
        n = lax.axis_size(name)
        me = lax.axis_index(name)

        @pl.loop(1, n)
        def _(s):
            pl.semaphore_signal(
                bar, inc=1, device_id={name: lax.rem(me + s, n)}, device_id_type=MESH
            )

        total += n - 1
    pl.semaphore_wait(bar, total)


def send_all(src, dst, send, recv, axis):
    n = lax.axis_size(axis)
    me = lax.axis_index(axis)

    @pl.loop(1, n)
    def _(s):
        to = lax.rem(me + s, n)
        pltpu.make_async_remote_copy(
            src_ref=src(to),
            dst_ref=dst,
            send_sem=send,
            recv_sem=recv,
            device_id={axis: to},
            device_id_type=MESH,
        ).start()


def wait_all(whole, send, recv, axis):
    n = lax.axis_size(axis)
    part = whole.at[pl.ds(0, n - 1)]
    copy = pltpu.make_async_remote_copy(
        src_ref=part,
        dst_ref=part,
        send_sem=send,
        recv_sem=recv,
        device_id={axis: lax.rem(lax.axis_index(axis) + 1, n)},
        device_id_type=MESH,
    )
    copy.wait_send()
    copy.wait_recv()


def exchange_kernel(x_ref, o_ref, send, recv, own):
    me = lax.axis_index("blk")
    greet(["blk"])
    mine = pltpu.make_async_copy(x_ref.at[me], o_ref.at[me], own)
    mine.start()
    send_all(lambda to: x_ref.at[to], o_ref.at[me], send, recv, "blk")
    mine.wait()
    wait_all(o_ref, send, recv, "blk")


def exchange(x, cid):
    return pl.pallas_call(
        exchange_kernel,
        out_shape=jax.ShapeDtypeStruct(x.shape, x.dtype),
        in_specs=[pl.BlockSpec(memory_space=pltpu.VMEM)],
        out_specs=pl.BlockSpec(memory_space=pltpu.VMEM),
        scratch_shapes=[pltpu.SemaphoreType.DMA] * 3,
        compiler_params=params(cid),
    )(x)


def reshard_kernel(x_ref, o_ref, send, recv, own, send_x, recv_x):
    me = lax.axis_index("blk")
    plane = lax.axis_index("grp")
    greet(["blk", "grp"])
    mine = pltpu.make_async_copy(x_ref.at[me], o_ref.at[plane, me], own)
    mine.start()
    send_all(lambda to: x_ref.at[to], o_ref.at[plane, me], send, recv, "blk")
    mine.wait()
    wait_all(x_ref, send, recv, "blk")
    send_all(lambda to: o_ref.at[plane], o_ref.at[plane], send_x, recv_x, "grp")
    wait_all(o_ref, send_x, recv_x, "grp")


def reshard(x, cid):
    planes = lax.axis_size("grp")
    return pl.pallas_call(
        reshard_kernel,
        out_shape=jax.ShapeDtypeStruct((planes,) + x.shape, x.dtype),
        in_specs=[pl.BlockSpec(memory_space=pltpu.VMEM)],
        out_specs=pl.BlockSpec(memory_space=pltpu.VMEM),
        scratch_shapes=[pltpu.SemaphoreType.DMA] * 5,
        compiler_params=params(cid),
    )(x)


def spread_kernel(x_ref, o_ref, send, recv, own):
    plane = lax.axis_index("grp")
    greet(["grp"])
    mine = pltpu.make_async_copy(x_ref.at[plane], o_ref.at[plane], own)
    mine.start()
    send_all(lambda to: x_ref.at[to], o_ref.at[plane], send, recv, "grp")
    mine.wait()
    wait_all(o_ref, send, recv, "grp")


def spread(x, cid):
    return pl.pallas_call(
        spread_kernel,
        out_shape=jax.ShapeDtypeStruct(x.shape, x.dtype),
        in_specs=[pl.BlockSpec(memory_space=pltpu.VMEM)],
        out_specs=pl.BlockSpec(memory_space=pltpu.VMEM),
        scratch_shapes=[pltpu.SemaphoreType.DMA] * 3,
        compiler_params=params(cid),
    )(x)


def potentials_kernel(
    inv, asked, posn, c_ref, logw_ref, beta_ref, lse_ref,
    padded, out1, in1, own, upper, summed, outx, inx, both, out2, in2,
    send1, recv1, send2, recv2, send3, recv3,
):
    me = lax.axis_index("blk")
    plane = lax.axis_index("grp")
    owners = lax.axis_size("blk")
    pairs, block = c_ref.shape
    rows = pairs // 8
    greet(["blk", "grp"])
    padded[pl.ds(0, pairs), :] = c_ref[...]
    padded[pl.ds(pairs, 8), :] = jnp.full((8, block), LOWEST, f32)

    @pl.loop(0, owners)
    def _(s):
        to = lax.rem(me + s, owners)
        out1[to, 0:1, :] = padded[pl.ds(inv[2 * to], 1), :]
        out1[to, 1:2, :] = padded[pl.ds(inv[2 * to + 1], 1), :]

        @pl.when(s > 0)
        def _():
            pltpu.make_async_remote_copy(
                src_ref=out1.at[to],
                dst_ref=in1.at[me],
                send_sem=send1,
                recv_sem=recv1,
                device_id={"blk": to},
                device_id_type=MESH,
            ).start()

    in1[me] = out1[me]
    own[...] = jnp.full(own.shape, LOWEST, f32)
    for r in range(rows):
        own[pl.ds(plane * rows + r, 1), :] = padded[pl.ds(8 * r, 1), :]
    wait_all(in1, send1, recv1, "blk")
    index = lax.broadcasted_iota(jnp.int32, own.shape, 0)

    def highest(t, best):
        for c in range(2):
            row = in1[t, c : c + 1, :]
            best = jnp.maximum(best, jnp.where(index == asked[2 * t + c], row, LOWEST))
        return best

    upper[pl.ds(0, own.shape[0]), :] = lax.fori_loop(0, owners, highest, own[...])
    upper[pl.ds(own.shape[0], 8), :] = jnp.zeros((8, block), f32)

    def add(t, total):
        for c in range(2):
            slot = asked[2 * t + c]
            value = jnp.exp(in1[t, c : c + 1, :] - upper[pl.ds(slot, 1), :])
            total = total + jnp.where(index == slot, value, 0.0)
        return total

    top = upper[pl.ds(0, own.shape[0]), :]
    first = jnp.where(own[...] > 0.5 * LOWEST, jnp.exp(own[...] - top), 0.0)
    total = lax.fori_loop(0, owners, add, first)
    mine = jnp.where(total > 0.0, top + jnp.log(jnp.where(total > 0.0, total, 1.0)), LOWEST)
    outx[...] = mine
    inx[plane] = mine
    send_all(lambda to: outx, inx.at[plane], send2, recv2, "grp")
    wait_all(inx, send2, recv2, "grp")
    planes = inx.shape[0]
    top = inx[0]
    for p in range(1, planes):
        top = jnp.maximum(top, inx[p])
    total = jnp.exp(inx[0] - top)
    for p in range(1, planes):
        total = total + jnp.exp(inx[p] - top)
    lse = top + jnp.log(total)
    both[0, pl.ds(0, lse.shape[0]), :] = logw_ref[...] - lse
    both[1, pl.ds(0, lse.shape[0]), :] = lse
    both[:, pl.ds(lse.shape[0], 8), :] = jnp.zeros((2, 8, block), f32)

    @pl.loop(0, owners)
    def _(s):
        to = lax.rem(me + s, owners)
        for c in range(2):
            slot = asked[2 * to + c]
            out2[to, 2 * c : 2 * c + 1, :] = both[0, pl.ds(slot, 1), :]
            out2[to, 2 * c + 1 : 2 * c + 2, :] = both[1, pl.ds(slot, 1), :]

        @pl.when(s > 0)
        def _():
            pltpu.make_async_remote_copy(
                src_ref=out2.at[to],
                dst_ref=in2.at[me],
                send_sem=send3,
                recv_sem=recv3,
                device_id={"blk": to},
                device_id_type=MESH,
            ).start()

    in2[me] = out2[me]
    wait_all(in2, send3, recv3, "blk")
    for r in range(rows):
        beta_ref[8 * r : 8 * r + 1, :] = both[0, pl.ds(plane * rows + r, 1), :]
        lse_ref[8 * r : 8 * r + 1, :] = both[1, pl.ds(plane * rows + r, 1), :]
        for k in range(7):
            where = posn[7 * r + k]
            owner = where // 2
            rank = where % 2
            beta_ref[8 * r + k + 1 : 8 * r + k + 2, :] = in2[owner, pl.ds(2 * rank, 1), :]
            lse_ref[8 * r + k + 1 : 8 * r + k + 2, :] = in2[owner, pl.ds(2 * rank + 1, 1), :]


def potentials(inv, asked, posn, c, logw, cid):
    pairs, block = c.shape
    owners = lax.axis_size("blk")
    planes = lax.axis_size("grp")
    held = logw.shape[0]
    smem = pl.BlockSpec(memory_space=pltpu.SMEM)
    vmem = pl.BlockSpec(memory_space=pltpu.VMEM)
    return pl.pallas_call(
        potentials_kernel,
        out_shape=(jax.ShapeDtypeStruct((pairs, block), f32),) * 2,
        in_specs=[smem, smem, smem, vmem, vmem],
        out_specs=(vmem, vmem),
        scratch_shapes=[
            pltpu.VMEM((pairs + 8, block), f32),
            pltpu.VMEM((owners, 2, block), f32),
            pltpu.VMEM((owners, 2, block), f32),
            pltpu.VMEM((held, block), f32),
            pltpu.VMEM((held + 8, block), f32),
            pltpu.VMEM((held, block), f32),
            pltpu.VMEM((held, block), f32),
            pltpu.VMEM((planes, held, block), f32),
            pltpu.VMEM((2, held + 8, block), f32),
            pltpu.VMEM((owners, 4, block), f32),
            pltpu.VMEM((owners, 4, block), f32),
        ]
        + [pltpu.SemaphoreType.DMA] * 6,
        compiler_params=params(cid),
    )(inv, asked, posn, c, logw)


def pack_kernel(groups, ids_ref, table_ref, o_ref, halves):
    count, width = table_ref.shape

    @pl.when(pl.program_id(0) == 0)
    def _():
        for start in range(0, count, 512):
            piece = table_ref[pl.ds(start, 512), :].astype(f32).reshape(32, 2, 8, width)
            for h in range(2):
                halves[h, pl.ds(start // 2, 256), :] = (
                    piece[:, h].reshape(256, width).astype(bf16)
                )

    ids = ids_ref[:, 0:1]
    index = lax.broadcasted_iota(jnp.int32, (ids.shape[0], count // 2), 1)
    hot = (index == ids).astype(f32).astype(bf16)
    low = nn(hot, halves[0])
    high = nn(hot, halves[1])
    for d in range(groups):
        for k in range(7):
            at = (d * 7 + k) * 8
            both = jnp.concatenate([low[at : at + 8], high[at : at + 8]], axis=0)
            o_ref[d, :, k * width : (k + 1) * width] = both.astype(bf16)


def pack(ids, table, dests):
    width = table.shape[-1]
    flat = table.reshape(-1, width)
    groups = 4
    return pl.pallas_call(
        functools.partial(pack_kernel, groups),
        grid=(dests // groups,),
        out_shape=jax.ShapeDtypeStruct((dests, 16, 7 * width), bf16),
        in_specs=[
            pl.BlockSpec((groups * 56, 128), lambda i: (i, 0)),
            pl.BlockSpec(flat.shape, lambda i: (0, 0)),
        ],
        out_specs=pl.BlockSpec((groups, 16, 7 * width), lambda i: (i, 0, 0)),
        scratch_shapes=[pltpu.VMEM((2, flat.shape[0] // 2, width), bf16)],
        compiler_params=params(),
    )(ids, flat)


def gather_rows_kernel(width, x_ref, o_ref, wide):
    lanes = x_ref.shape[1]
    for c in range(lanes // 128):
        wide[c] = x_ref[:, c * 128 : (c + 1) * 128].astype(f32)
    for r in range(8):
        for h in range(2):
            for c in range(2):
                if width == 128:
                    got = wide[c, pl.ds(h * 8 + r, 64, stride=16), :]
                    o_ref[r, 0, (2 * h + c) * 64 : (2 * h + c + 1) * 64, :] = got.astype(bf16)
            if width == 64:
                got = wide[0, pl.ds(h * 8 + r, 64, stride=16), :].astype(bf16)
                o_ref[r, 0, 2 * h * 64 : (2 * h + 1) * 64, :] = got[:, 0:64]
                o_ref[r, 0, (2 * h + 1) * 64 : (2 * h + 2) * 64, :] = got[:, 64:128]


def gather_rows(x, width):
    flat = x.reshape(x.shape[0] * 16, 7 * 2 * width)
    return pl.pallas_call(
        functools.partial(gather_rows_kernel, width),
        grid=(7,),
        out_shape=jax.ShapeDtypeStruct((8, 7, 256, width), bf16),
        in_specs=[pl.BlockSpec((flat.shape[0], 2 * width), lambda k: (0, k))],
        out_specs=pl.BlockSpec((8, 1, 256, width), lambda k: (0, k, 0, 0)),
        scratch_shapes=[pltpu.VMEM((2 * width // 128, flat.shape[0], 128), f32)],
        compiler_params=params(),
    )(flat)


def scatter_rows_kernel(x_ref, o_ref, wide):
    for r in range(8):
        for h in range(2):
            for c in range(2):
                at = (2 * h + c) * 64
                wide[c, pl.ds(h * 8 + r, 64, stride=16), :] = x_ref[r, 0, at : at + 64, :].astype(f32)
    for c in range(2):
        o_ref[:, c * 128 : (c + 1) * 128] = wide[c].astype(bf16)


def scatter_rows(x):
    rows = 1024
    return pl.pallas_call(
        scatter_rows_kernel,
        grid=(7,),
        out_shape=jax.ShapeDtypeStruct((rows, 7 * 256), bf16),
        in_specs=[pl.BlockSpec((8, 1, 256, 128), lambda k: (0, k, 0, 0))],
        out_specs=pl.BlockSpec((rows, 256), lambda k: (0, k)),
        scratch_shapes=[pltpu.VMEM((2, rows, 128), f32)],
        compiler_params=params(),
    )(x).reshape(64, 16, 7 * 256)


def squares_row(t):
    wide = t.astype(f32)
    square = wide * wide
    high = square.astype(bf16)
    low = (square - high.astype(f32)).astype(bf16)
    ones = jnp.ones((8, t.shape[1]), bf16)
    return SQUARE * (nt(ones, high) + nt(ones, low))[0:1]


def row_scores(first, x, own_ref, far_ref, beta_ref, scores):
    top = None
    for k in range(8):
        t = own_ref[...] if k == 0 else far_ref[0, k - 1]
        bias = -squares_row(t) if first else beta_ref[k : k + 1, :]
        z = nt(x, t) * CROSS + bias
        scores[k] = z
        top = z if top is None else jnp.maximum(top, z)
    return jnp.max(top, axis=1, keepdims=True)


def round_kernel(first, *refs):
    if first:
        x_ref, own_ref, far_ref, logw_ref, c_ref, alpha_ref, scores = refs
        beta_ref = None
    else:
        x_ref, own_ref, far_ref, logw_ref, beta_ref, c_ref, alpha_ref, scores = refs
    x = x_ref[...]
    peak = row_scores(first, x, own_ref, far_ref, beta_ref, scores)
    total = None
    for k in range(8):
        e = jnp.exp(scores[k] - peak)
        total = e if total is None else total + e
    alpha = logw_ref[...] - peak - jnp.log(jnp.sum(total, axis=1, keepdims=True))
    alpha_ref[...] = alpha
    for k in range(8):
        t = own_ref[...] if k == 0 else far_ref[0, k - 1]
        v = nt(x, t) * CROSS + alpha
        top = jnp.max(v, axis=0, keepdims=True)
        c_ref[k : k + 1, :] = top + jnp.log(jnp.sum(jnp.exp(v - top), axis=0, keepdims=True))


def one_round(x, own, far, logw, beta):
    first = beta is None
    specs = [
        pl.BlockSpec((256, 64), lambda r: (r, 0)),
        pl.BlockSpec((256, 64), lambda r: (r, 0)),
        pl.BlockSpec((1, 7, 256, 64), lambda r: (r, 0, 0, 0)),
        pl.BlockSpec((256, 1), lambda r: (r, 0)),
    ]
    args = [x, own, far, logw]
    if not first:
        specs.append(pl.BlockSpec((8, 256), lambda r: (r, 0)))
        args.append(beta)
    return pl.pallas_call(
        functools.partial(round_kernel, first),
        grid=(8,),
        out_shape=(jax.ShapeDtypeStruct((64, 256), f32), jax.ShapeDtypeStruct((2048, 1), f32)),
        in_specs=specs,
        out_specs=(
            pl.BlockSpec((8, 256), lambda r: (r, 0)),
            pl.BlockSpec((256, 1), lambda r: (r, 0)),
        ),
        scratch_shapes=[pltpu.VMEM((8, 256, 256), f32)],
        compiler_params=params(),
    )(*args)


def transport_kernel(
    x_ref, own_ref, far_ref, beta_ref, lse_ref, alpha_ref, ownf_ref, farf_ref, srcf_ref,
    moved_ref, diag_ref, parts_ref, scores,
):
    x = x_ref[...]
    peak = row_scores(False, x, own_ref, far_ref, beta_ref, scores)
    total = None
    mixed = None
    for k in range(8):
        e = jnp.exp(scores[k] - peak)
        total = e if total is None else total + e
        feats = ownf_ref[...] if k == 0 else farf_ref[0, k - 1]
        term = nn(e.astype(bf16), feats)
        mixed = term if mixed is None else mixed + term
    moved_ref[...] = (mixed / jnp.sum(total, axis=1, keepdims=True)).astype(bf16)
    alpha = alpha_ref[...]
    srcf = srcf_ref[...]
    for k in range(8):
        t = own_ref[...] if k == 0 else far_ref[0, k - 1]
        w = jnp.exp(nt(x, t) * CROSS + alpha - lse_ref[k : k + 1, :]).astype(bf16)
        part = tn(w, srcf).astype(bf16)
        if k == 0:
            diag_ref[...] = part
        else:
            parts_ref[0, k - 1] = part


def transport(x, own, far, beta, lse, alpha, ownf, farf, srcf):
    def row(width):
        return pl.BlockSpec((256, width), lambda r: (r, 0))

    def four(width):
        return pl.BlockSpec((1, 7, 256, width), lambda r: (r, 0, 0, 0))

    small = pl.BlockSpec((8, 256), lambda r: (r, 0))
    return pl.pallas_call(
        transport_kernel,
        grid=(8,),
        out_shape=(
            jax.ShapeDtypeStruct((2048, 128), bf16),
            jax.ShapeDtypeStruct((2048, 128), bf16),
            jax.ShapeDtypeStruct((8, 7, 256, 128), bf16),
        ),
        in_specs=[row(64), row(64), four(64), small, small, row(1), row(128), four(128), row(128)],
        out_specs=(row(128), row(128), four(128)),
        scratch_shapes=[pltpu.VMEM((8, 256, 256), f32)],
        compiler_params=params(),
    )(x, own, far, beta, lse, alpha, ownf, farf, srcf)


def collect_kernel(ids_ref, got_ref, o_ref, total):
    k = pl.program_id(0)
    got = got_ref[...].astype(f32).reshape(64, 2, 8, 256)
    index = lax.broadcasted_iota(jnp.int32, (total.shape[1], 512), 0)
    hot = (index == ids_ref[0]).astype(f32).astype(bf16)
    for h in range(2):
        piece = got[:, h].reshape(512, 256).astype(bf16)
        term = nn(hot, piece)

        @pl.when(k == 0)
        def _():
            total[h] = term

        @pl.when(k > 0)
        def _():
            total[h] += term

    @pl.when(k == 6)
    def _():
        for h in range(2):
            o_ref[:, h * 256 : (h + 1) * 256] = total[h].astype(bf16)


def collect(ids, got):
    flat = got.reshape(1024, 7 * 256)
    return pl.pallas_call(
        collect_kernel,
        grid=(7,),
        out_shape=jax.ShapeDtypeStruct((2048, 512), bf16),
        in_specs=[
            pl.BlockSpec((1, 1, 512), lambda k: (k, 0, 0)),
            pl.BlockSpec((1024, 256), lambda k: (0, k)),
        ],
        out_specs=pl.BlockSpec((2048, 512), lambda k: (0, 0)),
        scratch_shapes=[pltpu.VMEM((2, 2048, 256), f32)],
        compiler_params=params(),
    )(ids, flat)


def shards(
    source_points, target_points, source_logw, target_logw,
    source_feats, target_feats, pair_owner, pair_slot,
):
    n = lax.axis_size("blk")
    plane = lax.axis_index("grp")
    me = lax.axis_index("blk")
    start = plane * 2048
    own_points = lax.dynamic_slice_in_dim(target_points, start, 2048, 0)
    own_feats = lax.dynamic_slice_in_dim(target_feats, start, 2048, 0)

    requests = (pair_owner * 32 + pair_slot).reshape(56)
    table = lax.all_gather(requests, "blk")
    owner_of = table // 32
    slot_of = table % 32
    ids = (slot_of // 8) * 512 + owner_of * 8 + slot_of % 8
    ids = ids.reshape(n, 8, 7).transpose(0, 2, 1)
    ids_column = jnp.broadcast_to(ids.reshape(n * 56, 1), (n * 56, 128))
    ids_row = ids.transpose(1, 0, 2).reshape(7, 1, n * 8)
    here = owner_of == me
    rank = jnp.cumsum(here.astype(jnp.int32), axis=1) - 1
    asked = jnp.stack(
        [jnp.min(jnp.where(here & (rank == c), slot_of, 32), axis=1) for c in range(2)], axis=1
    ).reshape(2 * n)
    owners = pair_owner.reshape(56)
    earlier = jnp.tril(jnp.ones((56, 56), bool), -1) & (owners[:, None] == owners[None, :])
    posn = owners * 2 + jnp.sum(earlier.astype(jnp.int32), axis=1)
    order = jnp.arange(56, dtype=jnp.int32)
    row_of = order + order // 7 + 1
    inv = jnp.min(
        jnp.where(posn[None, :] == jnp.arange(2 * n)[:, None], row_of[None, :], 64), axis=1
    )

    def stripes(own, width):
        out = own.reshape(8, 2, 2, 64, width).transpose(3, 1, 0, 2, 4)
        return out.reshape(64, 16, 2 * width)

    point_table = reshard(stripes(own_points, 64), 0)
    feat_table = reshard(stripes(own_feats, 128), 1)
    far_points = gather_rows(exchange(pack(ids_column, point_table, n), 2), 64)
    sent_feats = pack(ids_column, feat_table, n)
    got_feats = lax.all_to_all(sent_feats, "blk", split_axis=0, concat_axis=0, tiled=True)

    logw = source_logw.reshape(2048, 1)
    owned_logw = target_logw.reshape(32, 256)
    beta = None
    for _ in range(ROUNDS):
        c, alpha = one_round(source_points, own_points, far_points, logw, beta)
        beta, lse = potentials(inv, asked, posn, c, owned_logw, 3)
    far_feats = gather_rows(got_feats, 128)
    moved_source, diag, parts = transport(
        source_points, own_points, far_points, beta, lse, alpha, own_feats, far_feats, source_feats
    )
    got_parts = exchange(scatter_rows(parts), 4)
    sums = collect(ids_row, got_parts)
    planes = spread(sums.reshape(4, 512, 512), 5)
    summed = jnp.sum(planes.astype(f32), axis=0).astype(bf16)
    final = exchange(
        summed.reshape(64, 8, 2, 256).transpose(0, 2, 1, 3).reshape(64, 16, 256), 6
    )
    far_sum = final.reshape(64, 2, 8, 2, 128).transpose(2, 1, 3, 0, 4).reshape(2048, 128)
    moved_target = (far_sum.astype(f32) + diag.astype(f32)).astype(bf16)
    return moved_source, moved_target


def solution(mesh):
    return jax.shard_map(
        shards,
        mesh=mesh,
        in_specs=(
            P(("blk", "grp"), None),
            P("blk", None),
            P(("blk", "grp")),
            P("blk"),
            P(("blk", "grp"), None),
            P("blk", None),
            P(("blk", "grp"), None),
            P(("blk", "grp"), None),
        ),
        out_specs=(P(("blk", "grp"), None), P(("blk", "grp"), None)),
        check_vma=False,
    )
```

time: 935 us -> 583 us (0.62); the launches traced: 924 us -> 582 us
  waiting for transfers between devices: 554 us -> 0.01 us
  Pallas kernels: 0 us -> 502 us
  matrix products: 117 us -> 0 us
  starting transfers between devices: 90.8 us -> 8.02 us
  local copies, waits for them, and re-layouts: 69.8 us -> 22.4 us
  other arithmetic: 35.7 us -> 4.8 us
  between operations: 15.1 us -> 1.06 us
    all_to_all x11 -> x1, waiting for transfers between devices: 505 us -> 0.01 us  [shards(): lax.all_to_all(sent_feats, 'blk', split_axis=0, concat_axis=0, tiled=True)]
    pallas_call x0 -> x17, Pallas kernels: none -> 502 us  [the longest x3 162 us: exchange(): pl.pallas_call(exchange_kernel, out_shape=jax.ShapeDtypeStruct(x.shape, x...]
    dot_general x57 -> x0, matrix products: 117 us -> none  [the longest x40 68.9 us: block_cost(): jnp.einsum('id,kjd->kij', points, targets, preferred_element_type=jnp.flo...]
    all_to_all x11 -> x1, starting transfers between devices: 90.6 us -> 8.02 us  [shards(): lax.all_to_all(sent_feats, 'blk', split_axis=0, concat_axis=0, tiled=True)]
    reduce_scatter x1 -> x0, waiting for transfers between devices: 49.6 us -> none  [shards(): lax.psum_scatter(totals_all, 'grp', scatter_dimension=0, tiled=True)]
    gather x13 -> x0, local copies, waits for them, and re-layouts: 26 us -> none  [the longest x5 12.4 us: per_pair(): return flat[position].reshape((dev_blocks, neighbours) + tail)]
    reduce_sum x45 -> x2, other arithmetic: 19.6 us -> 2.35 us  [the longest x1 2.18 us: shards(): summed = jnp.sum(planes.astype(f32), axis=0).astype(bf16)]
    scatter x6 -> x0, local copies, waits for them, and re-layouts: 15.7 us -> none  [the longest x5 14.9 us: spread(): buffer = jnp.full((slots,) + values.shape[2:], fill, dtype).at[position]....]
  transfers between devices with their start and end apart: 12 -> 1, of which waited for: 11 -> 0; matrix products, arithmetic and copies ran while one was open for 2% -> 1% of each run, Pallas kernels for 0% -> 43%
where the time goes in v1:
time: 583 us; the launch traced here: 582 us
  Pallas kernels  502 us (86%)
  blocking collectives  44.2 us (8%)
  local copies, waits for them, and re-layouts  22.4 us (4%)
  starting transfers between devices  8.02 us (1%)
    pallas_call x3, Pallas kernels, exchange(): pl.pallas_call(exchange_kernel, out_shape=jax.ShapeDtypeStruct(x.shape, x...  162 us
    pallas_call x2, Pallas kernels, reshard(): pl.pallas_call(reshard_kernel, out_shape=jax.ShapeDtypeStruct((planes,) +...  145 us
    pallas_call x2, Pallas kernels, potentials(): pl.pallas_call(potentials_kernel, out_shape=(jax.ShapeDtypeStruct((pairs,...  64.6 us
    all_gather x1, blocking collectives, shards(): table = lax.all_gather(requests, 'blk')  44.2 us
    pallas_call x2, Pallas kernels, one_round(): pl.pallas_call(functools.partial(round_kernel, first), grid=(8,), out_sha...  28.3 us
    pallas_call x1, Pallas kernels, spread(): pl.pallas_call(spread_kernel, out_shape=jax.ShapeDtypeStruct(x.shape, x.d...  26.1 us
    pallas_call x2, Pallas kernels, pack(): pl.pallas_call(functools.partial(pack_kernel, groups), grid=(dests // gro...  23.7 us
    pallas_call x1, Pallas kernels, collect(): pl.pallas_call(collect_kernel, grid=(7,), out_shape=jax.ShapeDtypeStruct(...  20.9 us
  transfers between devices with their start and end apart: 1, of which 0 were waited for; matrix products, arithmetic and copies ran while one was open for 1% of the time, Pallas kernels for 43%

profile of v1, /device:TPU:1, one launch (start us, length us, event | category | flops | bytes accessed | tf_op | source)
XLA Modules:
  0.0 582.2 jit_solution(15742258810338418340)
XLA Ops:
  1.6 44.2 %all-gather = s32[64,1,56]{2,1,0:T(1,128)S(1)} all-gather(s32[1,1,56]{2,1,0:T(1,128)S(1)} %reshape.116), channel_id=1, replica_groups=mesh['blk'=64,'grp'=4] {'blk'}, dimensions={0}, use_global_device_ids=true | all-gather | bytes 14560 | tf_op jit(solution)/shard_map/all_gather | solution.py:553
  47.5 44.9 %shard_map.103 = bf16[4,64,16,256]{3,2,1,0:T(8,128)(2,1)S(1)} custom-call(bf16[64,16,256]{2,1,0:T(8,128)(2,1)S(1)} %bitcast.48), custom_call_target="tpu_custom_call" | custom-call | tf_op jit(solution)/shard_map/pallas_call | solution.py:124
  92.9 11.9 %shard_map.104 = bf16[64,16,1792]{2,1,0:T(8,128)(2,1)} custom-call(s32[3584,128]{1,0:T(8,128)S(1)} %broadcast_in_dim.29.ids_ref, bf16[4096,256]{1,0:T(8,128)(2,1)S(1)} %bitcast.43), custom_call_target="tpu_custom_call" | custom-call | tf_op jit(solution)/shard_map/pallas_call | solution.py:319
  106.1 8.0 %all-to-all-start = ((bf16[64,16,1792]{2,1,0:T(8,128)(2,1)}), bf16[64,16,1792]{2,1,0:T(8,128)(2,1)}, u32[]{:S(2)}, u32[]{:S(2)}) async-start(bf16[64,16,1792]{2,1,0:T(8,128)(2,1)} %shard_map.104), calls=%async_computation | async-start | bytes 7340032 | tf_op jit(solution)/shard_map/all_to_all | solution.py:582
  119.1 99.7 %shard_map.95 = bf16[4,64,16,128]{3,2,1,0:T(8,128)(2,1)S(1)} custom-call(bf16[64,16,128]{2,1,0:T(8,128)(2,1)S(1)} %reshape.97.x_ref), custom_call_target="tpu_custom_call" | custom-call | tf_op jit(solution)/shard_map/pallas_call | solution.py:124
  221.1 1.5 copy-done.3
  223.8 11.8 %shard_map.96.x_ref = bf16[64,16,896]{2,1,0:T(8,128)(2,1)S(1)} custom-call(s32[3584,128]{1,0:T(8,128)S(1)} %copy-done.3, bf16[4096,128]{1,0:T(8,128)(2,1)S(1)} %bitcast.47), custom_call_target="tpu_custom_call" | custom-call | tf_op jit(solution)/shard_map/pallas_call | solution.py:319
  235.6 44.2 %shard_map.97 = bf16[64,16,896]{2,1,0:T(8,128)(2,1)S(1)} custom-call(bf16[64,16,896]{2,1,0:T(8,128)(2,1)S(1)} %shard_map.96.x_ref), custom_call_target="tpu_custom_call" | custom-call | tf_op jit(solution)/shard_map/pallas_call | solution.py:99
  279.8 2.6 shard_map.98.refs_2_.far_ref
  282.5 1.9 copy-done.1
  284.4 15.5 %shard_map.99 = (f32[64,256]{1,0:T(8,128)S(1)}, f32[2048,1]{1,0:T(8,128)}) custom-call(bf16[2048,64]{1,0:T(8,128)(2,1)S(1)} %copy.60.refs_0_.x_ref, bf16[2048,64]{1,0:T(8,128)(2,1)S(1)} %copy.66.refs_1_.own_ref, bf16[8,7,256,64]{3,2,1,0:T(8,128)(2,1)} %copy-done.1, f32[2048,1]{1,0:T(8,128)S(1)} %copy-done.6), custom_call_target="tpu_custom_call" | custom-call | tf_op jit(solution)/shard_map/pallas_call | solution.py:438
  300.2 36.0 %shard_map.100 = (f32[64,256]{1,0:T(8,128)S(1)}, f32[64,256]{1,0:T(8,128)}) custom-call(s32[128]{0:T(128)S(1)} %select_reduce_fusion.2.inv, s32[128]{0:T(128)S(1)} %reshape.101.asked, s32[56]{0:T(128)S(1)} %multiply_add_fusion.1.posn, f32[64,256]{1,0:T(8,128)S(1)} %get-tuple-element.11.c_ref, f32[32,256]{1,0:T(8,128)S(1)} %reshape.103.logw_ref), custom_call_target="tpu_custom_call" | custom-call | tf_op jit(solution)/shard_map/pallas_call | solution.py:268
  336.2 12.8 %shard_map.101 = (f32[64,256]{1,0:T(8,128)S(1)}, f32[2048,1]{1,0:T(8,128)S(1)}) custom-call(bf16[2048,64]{1,0:T(8,128)(2,1)S(1)} %copy.60.refs_0_.x_ref, bf16[2048,64]{1,0:T(8,128)(2,1)S(1)} %copy.66.refs_1_.own_ref, bf16[8,7,256,64]{3,2,1,0:T(8,128)(2,1)} %copy-done.1, f32[2048,1]{1,0:T(8,128)S(1)} %copy-done.6, f32[64,256]{1,0:T(8,128)S(1)} %get-tuple-element.12.refs_4_), custom_call_target="tpu_custom_call" | custom-call | tf_op jit(solution)/shard_map/pallas_call | solution.py:438
  350.0 28.6 %shard_map.102 = (f32[64,256]{1,0:T(8,128)S(1)}, f32[64,256]{1,0:T(8,128)S(1)}) custom-call(s32[128]{0:T(128)S(1)} %select_reduce_fusion.2.inv, s32[128]{0:T(128)S(1)} %reshape.101.asked, s32[56]{0:T(128)S(1)} %multiply_add_fusion.1.posn, f32[64,256]{1,0:T(8,128)S(1)} %get-tuple-element.13.c_ref, f32[32,256]{1,0:T(8,128)S(1)} %reshape.103.logw_ref), custom_call_target="tpu_custom_call" | custom-call | tf_op jit(solution)/shard_map/pallas_call | solution.py:268
  378.6 6.0 %shard_map.105.farf_ref = bf16[8,7,256,128]{3,2,1,0:T(8,128)(2,1)S(1)} custom-call(bf16[1024,1792]{1,0:T(8,128)(2,1)} %bitcast.14.x_ref), custom_call_target="tpu_custom_call" | custom-call | tf_op jit(solution)/shard_map/pallas_call | solution.py:351
  384.6 1.8 copy-done.5
  386.4 15.8 %shard_map.106 = (bf16[2048,128]{1,0:T(8,128)(2,1)}, bf16[2048,128]{1,0:T(8,128)(2,1)S(1)}, bf16[8,7,256,128]{3,2,1,0:T(8,128)(2,1)}) custom-call(bf16[2048,64]{1,0:T(8,128)(2,1)S(1)} %copy.60.refs_0_.x_ref, bf16[2048,64]{1,0:T(8,128)(2,1)S(1)} %copy.66.refs_1_.own_ref, bf16[8,7,256,64]{3,2,1,0:T(8,128)(2,1)} %copy-done.1, ...), custom_call_target="tpu_custom_call" | custom-call | tf_op jit(solution)/shard_map/pallas_call | solution.py:487
  403.1 6.8 %shard_map.107 = bf16[1024,1792]{1,0:T(8,128)(2,1)S(1)} custom-call(bf16[8,7,256,128]{3,2,1,0:T(8,128)(2,1)} %get-tuple-element.18.x_ref), custom_call_target="tpu_custom_call" | custom-call | tf_op jit(solution)/shard_map/pallas_call | solution.py:374
  409.9 1.8 copy-done.4
  411.6 87.3 %shard_map.108 = bf16[64,16,1792]{2,1,0:T(8,128)(2,1)S(1)} custom-call(bf16[64,16,1792]{2,1,0:T(8,128)(2,1)} %bitcast.40), custom_call_target="tpu_custom_call" | custom-call | tf_op jit(solution)/shard_map/pallas_call | solution.py:99
  499.0 20.9 %shard_map.109 = bf16[2048,512]{1,0:T(8,128)(2,1)S(1)} custom-call(s32[7,1,512]{2,1,0:T(1,128)S(1)} %reshape.119.ids_ref, bf16[1024,1792]{1,0:T(8,128)(2,1)S(1)} %bitcast.41), custom_call_target="tpu_custom_call" | custom-call | tf_op jit(solution)/shard_map/pallas_call | solution.py:527
  519.8 26.1 %shard_map.110 = bf16[4,512,512]{2,1,0:T(8,128)(2,1)S(1)} custom-call(bf16[4,512,512]{2,1,0:T(8,128)(2,1)S(1)} %bitcast.44), custom_call_target="tpu_custom_call" | custom-call | tf_op jit(solution)/shard_map/pallas_call | solution.py:145
  547.3 2.2 reduce_sum.22
  549.4 30.8 %shard_map.111 = bf16[64,16,256]{2,1,0:T(8,128)(2,1)S(1)} custom-call(bf16[64,16,256]{2,1,0:T(8,128)(2,1)S(1)} %bitcast.49), custom_call_target="tpu_custom_call" | custom-call | tf_op jit(solution)/shard_map/pallas_call | solution.py:99
  (72 shorter events, 18.1 us)
Async XLA Ops:
  0.6 46.0 %copy-start = (bf16[8192,128]{1,0:T(8,128)(2,1)S(1)}, bf16[8192,128]{1,0:T(8,128)(2,1)}, u32[]{:S(2)}) copy-start(bf16[8192,128]{1,0:T(8,128)(2,1)} %param.13) | copy-start | bytes 6291460
  46.7 0.8 copy-start.8
  104.8 1.3 copy-start.2
  106.1 8.0 %copy-start.19 = (s32[8,7]{1,0:T(8,128)S(1)}, s32[8,7]{1,0:T(8,128)}, u32[]{:S(2)}) copy-start(s32[8,7]{1,0:T(8,128)} %param.14) | copy-start | bytes 676
  106.1 8.1 %copy-start.18 = (f32[8192]{0:T(1024)S(1)}, f32[8192]{0:T(1024)}, u32[]{:S(2)}) copy-start(f32[8192]{0:T(1024)} %param.11) | copy-start | bytes 98308
  106.1 272.5 %all-to-all-start = ((bf16[64,16,1792]{2,1,0:T(8,128)(2,1)}), bf16[64,16,1792]{2,1,0:T(8,128)(2,1)}, u32[]{:S(2)}, u32[]{:S(2)}) async-start(bf16[64,16,1792]{2,1,0:T(8,128)(2,1)} %shard_map.104), calls=%async_computation | async-start | bytes 7340032 | tf_op jit(solution)/shard_map/all_to_all | solution.py:582
  114.2 1.9 copy-start.17
  116.1 103.6 %copy-start.20 = (f32[2048]{0:T(1024)S(1)}, f32[2048]{0:T(1024)}, u32[]{:S(2)}) copy-start(f32[2048]{0:T(1024)} %param.10) | copy-start | bytes 24580
  218.8 1.0 copy-start.10
  221.1 1.5 copy-start.3
  222.6 1.2 copy-start.11
  279.8 4.6 copy-start.6
  282.5 1.9 copy-start.1
  349.0 1.0 copy-start.12
  378.6 7.8 %copy-start.9 = (bf16[2048,128]{1,0:T(8,128)(2,1)S(1)}, bf16[2048,128]{1,0:T(8,128)(2,1)}, u32[]{:S(2)}) copy-start(bf16[2048,128]{1,0:T(8,128)(2,1)} %copy-done.8) | copy-start | bytes 1572868
  378.6 7.8 %copy-start.13 = (f32[2048,1]{1,0:T(8,128)S(1)}, f32[2048,1]{1,0:T(8,128)}, u32[]{:S(2)}) copy-start(f32[2048,1]{1,0:T(8,128)} %copy-done.12) | copy-start | bytes 24580
  378.6 7.8 %copy-start.16 = (bf16[2048,128]{1,0:T(8,128)(2,1)S(1)}, bf16[2048,128]{1,0:T(8,128)(2,1)}, u32[]{:S(2)}) copy-start(bf16[2048,128]{1,0:T(8,128)(2,1)} %srcf_ref.1) | copy-start | bytes 1572868
  384.6 1.8 copy-start.5
  402.3 0.8 copy-start.14
  409.8 1.8 copy-start.4
  545.9 1.3 copy-start.7
  580.2 1.0 copy-start.15

commit v2 on v1

v2 whole, which is shorter than its diff:
```python
import functools
import jax
import jax.numpy as jnp
from jax import lax
from jax.experimental import pallas as pl
from jax.experimental.pallas import tpu as pltpu
from jax.sharding import PartitionSpec as P

LOWEST = -1e30
CROSS = 0.3125
SQUARE = 0.15625
MESH = pl.DeviceIdType.MESH
MIB = 2**20
f32 = jnp.float32
bf16 = jnp.bfloat16


def params(cid=None, vmem=48):
    if cid is None:
        return pltpu.CompilerParams(vmem_limit_bytes=vmem * MIB)
    return pltpu.CompilerParams(
        collective_id=cid, has_side_effects=True, vmem_limit_bytes=vmem * MIB
    )


def nt(a, b):
    return lax.dot_general(a, b, (((1,), (1,)), ((), ())), preferred_element_type=f32)


def tn(a, b):
    return lax.dot_general(a, b, (((0,), (0,)), ((), ())), preferred_element_type=f32)


def nn(a, b):
    return jnp.dot(a, b, preferred_element_type=f32)


def greet(axes):
    bar = pltpu.get_barrier_semaphore()
    total = 0
    for name in axes:
        n = lax.axis_size(name)
        me = lax.axis_index(name)

        @pl.loop(1, n)
        def _(s):
            pl.semaphore_signal(
                bar, inc=1, device_id={name: lax.rem(me + s, n)}, device_id_type=MESH
            )

        total += n - 1
    pl.semaphore_wait(bar, total)


def send_all(src, dst, send, recv, axis):
    n = lax.axis_size(axis)
    me = lax.axis_index(axis)

    @pl.loop(1, n)
    def _(s):
        to = lax.rem(me + s, n)
        pltpu.make_async_remote_copy(
            src_ref=src(to),
            dst_ref=dst,
            send_sem=send,
            recv_sem=recv,
            device_id={axis: to},
            device_id_type=MESH,
        ).start()


def wait_all(whole, send, recv, axis):
    n = lax.axis_size(axis)
    part = whole.at[pl.ds(0, n - 1)]
    copy = pltpu.make_async_remote_copy(
        src_ref=part,
        dst_ref=part,
        send_sem=send,
        recv_sem=recv,
        device_id={axis: lax.rem(lax.axis_index(axis) + 1, n)},
        device_id_type=MESH,
    )
    copy.wait_send()
    copy.wait_recv()


def exchange_kernel(x_ref, o_ref, send, recv, own):
    me = lax.axis_index("blk")
    greet(["blk"])
    mine = pltpu.make_async_copy(x_ref.at[me], o_ref.at[me], own)
    mine.start()
    send_all(lambda to: x_ref.at[to], o_ref.at[me], send, recv, "blk")
    mine.wait()
    wait_all(o_ref, send, recv, "blk")


def exchange(x, cid):
    return pl.pallas_call(
        exchange_kernel,
        out_shape=jax.ShapeDtypeStruct(x.shape, x.dtype),
        in_specs=[pl.BlockSpec(memory_space=pltpu.VMEM)],
        out_specs=pl.BlockSpec(memory_space=pltpu.VMEM),
        scratch_shapes=[pltpu.SemaphoreType.DMA] * 3,
        compiler_params=params(cid),
    )(x)


def front_kernel(
    ids_ref, points_ref, feats_ref, far_ref, packed_ref, table_ref,
    ids_all, ids_wide, table_p, table_f, halves_p, halves_f, out_p, in_p, wide,
    send_i, recv_i, send_p, recv_p, send_f, recv_f, own, sendx_p, recvx_p, sendx_f, recvx_f,
    send_t, recv_t,
):
    n = lax.axis_size("blk")
    me = lax.axis_index("blk")
    plane = lax.axis_index("grp")
    greet(["blk", "grp"])

    def remote(src, dst, send, recv, to):
        pltpu.make_async_remote_copy(
            src_ref=src,
            dst_ref=dst,
            send_sem=send,
            recv_sem=recv,
            device_id={"blk": to},
            device_id_type=MESH,
        ).start()

    @pl.loop(1, n)
    def _(s):
        to = lax.rem(me + s, n)
        remote(points_ref.at[to], table_p.at[plane, me], send_p, recv_p, to)
        remote(ids_ref, ids_all.at[n - s], send_i, recv_i, to)

    @pl.loop(1, n)
    def _(s):
        to = lax.rem(me + s, n)
        remote(feats_ref.at[to], table_f.at[plane, me], send_f, recv_f, to)

    ids_all[0] = ids_ref[...]
    table_p[plane, me] = points_ref[me]
    table_f[plane, me] = feats_ref[me]
    wait_all(points_ref, send_p, recv_p, "blk")
    send_all(lambda to: table_p.at[plane], table_p.at[plane], sendx_p, recvx_p, "grp")
    wait_all(ids_all, send_i, recv_i, "blk")
    ids = ids_all[...].reshape(n, 128)
    table_ref[...] = ids
    turned = jnp.transpose(ids.astype(f32))
    for s in range(n):
        ids_wide[s] = jnp.broadcast_to(turned[0:56, s : s + 1], (56, 128))
    wait_all(feats_ref, send_f, recv_f, "blk")
    send_all(lambda to: table_f.at[plane], table_f.at[plane], sendx_f, recvx_f, "grp")

    def halve(table, halves):
        width = halves.shape[2]

        @pl.loop(0, 4)
        def _(p):
            for start in range(0, n, 16):
                piece = table[p, pl.ds(start, 16)].astype(f32)
                for h in range(2):
                    halves[h, pl.ds(p * (8 * n) + start * 8, 128), :] = (
                        piece[:, 8 * h : 8 * h + 8].reshape(128, width).astype(bf16)
                    )

    def pack(halves, out, then):
        width = halves.shape[2]

        @pl.loop(0, n // 4)
        def _(g):
            ids = ids_wide[pl.ds(4 * g, 4)].reshape(224, 128)[:, 0:1]
            index = lax.broadcasted_iota(jnp.int32, (224, halves.shape[1]), 1)
            hot = (index == ids.astype(jnp.int32)).astype(f32).astype(bf16)
            low = nn(hot, halves[0])
            high = nn(hot, halves[1])
            for d in range(4):
                for k in range(7):
                    at = (d * 7 + k) * 8
                    both = jnp.concatenate([low[at : at + 8], high[at : at + 8]], axis=0)
                    out[4 * g + d, :, k * width : (k + 1) * width] = both.astype(bf16)
                then(4 * g + d)

    def send_points(s):
        @pl.when(s > 0)
        def _():
            to = lax.rem(me + s, n)
            remote(out_p.at[s], in_p.at[me], send_t, recv_t, to)

    wait_all(table_p, sendx_p, recvx_p, "grp")
    halve(table_p, halves_p)
    pack(halves_p, out_p, send_points)
    in_p[me] = out_p[0]
    wait_all(table_f, sendx_f, recvx_f, "grp")
    halve(table_f, halves_f)
    pack(halves_f, packed_ref, lambda s: None)
    wait_all(in_p, send_t, recv_t, "blk")
    for k in range(7):
        wide[...] = in_p[:, :, 128 * k : 128 * (k + 1)].astype(f32).reshape(n * 16, 128)
        for r in range(8):
            for h in range(2):
                got = wide[pl.ds(h * 8 + r, n, stride=16), :].astype(bf16)
                far_ref[r, k, 2 * h * 64 : (2 * h + 1) * 64, :] = got[:, 0:64]
                far_ref[r, k, (2 * h + 1) * 64 : (2 * h + 2) * 64, :] = got[:, 64:128]


def front(ids, points, feats, cid):
    n = lax.axis_size("blk")
    vmem = pl.BlockSpec(memory_space=pltpu.VMEM)
    return pl.pallas_call(
        front_kernel,
        out_shape=(
            jax.ShapeDtypeStruct((8, 7, 256, 64), bf16),
            jax.ShapeDtypeStruct((n, 16, 7 * 256), bf16),
            jax.ShapeDtypeStruct((n, 128), jnp.int32),
        ),
        in_specs=[vmem] * 3,
        out_specs=(vmem,) * 3,
        scratch_shapes=[
            pltpu.VMEM((n, 1, 128), jnp.int32),
            pltpu.VMEM((n, 56, 128), f32),
            pltpu.VMEM((4, n, 16, 128), bf16),
            pltpu.VMEM((4, n, 16, 256), bf16),
            pltpu.VMEM((2, 32 * n, 128), bf16),
            pltpu.VMEM((2, 32 * n, 256), bf16),
            pltpu.VMEM((n, 16, 7 * 128), bf16),
            pltpu.VMEM((n, 16, 7 * 128), bf16),
            pltpu.VMEM((n * 16, 128), f32),
        ]
        + [pltpu.SemaphoreType.DMA] * 13,
        compiler_params=params(cid),
    )(ids, points, feats)


def spread_kernel(x_ref, o_ref, send, recv, own):
    plane = lax.axis_index("grp")
    greet(["grp"])
    mine = pltpu.make_async_copy(x_ref.at[plane], o_ref.at[plane], own)
    mine.start()
    send_all(lambda to: x_ref.at[to], o_ref.at[plane], send, recv, "grp")
    mine.wait()
    wait_all(o_ref, send, recv, "grp")


def spread(x, cid):
    return pl.pallas_call(
        spread_kernel,
        out_shape=jax.ShapeDtypeStruct(x.shape, x.dtype),
        in_specs=[pl.BlockSpec(memory_space=pltpu.VMEM)],
        out_specs=pl.BlockSpec(memory_space=pltpu.VMEM),
        scratch_shapes=[pltpu.SemaphoreType.DMA] * 3,
        compiler_params=params(cid),
    )(x)


def rounds_kernel(
    inv, asked, posn, x_ref, own_ref, far_ref, logw_ref, logwt_ref, packed_ref,
    beta_ref, lse_ref, alpha_ref, got_ref,
    scores, padded, out1, in1, own, upper, outx, inx, both, out2, in2,
    send1, recv1, send2, recv2, send3, recv3, send_f, recv_f,
):
    me = lax.axis_index("blk")
    plane = lax.axis_index("grp")
    n = lax.axis_size("blk")
    pairs, block = beta_ref.shape
    rows = pairs // 8
    held = own.shape[0]
    greet(["blk", "grp"])
    padded[pl.ds(pairs, 8), :] = jnp.full((8, block), LOWEST, f32)

    def remote(src, dst, send, recv, to):
        pltpu.make_async_remote_copy(
            src_ref=src,
            dst_ref=dst,
            send_sem=send,
            recv_sem=recv,
            device_id={"blk": to},
            device_id_type=MESH,
        ).start()

    def bulk(chunk):
        @pl.loop(0, n // 8)
        def _(j):
            s = 8 * j + chunk

            @pl.when(s > 0)
            def _():
                remote(packed_ref.at[s], got_ref.at[me], send_f, recv_f, lax.rem(me + s, n))

    def compute(first, chunks):
        @pl.loop(0, rows)
        def _(r):
            for i, chunk in enumerate(chunks):

                @pl.when(r == i * (rows // len(chunks)))
                def _():
                    bulk(chunk)

            at = pl.ds(pl.multiple_of(r * block, block), block)
            x = x_ref[at, :]
            top = None
            for k in range(8):
                t = own_ref[at, :] if k == 0 else far_ref[r, k - 1]
                bias = -squares_row(t) if first else beta_ref[pl.ds(8 * r + k, 1), :]
                z = nt(x, t) * CROSS + bias
                scores[k] = z
                top = z if top is None else jnp.maximum(top, z)
            peak = jnp.max(top, axis=1, keepdims=True)
            total = None
            for k in range(8):
                e = jnp.exp(scores[k] - peak)
                total = e if total is None else total + e
            alpha = logw_ref[at, :] - peak - jnp.log(jnp.sum(total, axis=1, keepdims=True))
            alpha_ref[at, :] = alpha
            for k in range(8):
                t = own_ref[at, :] if k == 0 else far_ref[r, k - 1]
                v = nt(x, t) * CROSS + alpha
                top = jnp.max(v, axis=0, keepdims=True)
                padded[pl.ds(8 * r + k, 1), :] = top + jnp.log(
                    jnp.sum(jnp.exp(v - top), axis=0, keepdims=True)
                )

    def potentials(turn, chunks):
        @pl.loop(0, n)
        def _(s):
            to = lax.rem(me + s, n)
            out1[to, 0:1, :] = padded[pl.ds(inv[2 * to], 1), :]
            out1[to, 1:2, :] = padded[pl.ds(inv[2 * to + 1], 1), :]

            @pl.when(s > 0)
            def _():
                remote(out1.at[to], in1.at[me], send1, recv1, to)

        bulk(chunks[0])
        in1[me] = out1[me]
        own[...] = jnp.full(own.shape, LOWEST, f32)
        for r in range(rows):
            own[pl.ds(plane * rows + r, 1), :] = padded[pl.ds(8 * r, 1), :]
        wait_all(in1, send1, recv1, "blk")
        index = lax.broadcasted_iota(jnp.int32, own.shape, 0)

        def highest(t, best):
            for c in range(2):
                row = in1[t, c : c + 1, :]
                best = jnp.maximum(best, jnp.where(index == asked[2 * t + c], row, LOWEST))
            return best

        upper[pl.ds(0, held), :] = lax.fori_loop(0, n, highest, own[...])
        upper[pl.ds(held, 8), :] = jnp.zeros((8, block), f32)

        def add(t, total):
            for c in range(2):
                slot = asked[2 * t + c]
                value = jnp.exp(in1[t, c : c + 1, :] - upper[pl.ds(slot, 1), :])
                total = total + jnp.where(index == slot, value, 0.0)
            return total

        top = upper[pl.ds(0, held), :]
        first = jnp.where(own[...] > 0.5 * LOWEST, jnp.exp(own[...] - top), 0.0)
        total = lax.fori_loop(0, n, add, first)
        mine = jnp.where(total > 0.0, top + jnp.log(jnp.where(total > 0.0, total, 1.0)), LOWEST)
        outx[...] = mine
        here = inx.at[turn]
        here[plane] = mine
        send_all(lambda to: outx, here.at[plane], send2.at[turn], recv2.at[turn], "grp")
        wait_all(here, send2.at[turn], recv2.at[turn], "grp")
        planes = inx.shape[1]
        top = inx[turn, 0]
        for p in range(1, planes):
            top = jnp.maximum(top, inx[turn, p])
        total = jnp.exp(inx[turn, 0] - top)
        for p in range(1, planes):
            total = total + jnp.exp(inx[turn, p] - top)
        lse = top + jnp.log(total)
        both[0, pl.ds(0, held), :] = logwt_ref[...] - lse
        both[1, pl.ds(0, held), :] = lse
        both[:, pl.ds(held, 8), :] = jnp.zeros((2, 8, block), f32)

        @pl.loop(0, n)
        def _(s):
            to = lax.rem(me + s, n)
            for c in range(2):
                slot = asked[2 * to + c]
                out2[to, 2 * c : 2 * c + 1, :] = both[0, pl.ds(slot, 1), :]
                out2[to, 2 * c + 1 : 2 * c + 2, :] = both[1, pl.ds(slot, 1), :]

            @pl.when(s > 0)
            def _():
                remote(out2.at[to], in2.at[me], send3, recv3, to)

        bulk(chunks[1])
        in2[me] = out2[me]
        wait_all(in2, send3, recv3, "blk")
        for r in range(rows):
            beta_ref[8 * r : 8 * r + 1, :] = both[0, pl.ds(plane * rows + r, 1), :]
            lse_ref[8 * r : 8 * r + 1, :] = both[1, pl.ds(plane * rows + r, 1), :]
            for k in range(7):
                where = posn[8 * k + r]
                owner = where // 2
                rank = where % 2
                row = 8 * r + k + 1
                beta_ref[row : row + 1, :] = in2[owner, pl.ds(2 * rank, 1), :]
                lse_ref[row : row + 1, :] = in2[owner, pl.ds(2 * rank + 1, 1), :]

    compute(True, [0, 1])
    potentials(0, [2, 3])
    compute(False, [4, 5])
    potentials(1, [6, 7])
    got_ref[me] = packed_ref[0]
    wait_all(got_ref, send_f, recv_f, "blk")


def rounds(inv, asked, posn, x, own, far, logw, logwt, packed, cid):
    n = lax.axis_size("blk")
    planes = lax.axis_size("grp")
    pairs, block = 64, 256
    held = logwt.shape[0]
    smem = pl.BlockSpec(memory_space=pltpu.SMEM)
    vmem = pl.BlockSpec(memory_space=pltpu.VMEM)
    return pl.pallas_call(
        rounds_kernel,
        out_shape=(
            jax.ShapeDtypeStruct((pairs, block), f32),
            jax.ShapeDtypeStruct((pairs, block), f32),
            jax.ShapeDtypeStruct((2048, 1), f32),
            jax.ShapeDtypeStruct(packed.shape, bf16),
        ),
        in_specs=[smem] * 3 + [vmem] * 6,
        out_specs=(vmem,) * 4,
        scratch_shapes=[
            pltpu.VMEM((8, block, block), f32),
            pltpu.VMEM((pairs + 8, block), f32),
            pltpu.VMEM((n, 2, block), f32),
            pltpu.VMEM((n, 2, block), f32),
            pltpu.VMEM((held, block), f32),
            pltpu.VMEM((held + 8, block), f32),
            pltpu.VMEM((held, block), f32),
            pltpu.VMEM((2, planes, held, block), f32),
            pltpu.VMEM((2, held + 8, block), f32),
            pltpu.VMEM((n, 4, block), f32),
            pltpu.VMEM((n, 4, block), f32),
        ]
        + [pltpu.SemaphoreType.DMA] * 2
        + [pltpu.SemaphoreType.DMA((2,))] * 2
        + [pltpu.SemaphoreType.DMA] * 4,
        compiler_params=params(cid, 56),
    )(inv, asked, posn, x, own, far, logw, logwt, packed)


def gather_rows_kernel(width, x_ref, o_ref, wide):
    lanes = x_ref.shape[1]
    for c in range(lanes // 128):
        wide[c] = x_ref[:, c * 128 : (c + 1) * 128].astype(f32)
    for r in range(8):
        for h in range(2):
            for c in range(2):
                if width == 128:
                    got = wide[c, pl.ds(h * 8 + r, 64, stride=16), :]
                    o_ref[r, 0, (2 * h + c) * 64 : (2 * h + c + 1) * 64, :] = got.astype(bf16)
            if width == 64:
                got = wide[0, pl.ds(h * 8 + r, 64, stride=16), :].astype(bf16)
                o_ref[r, 0, 2 * h * 64 : (2 * h + 1) * 64, :] = got[:, 0:64]
                o_ref[r, 0, (2 * h + 1) * 64 : (2 * h + 2) * 64, :] = got[:, 64:128]


def gather_rows(x, width):
    flat = x.reshape(x.shape[0] * 16, 7 * 2 * width)
    return pl.pallas_call(
        functools.partial(gather_rows_kernel, width),
        grid=(7,),
        out_shape=jax.ShapeDtypeStruct((8, 7, 256, width), bf16),
        in_specs=[pl.BlockSpec((flat.shape[0], 2 * width), lambda k: (0, k))],
        out_specs=pl.BlockSpec((8, 1, 256, width), lambda k: (0, k, 0, 0)),
        scratch_shapes=[pltpu.VMEM((2 * width // 128, flat.shape[0], 128), f32)],
        compiler_params=params(),
    )(flat)


def scatter_rows_kernel(x_ref, o_ref, wide):
    for r in range(8):
        for h in range(2):
            for c in range(2):
                at = (2 * h + c) * 64
                wide[c, pl.ds(h * 8 + r, 64, stride=16), :] = x_ref[r, 0, at : at + 64, :].astype(f32)
    for c in range(2):
        o_ref[:, c * 128 : (c + 1) * 128] = wide[c].astype(bf16)


def scatter_rows(x):
    rows = 1024
    return pl.pallas_call(
        scatter_rows_kernel,
        grid=(7,),
        out_shape=jax.ShapeDtypeStruct((rows, 7 * 256), bf16),
        in_specs=[pl.BlockSpec((8, 1, 256, 128), lambda k: (0, k, 0, 0))],
        out_specs=pl.BlockSpec((rows, 256), lambda k: (0, k)),
        scratch_shapes=[pltpu.VMEM((2, rows, 128), f32)],
        compiler_params=params(),
    )(x).reshape(64, 16, 7 * 256)


def squares_row(t):
    wide = t.astype(f32)
    square = wide * wide
    high = square.astype(bf16)
    low = (square - high.astype(f32)).astype(bf16)
    ones = jnp.ones((8, t.shape[1]), bf16)
    return SQUARE * (nt(ones, high) + nt(ones, low))[0:1]


def row_scores(x, own_ref, far_ref, beta_ref, scores):
    top = None
    for k in range(8):
        t = own_ref[...] if k == 0 else far_ref[0, k - 1]
        z = nt(x, t) * CROSS + beta_ref[k : k + 1, :]
        scores[k] = z
        top = z if top is None else jnp.maximum(top, z)
    return jnp.max(top, axis=1, keepdims=True)


def transport_kernel(
    x_ref, own_ref, far_ref, beta_ref, lse_ref, alpha_ref, ownf_ref, farf_ref, srcf_ref,
    moved_ref, diag_ref, parts_ref, scores,
):
    x = x_ref[...]
    peak = row_scores(x, own_ref, far_ref, beta_ref, scores)
    total = None
    mixed = None
    for k in range(8):
        e = jnp.exp(scores[k] - peak)
        total = e if total is None else total + e
        feats = ownf_ref[...] if k == 0 else farf_ref[0, k - 1]
        term = nn(e.astype(bf16), feats)
        mixed = term if mixed is None else mixed + term
    moved_ref[...] = (mixed / jnp.sum(total, axis=1, keepdims=True)).astype(bf16)
    alpha = alpha_ref[...]
    srcf = srcf_ref[...]
    for k in range(8):
        t = own_ref[...] if k == 0 else far_ref[0, k - 1]
        w = jnp.exp(nt(x, t) * CROSS + alpha - lse_ref[k : k + 1, :]).astype(bf16)
        part = tn(w, srcf).astype(bf16)
        if k == 0:
            diag_ref[...] = part
        else:
            parts_ref[0, k - 1] = part


def transport(x, own, far, beta, lse, alpha, ownf, farf, srcf):
    def row(width):
        return pl.BlockSpec((256, width), lambda r: (r, 0))

    def four(width):
        return pl.BlockSpec((1, 7, 256, width), lambda r: (r, 0, 0, 0))

    small = pl.BlockSpec((8, 256), lambda r: (r, 0))
    return pl.pallas_call(
        transport_kernel,
        grid=(8,),
        out_shape=(
            jax.ShapeDtypeStruct((2048, 128), bf16),
            jax.ShapeDtypeStruct((2048, 128), bf16),
            jax.ShapeDtypeStruct((8, 7, 256, 128), bf16),
        ),
        in_specs=[row(64), row(64), four(64), small, small, row(1), row(128), four(128), row(128)],
        out_specs=(row(128), row(128), four(128)),
        scratch_shapes=[pltpu.VMEM((8, 256, 256), f32)],
        compiler_params=params(),
    )(x, own, far, beta, lse, alpha, ownf, farf, srcf)


def collect_kernel(ids_ref, got_ref, o_ref, total):
    k = pl.program_id(0)
    got = got_ref[...].astype(f32).reshape(64, 2, 8, 256)
    index = lax.broadcasted_iota(jnp.int32, (total.shape[1], 512), 0)
    hot = (index == ids_ref[0]).astype(f32).astype(bf16)
    for h in range(2):
        piece = got[:, h].reshape(512, 256).astype(bf16)
        term = nn(hot, piece)

        @pl.when(k == 0)
        def _():
            total[h] = term

        @pl.when(k > 0)
        def _():
            total[h] += term

    @pl.when(k == 6)
    def _():
        for h in range(2):
            o_ref[:, h * 256 : (h + 1) * 256] = total[h].astype(bf16)


def collect(ids, got):
    flat = got.reshape(1024, 7 * 256)
    return pl.pallas_call(
        collect_kernel,
        grid=(7,),
        out_shape=jax.ShapeDtypeStruct((2048, 512), bf16),
        in_specs=[
            pl.BlockSpec((1, 1, 512), lambda k: (k, 0, 0)),
            pl.BlockSpec((1024, 256), lambda k: (0, k)),
        ],
        out_specs=pl.BlockSpec((2048, 512), lambda k: (0, 0)),
        scratch_shapes=[pltpu.VMEM((2, 2048, 256), f32)],
        compiler_params=params(),
    )(ids, flat)


def shards(
    source_points, target_points, source_logw, target_logw,
    source_feats, target_feats, pair_owner, pair_slot,
):
    n = lax.axis_size("blk")
    plane = lax.axis_index("grp")
    me = lax.axis_index("blk")
    start = plane * 2048
    own_points = lax.dynamic_slice_in_dim(target_points, start, 2048, 0)
    own_feats = lax.dynamic_slice_in_dim(target_feats, start, 2048, 0)

    def stripes(own, width):
        out = own.reshape(8, 2, 2, 64, width).transpose(3, 1, 0, 2, 4)
        return out.reshape(64, 16, 2 * width)

    wanted = (pair_slot // 8) * 512 + pair_owner * 8 + pair_slot % 8
    ids = jnp.pad(wanted.T.reshape(1, 56), ((0, 0), (0, 72)))
    far_points, packed, near = front(
        ids, stripes(own_points, 64), stripes(own_feats, 128), 0
    )
    spin = lax.rem(jnp.arange(n) - me + n, n)
    table = near[spin][:, :56]
    ids_row = table.reshape(n, 7, 8).transpose(1, 0, 2).reshape(7, 1, n * 8)
    owner_of = (table // 8) % 64
    slot_of = (table // 512) * 8 + table % 8
    here = owner_of == me
    rank = jnp.cumsum(here.astype(jnp.int32), axis=1) - 1
    asked = jnp.stack(
        [jnp.min(jnp.where(here & (rank == c), slot_of, 32), axis=1) for c in range(2)], axis=1
    ).reshape(2 * n)
    owners = pair_owner.T.reshape(56)
    earlier = jnp.tril(jnp.ones((56, 56), bool), -1) & (owners[:, None] == owners[None, :])
    posn = owners * 2 + jnp.sum(earlier.astype(jnp.int32), axis=1)
    order = jnp.arange(56, dtype=jnp.int32)
    row_of = (order % 8) * 8 + order // 8 + 1
    inv = jnp.min(
        jnp.where(posn[None, :] == jnp.arange(2 * n)[:, None], row_of[None, :], 64), axis=1
    )

    logw = source_logw.reshape(2048, 1)
    owned_logw = target_logw.reshape(32, 256)
    beta, lse, alpha, got_feats = rounds(
        inv, asked, posn, source_points, own_points, far_points, logw, owned_logw, packed, 3
    )
    far_feats = gather_rows(got_feats, 128)
    moved_source, diag, parts = transport(
        source_points, own_points, far_points, beta, lse, alpha, own_feats, far_feats, source_feats
    )
    got_parts = exchange(scatter_rows(parts), 4)
    sums = collect(ids_row, got_parts)
    planes = spread(sums.reshape(4, 512, 512), 5)
    summed = jnp.sum(planes.astype(f32), axis=0).astype(bf16)
    final = exchange(
        summed.reshape(64, 8, 2, 256).transpose(0, 2, 1, 3).reshape(64, 16, 256), 6
    )
    far_sum = final.reshape(64, 2, 8, 2, 128).transpose(2, 1, 3, 0, 4).reshape(2048, 128)
    moved_target = (far_sum.astype(f32) + diag.astype(f32)).astype(bf16)
    return moved_source, moved_target


def solution(mesh):
    return jax.shard_map(
        shards,
        mesh=mesh,
        in_specs=(
            P(("blk", "grp"), None),
            P("blk", None),
            P(("blk", "grp")),
            P("blk"),
            P(("blk", "grp"), None),
            P("blk", None),
            P(("blk", "grp"), None),
            P(("blk", "grp"), None),
        ),
        out_specs=(P(("blk", "grp"), None), P(("blk", "grp"), None)),
        check_vma=False,
    )
```

time: 583 us -> 426 us (0.73)
  Pallas kernels: 502 us -> 397 us
  blocking collectives: 44.2 us -> 0 us
  starting transfers between devices: 8.02 us -> 0 us
    pallas_call x8 -> x2, Pallas kernels: 261 us -> 199 us  [the longest x1 115 us: rounds(): pl.pallas_call(rounds_kernel, out_shape=(jax.ShapeDtypeStruct((pairs, blo...]
    all_gather x1 -> x0, blocking collectives: 44.2 us -> none  [shards(): table = lax.all_gather(requests, 'blk')]
    pallas_call x3 -> x2, Pallas kernels: 162 us -> 123 us  [exchange(): pl.pallas_call(exchange_kernel, out_shape=jax.ShapeDtypeStruct(x.shape, x...]
    all_to_all x1 -> x0, starting transfers between devices: 8.02 us -> none  [shards(): lax.all_to_all(sent_feats, 'blk', split_axis=0, concat_axis=0, tiled=True)]
    unnamed x45 -> x36, local copies, waits for them, and re-layouts: 14.9 us -> 11 us
  transfers between devices with their start and end apart: 1 -> 0, of which waited for: 0 -> 0; matrix products, arithmetic and copies ran while one was open for 1% -> 0% of each run, Pallas kernels for 43% -> 0%
where the time goes in v2:
time: 426 us; the launch traced here: 425 us
  Pallas kernels  397 us (93%)
  local copies, waits for them, and re-layouts  21.9 us (5%)
  other arithmetic  5.43 us (1%)
    pallas_call x2, Pallas kernels, exchange(): pl.pallas_call(exchange_kernel, out_shape=jax.ShapeDtypeStruct(x.shape, x...  123 us
    pallas_call x1, Pallas kernels, rounds(): pl.pallas_call(rounds_kernel, out_shape=(jax.ShapeDtypeStruct((pairs, blo...  115 us
    pallas_call x1, Pallas kernels, front(): pl.pallas_call(front_kernel, out_shape=(jax.ShapeDtypeStruct((8, 7, 256,...  83.9 us
    pallas_call x1, Pallas kernels, spread(): pl.pallas_call(spread_kernel, out_shape=jax.ShapeDtypeStruct(x.shape, x.d...  25.7 us
    pallas_call x1, Pallas kernels, collect(): pl.pallas_call(collect_kernel, grid=(7,), out_shape=jax.ShapeDtypeStruct(...  20.8 us
    pallas_call x1, Pallas kernels, transport(): pl.pallas_call(transport_kernel, grid=(8,), out_shape=(jax.ShapeDtypeStru...  15.9 us
    unnamed x36, local copies, waits for them, and re-layouts  11 us

profile of v2, /device:TPU:1, one launch (start us, length us, event | category | flops | bytes accessed | tf_op | source)
XLA Modules:
  0.0 425.4 jit_solution(7457573069437695362)
XLA Ops:
  0.7 0.9 fusion.14
  3.5 1.4 reshape.139.logwt_ref
  4.8 1.0 constant_dynamic-slice_fusion.1
  6.2 2.1 copy.41.x_ref
  8.2 1.1 copy.52
  9.4 1.3 copy.51
  10.7 1.3 reshape.133.points_ref
  12.0 1.4 copy.40.logw_ref
  13.4 1.0 copy-done.8
  14.4 83.9 %shard_map.95 = (bf16[8,7,256,64]{3,2,1,0:T(8,128)(2,1)S(1)}, bf16[64,16,1792]{2,1,0:T(8,128)(2,1)}, s32[64,128]{1,0:T(8,128)S(1)}) custom-call(s32[1,128]{1,0:T(1,128)S(1)} %pad.4.ids_ref, bf16[64,16,128]{2,1,0:T(8,128)(2,1)S(1)} %reshape.133.points_ref, bf16[64,16,256]{2,1,0:T(8,128)(2,1)S(1)} %bitcast.45), custom_call_target="tpu_custom_call" | custom-call | tf_op jit(solution)/shard_map/pallas_call | solution.py:209
  98.4 1.8 copy-done.2
  102.1 115.4 %shard_map.96 = (f32[64,256]{1,0:T(8,128)}, f32[64,256]{1,0:T(8,128)}, f32[2048,1]{1,0:T(8,128)}, bf16[64,16,1792]{2,1,0:T(8,128)(2,1)}) custom-call(s32[128]{0:T(128)} %select_reduce_fusion.2.inv, s32[128]{0:T(128)} %reshape.137.asked, s32[56]{0:T(128)} %copy-done.16, bf16[2048,64]{1,0:T(8,128)(2,1)} %copy.41.x_ref, bf16[2048,64]{1,0:T(8,128)(2,1)} %copy-done.5, ...), custom_call_target="tpu_custom_call" | custom-call | tf_op jit(solution)/shard_map/pallas_call | solution.py:419
  217.9 6.0 %shard_map.97.farf_ref = bf16[8,7,256,128]{3,2,1,0:T(8,128)(2,1)S(1)} custom-call(bf16[1024,1792]{1,0:T(8,128)(2,1)} %bitcast.47), custom_call_target="tpu_custom_call" | custom-call | tf_op jit(solution)/shard_map/pallas_call | solution.py:467
  223.9 1.8 copy-done.3
  225.7 15.9 %shard_map.98 = (bf16[2048,128]{1,0:T(8,128)(2,1)}, bf16[2048,128]{1,0:T(8,128)(2,1)S(1)}, bf16[8,7,256,128]{3,2,1,0:T(8,128)(2,1)}) custom-call(bf16[2048,64]{1,0:T(8,128)(2,1)S(1)} %copy-done.7, bf16[2048,64]{1,0:T(8,128)(2,1)S(1)} %copy-done.6, bf16[8,7,256,64]{3,2,1,0:T(8,128)(2,1)} %copy-done.2, f32[64,256]{1,0:T(8,128)S(1)} %copy-done.13, ...), custom_call_target="tpu_custom_call" | custom-call | tf_op jit(solution)/shard_map/pallas_call | solution.py:555
  242.4 6.8 %shard_map.99 = bf16[1024,1792]{1,0:T(8,128)(2,1)S(1)} custom-call(bf16[8,7,256,128]{3,2,1,0:T(8,128)(2,1)} %get-tuple-element.20.x_ref), custom_call_target="tpu_custom_call" | custom-call | tf_op jit(solution)/shard_map/pallas_call | solution.py:490
  249.2 1.8 copy-done.1
  251.0 88.1 %shard_map.100 = bf16[64,16,1792]{2,1,0:T(8,128)(2,1)S(1)} custom-call(bf16[64,16,1792]{2,1,0:T(8,128)(2,1)} %bitcast.40), custom_call_target="tpu_custom_call" | custom-call | tf_op jit(solution)/shard_map/pallas_call | solution.py:98
  339.1 20.8 %shard_map.101 = bf16[2048,512]{1,0:T(8,128)(2,1)S(1)} custom-call(s32[7,1,512]{2,1,0:T(1,128)S(1)} %reshape.158.ids_ref, bf16[1024,1792]{1,0:T(8,128)(2,1)S(1)} %bitcast.41), custom_call_target="tpu_custom_call" | custom-call | tf_op jit(solution)/shard_map/pallas_call | solution.py:595
  359.9 25.7 %shard_map.102 = bf16[4,512,512]{2,1,0:T(8,128)(2,1)S(1)} custom-call(bf16[4,512,512]{2,1,0:T(8,128)(2,1)S(1)} %bitcast.42), custom_call_target="tpu_custom_call" | custom-call | tf_op jit(solution)/shard_map/pallas_call | solution.py:245
  385.6 1.3 copy-done.4
  387.0 2.2 reduce_sum.22
  389.2 34.5 %shard_map.103 = bf16[64,16,256]{2,1,0:T(8,128)(2,1)S(1)} custom-call(bf16[64,16,256]{2,1,0:T(8,128)(2,1)S(1)} %bitcast.46), custom_call_target="tpu_custom_call" | custom-call | tf_op jit(solution)/shard_map/pallas_call | solution.py:98
  424.5 0.9 fusion
  (54 shorter events, 6.0 us)
Async XLA Ops:
  0.6 5.5 %copy-start = (bf16[8192,128]{1,0:T(8,128)(2,1)S(1)}, bf16[8192,128]{1,0:T(8,128)(2,1)}, u32[]{:S(2)}) copy-start(bf16[8192,128]{1,0:T(8,128)(2,1)} %param.13) | copy-start | bytes 6291460
  0.6 11.4 %copy-start.15 = (f32[2048]{0:T(1024)S(1)}, f32[2048]{0:T(1024)}, u32[]{:S(2)}) copy-start(f32[2048]{0:T(1024)} %param.10) | copy-start | bytes 24580
  2.8 95.6 %copy-start.16 = (s32[56]{0:T(128)}, s32[56]{0:T(128)S(1)}, u32[]{:S(2)}) copy-start(s32[56]{0:T(128)S(1)} %get-tuple-element.28.posn) | copy-start | bytes 676
  6.1 96.0 %copy-start.5 = (bf16[2048,64]{1,0:T(8,128)(2,1)}, bf16[2048,64]{1,0:T(8,128)(2,1)S(1)}, u32[]{:S(2)}) copy-start(bf16[2048,64]{1,0:T(8,128)(2,1)S(1)} %copy.48.own_ref) | copy-start | bytes 786436
  13.4 1.0 copy-start.8
  98.4 1.8 copy-start.2
  217.8 7.9 %copy-start.6 = (bf16[2048,64]{1,0:T(8,128)(2,1)S(1)}, bf16[2048,64]{1,0:T(8,128)(2,1)}, u32[]{:S(2)}) copy-start(bf16[2048,64]{1,0:T(8,128)(2,1)} %copy-done.5) | copy-start | bytes 786436
  217.8 7.9 %copy-start.7 = (bf16[2048,64]{1,0:T(8,128)(2,1)S(1)}, bf16[2048,64]{1,0:T(8,128)(2,1)}, u32[]{:S(2)}) copy-start(bf16[2048,64]{1,0:T(8,128)(2,1)} %copy.41.x_ref) | copy-start | bytes 786436
  217.8 7.9 %copy-start.9 = (f32[2048,1]{1,0:T(8,128)S(1)}, f32[2048,1]{1,0:T(8,128)}, u32[]{:S(2)}) copy-start(f32[2048,1]{1,0:T(8,128)} %get-tuple-element.17.alpha_ref) | copy-start | bytes 24580
  217.8 7.9 %copy-start.12 = (bf16[2048,128]{1,0:T(8,128)(2,1)S(1)}, bf16[2048,128]{1,0:T(8,128)(2,1)}, u32[]{:S(2)}) copy-start(bf16[2048,128]{1,0:T(8,128)(2,1)} %srcf_ref.1) | copy-start | bytes 1572868
  217.8 7.9 %copy-start.13 = (f32[64,256]{1,0:T(8,128)S(1)}, f32[64,256]{1,0:T(8,128)}, u32[]{:S(2)}) copy-start(f32[64,256]{1,0:T(8,128)} %get-tuple-element.15.beta_ref) | copy-start | bytes 196612
  217.8 7.9 %copy-start.14 = (f32[64,256]{1,0:T(8,128)S(1)}, f32[64,256]{1,0:T(8,128)}, u32[]{:S(2)}) copy-start(f32[64,256]{1,0:T(8,128)} %get-tuple-element.16.lse_ref) | copy-start | bytes 196612
  223.9 1.8 copy-start.3
  241.6 0.8 copy-start.10
  249.2 1.8 copy-start.1
  385.6 1.3 copy-start.4
  387.0 37.6 %copy-start.11 = (bf16[2048,128]{1,0:T(8,128)(2,1)S(1)}, bf16[2048,128]{1,0:T(8,128)(2,1)}, u32[]{:S(2)}) copy-start(bf16[2048,128]{1,0:T(8,128)(2,1)} %copy-done.10) | copy-start | bytes 1572868

commit v3 on v2

--- a/solution.py
+++ b/solution.py
@@ -82,27 +82,6 @@
     )
     copy.wait_send()
     copy.wait_recv()
-
-
-def exchange_kernel(x_ref, o_ref, send, recv, own):
-    me = lax.axis_index("blk")
-    greet(["blk"])
-    mine = pltpu.make_async_copy(x_ref.at[me], o_ref.at[me], own)
-    mine.start()
-    send_all(lambda to: x_ref.at[to], o_ref.at[me], send, recv, "blk")
-    mine.wait()
-    wait_all(o_ref, send, recv, "blk")
-
-
-def exchange(x, cid):
-    return pl.pallas_call(
-        exchange_kernel,
-        out_shape=jax.ShapeDtypeStruct(x.shape, x.dtype),
-        in_specs=[pl.BlockSpec(memory_space=pltpu.VMEM)],
-        out_specs=pl.BlockSpec(memory_space=pltpu.VMEM),
-        scratch_shapes=[pltpu.SemaphoreType.DMA] * 3,
-        compiler_params=params(cid),
-    )(x)
 
 
 def front_kernel(
@@ -229,27 +208,6 @@
         + [pltpu.SemaphoreType.DMA] * 13,
         compiler_params=params(cid),
     )(ids, points, feats)
-
-
-def spread_kernel(x_ref, o_ref, send, recv, own):
-    plane = lax.axis_index("grp")
-    greet(["grp"])
-    mine = pltpu.make_async_copy(x_ref.at[plane], o_ref.at[plane], own)
-    mine.start()
-    send_all(lambda to: x_ref.at[to], o_ref.at[plane], send, recv, "grp")
-    mine.wait()
-    wait_all(o_ref, send, recv, "grp")
-
-
-def spread(x, cid):
-    return pl.pallas_call(
-        spread_kernel,
-        out_shape=jax.ShapeDtypeStruct(x.shape, x.dtype),
-        in_specs=[pl.BlockSpec(memory_space=pltpu.VMEM)],
-        out_specs=pl.BlockSpec(memory_space=pltpu.VMEM),
-        scratch_shapes=[pltpu.SemaphoreType.DMA] * 3,
-        compiler_params=params(cid),
-    )(x)
 
 
 def rounds_kernel(
@@ -446,58 +404,6 @@
     )(inv, asked, posn, x, own, far, logw, logwt, packed)
 
 
-def gather_rows_kernel(width, x_ref, o_ref, wide):
-    lanes = x_ref.shape[1]
-    for c in range(lanes // 128):
-        wide[c] = x_ref[:, c * 128 : (c + 1) * 128].astype(f32)
-    for r in range(8):
-        for h in range(2):
-            for c in range(2):
-                if width == 128:
-                    got = wide[c, pl.ds(h * 8 + r, 64, stride=16), :]
-                    o_ref[r, 0, (2 * h + c) * 64 : (2 * h + c + 1) * 64, :] = got.astype(bf16)
-            if width == 64:
-                got = wide[0, pl.ds(h * 8 + r, 64, stride=16), :].astype(bf16)
-                o_ref[r, 0, 2 * h * 64 : (2 * h + 1) * 64, :] = got[:, 0:64]
-                o_ref[r, 0, (2 * h + 1) * 64 : (2 * h + 2) * 64, :] = got[:, 64:128]
-
-
-def gather_rows(x, width):
-    flat = x.reshape(x.shape[0] * 16, 7 * 2 * width)
-    return pl.pallas_call(
-        functools.partial(gather_rows_kernel, width),
-        grid=(7,),
-        out_shape=jax.ShapeDtypeStruct((8, 7, 256, width), bf16),
-        in_specs=[pl.BlockSpec((flat.shape[0], 2 * width), lambda k: (0, k))],
-        out_specs=pl.BlockSpec((8, 1, 256, width), lambda k: (0, k, 0, 0)),
-        scratch_shapes=[pltpu.VMEM((2 * width // 128, flat.shape[0], 128), f32)],
-        compiler_params=params(),
-    )(flat)
-
-
-def scatter_rows_kernel(x_ref, o_ref, wide):
-    for r in range(8):
-        for h in range(2):
-            for c in range(2):
-                at = (2 * h + c) * 64
-                wide[c, pl.ds(h * 8 + r, 64, stride=16), :] = x_ref[r, 0, at : at + 64, :].astype(f32)
-    for c in range(2):
-        o_ref[:, c * 128 : (c + 1) * 128] = wide[c].astype(bf16)
-
-
-def scatter_rows(x):
-    rows = 1024
-    return pl.pallas_call(
-        scatter_rows_kernel,
-        grid=(7,),
-        out_shape=jax.ShapeDtypeStruct((rows, 7 * 256), bf16),
-        in_specs=[pl.BlockSpec((8, 1, 256, 128), lambda k: (0, k, 0, 0))],
-        out_specs=pl.BlockSpec((rows, 256), lambda k: (0, k)),
-        scratch_shapes=[pltpu.VMEM((2, rows, 128), f32)],
-        compiler_params=params(),
-    )(x).reshape(64, 16, 7 * 256)
-
-
 def squares_row(t):
     wide = t.astype(f32)
     square = wide * wide
@@ -507,103 +413,227 @@
     return SQUARE * (nt(ones, high) + nt(ones, low))[0:1]
 
 
-def row_scores(x, own_ref, far_ref, beta_ref, scores):
-    top = None
-    for k in range(8):
-        t = own_ref[...] if k == 0 else far_ref[0, k - 1]
-        z = nt(x, t) * CROSS + beta_ref[k : k + 1, :]
-        scores[k] = z
-        top = z if top is None else jnp.maximum(top, z)
-    return jnp.max(top, axis=1, keepdims=True)
-
-
-def transport_kernel(
-    x_ref, own_ref, far_ref, beta_ref, lse_ref, alpha_ref, ownf_ref, farf_ref, srcf_ref,
-    moved_ref, diag_ref, parts_ref, scores,
+def back_kernel(
+    ids_ref, x_ref, own_ref, far_ref, beta_ref, lse_ref, alpha_ref, ownf_ref, gotf_ref, srcf_ref,
+    moved_ref, out_ref,
+    scores, farf, wide, diag, out_h, in_h, pieces, total, out_x, in_x, out_f, in_f,
+    send_m, recv_m, send_x, recv_x, send_f, recv_f,
 ):
-    x = x_ref[...]
-    peak = row_scores(x, own_ref, far_ref, beta_ref, scores)
-    total = None
-    mixed = None
-    for k in range(8):
-        e = jnp.exp(scores[k] - peak)
-        total = e if total is None else total + e
-        feats = ownf_ref[...] if k == 0 else farf_ref[0, k - 1]
-        term = nn(e.astype(bf16), feats)
-        mixed = term if mixed is None else mixed + term
-    moved_ref[...] = (mixed / jnp.sum(total, axis=1, keepdims=True)).astype(bf16)
-    alpha = alpha_ref[...]
-    srcf = srcf_ref[...]
-    for k in range(8):
-        t = own_ref[...] if k == 0 else far_ref[0, k - 1]
-        w = jnp.exp(nt(x, t) * CROSS + alpha - lse_ref[k : k + 1, :]).astype(bf16)
-        part = tn(w, srcf).astype(bf16)
-        if k == 0:
-            diag_ref[...] = part
-        else:
-            parts_ref[0, k - 1] = part
-
-
-def transport(x, own, far, beta, lse, alpha, ownf, farf, srcf):
-    def row(width):
-        return pl.BlockSpec((256, width), lambda r: (r, 0))
-
-    def four(width):
-        return pl.BlockSpec((1, 7, 256, width), lambda r: (r, 0, 0, 0))
-
-    small = pl.BlockSpec((8, 256), lambda r: (r, 0))
+    n = lax.axis_size("blk")
+    me = lax.axis_index("blk")
+    plane = lax.axis_index("grp")
+    greet(["blk", "grp"])
+
+    def remote(src, dst, send, recv, to):
+        pltpu.make_async_remote_copy(
+            src_ref=src,
+            dst_ref=dst,
+            send_sem=send,
+            recv_sem=recv,
+            device_id={"blk": to},
+            device_id_type=MESH,
+        ).start()
+
+    def parts(h):
+        @pl.loop(0, 8)
+        def _(r):
+            at = pl.ds(pl.multiple_of(r * 256, 256), 256)
+            x = x_ref[at, :]
+            alpha = alpha_ref[at, :]
+            srcf = srcf_ref[at, :]
+            half = pl.ds(pl.multiple_of(r * 256 + 128 * h, 128), 128)
+            for k in range(8):
+                t = own_ref[half, :] if k == 0 else far_ref[r, k - 1, 128 * h : 128 * h + 128, :]
+                shift = lse_ref[pl.ds(8 * r + k, 1), :][:, 128 * h : 128 * h + 128]
+                w = jnp.exp(nt(x, t) * CROSS + alpha - shift).astype(bf16)
+                part = tn(w, srcf).astype(bf16).astype(f32)
+                if k == 0:
+                    diag[half, :] = part
+                else:
+                    for c in range(2):
+                        wide[k - 1, pl.ds(c * 8 + r, n, stride=16), :] = part[64 * c : 64 * c + 64]
+
+        for k in range(7):
+            out_h[h, :, :, 128 * k : 128 * (k + 1)] = wide[k].reshape(n, 16, 128).astype(bf16)
+        for chunk in range(8):
+
+            @pl.loop(0, n // 8)
+            def _(j):
+                s = 8 * j + chunk
+
+                @pl.when(s > 0)
+                def _():
+                    to = lax.rem(me + s, n)
+                    remote(
+                        out_h.at[h, to], in_h.at[h, me], send_m.at[h], recv_m.at[h, chunk // 2], to
+                    )
+
+        in_h[h, me] = out_h[h, me]
+
+    def rows():
+        for k in range(7):
+            for c in range(2):
+                lanes = 128 * (2 * k + c)
+                buffer = (2 * k + c) % 7
+                wide[buffer] = gotf_ref[:, :, lanes : lanes + 128].astype(f32).reshape(16 * n, 128)
+                for r in range(8):
+                    for h in range(2):
+                        got = wide[buffer, pl.ds(h * 8 + r, n, stride=16), :]
+                        farf[r, k, 64 * (2 * h + c) : 64 * (2 * h + c + 1), :] = got.astype(bf16)
+
+        @pl.loop(0, 8)
+        def _(r):
+            at = pl.ds(pl.multiple_of(r * 256, 256), 256)
+            x = x_ref[at, :]
+            top = None
+            for k in range(8):
+                t = own_ref[at, :] if k == 0 else far_ref[r, k - 1]
+                z = nt(x, t) * CROSS + beta_ref[pl.ds(8 * r + k, 1), :]
+                scores[k] = z
+                top = z if top is None else jnp.maximum(top, z)
+            peak = jnp.max(top, axis=1, keepdims=True)
+            weight = None
+            mixed = None
+            for k in range(8):
+                e = jnp.exp(scores[k] - peak)
+                weight = e if weight is None else weight + e
+                feats = ownf_ref[at, :] if k == 0 else farf[r, k - 1]
+                term = nn(e.astype(bf16), feats)
+                mixed = term if mixed is None else mixed + term
+            moved_ref[at, :] = (mixed / jnp.sum(weight, axis=1, keepdims=True)).astype(bf16)
+
+    def collect(h, group):
+        first = 1 if group == 0 else 0
+        got = in_h.at[h, pl.ds(0, 16 - first)]
+        pltpu.make_async_remote_copy(
+            src_ref=got,
+            dst_ref=got,
+            send_sem=send_m.at[h],
+            recv_sem=recv_m.at[h, group],
+            device_id={"blk": lax.rem(me + 1, n)},
+            device_id_type=MESH,
+        ).wait_recv()
+
+        @pl.loop(0, 8)
+        def _(pair):
+            chunk = 2 * group + pair // 4
+            j = lax.rem(2 * pair, 8)
+            one = in_h[h, lax.rem(me - 8 * j - chunk + 2 * n, n)].astype(f32)
+            two = in_h[h, lax.rem(me - 8 * j - 8 - chunk + 2 * n, n)].astype(f32)
+            for k in range(7):
+                for c in range(2):
+                    lanes = slice(128 * k, 128 * (k + 1))
+                    both = jnp.concatenate(
+                        [one[8 * c : 8 * c + 8, lanes], two[8 * c : 8 * c + 8, lanes]], axis=0
+                    )
+                    at = pl.ds(pl.multiple_of(128 * k + 16 * pair, 16), 16)
+                    pieces[at, 128 * c : 128 * (c + 1)] = both.astype(bf16)
+
+        @pl.loop(0, 8)
+        def _(m):
+            at = pl.ds(pl.multiple_of(256 * m, 256), 256)
+            index = lax.broadcasted_iota(jnp.int32, (256, 896), 0) + 256 * m
+            hot = (index == ids_ref[group]).astype(f32).astype(bf16)
+            term = nn(hot, pieces[...])
+            if group == 0:
+                total[at, :] = term
+            else:
+                total[at, :] += term
+
+    def spread(h):
+        planes = out_x.shape[1]
+        for p in range(planes):
+            out_x[h, p] = total[512 * p : 512 * (p + 1), :].astype(bf16)
+        in_x[h, plane] = out_x[h, plane]
+        send_all(
+            lambda to: out_x.at[h, to], in_x.at[h, plane], send_x.at[h], recv_x.at[h], "grp"
+        )
+
+    def finish(h):
+        wait_all(in_x.at[h], send_x.at[h], recv_x.at[h], "grp")
+        planes = in_x.shape[1]
+        whole = in_x[h, 0].astype(f32)
+        for p in range(1, planes):
+            whole = whole + in_x[h, p].astype(f32)
+        both = jnp.concatenate(
+            [whole[:, 128 * c : 128 * (c + 1)].reshape(n, 8, 128) for c in range(2)], axis=1
+        )
+        out_f[h] = both.astype(bf16)
+
+        @pl.loop(1, n)
+        def _(s):
+            to = lax.rem(me + s, n)
+            remote(out_f.at[h, to], in_f.at[h, me], send_f.at[h], recv_f.at[h], to)
+
+        in_f[h, me] = out_f[h, me]
+
+    def deliver(h):
+        wait_all(in_f.at[h], send_f.at[h], recv_f.at[h], "blk")
+        wide[h] = in_f[h].astype(f32).reshape(16 * n, 128)
+        for s in range(8):
+            for c in range(2):
+                at = 256 * s + 64 * (2 * h + c)
+                got = wide[h, pl.ds(c * 8 + s, n, stride=16), :]
+                out_ref[at : at + 64, :] = (got + diag[at : at + 64, :]).astype(bf16)
+
+    parts(0)
+    parts(1)
+    rows()
+    for group in range(4):
+        collect(0, group)
+    spread(0)
+    collect(1, 0)
+    collect(1, 1)
+    finish(0)
+    collect(1, 2)
+    collect(1, 3)
+    spread(1)
+    finish(1)
+    deliver(0)
+    deliver(1)
+    for h in range(2):
+        sent = out_h.at[h, pl.ds(0, n - 1)]
+        pltpu.make_async_remote_copy(
+            src_ref=sent,
+            dst_ref=sent,
+            send_sem=send_m.at[h],
+            recv_sem=recv_m.at[h, 0],
+            device_id={"blk": lax.rem(me + 1, n)},
+            device_id_type=MESH,
+        ).wait_send()
+
+
+def back(ids, x, own, far, beta, lse, alpha, ownf, gotf, srcf, cid):
+    n = lax.axis_size("blk")
+    planes = lax.axis_size("grp")
+    vmem = pl.BlockSpec(memory_space=pltpu.VMEM)
     return pl.pallas_call(
-        transport_kernel,
-        grid=(8,),
+        back_kernel,
         out_shape=(
             jax.ShapeDtypeStruct((2048, 128), bf16),
             jax.ShapeDtypeStruct((2048, 128), bf16),
-            jax.ShapeDtypeStruct((8, 7, 256, 128), bf16),
         ),
-        in_specs=[row(64), row(64), four(64), small, small, row(1), row(128), four(128), row(128)],
-        out_specs=(row(128), row(128), four(128)),
-        scratch_shapes=[pltpu.VMEM((8, 256, 256), f32)],
-        compiler_params=params(),
-    )(x, own, far, beta, lse, alpha, ownf, farf, srcf)
-
-
-def collect_kernel(ids_ref, got_ref, o_ref, total):
-    k = pl.program_id(0)
-    got = got_ref[...].astype(f32).reshape(64, 2, 8, 256)
-    index = lax.broadcasted_iota(jnp.int32, (total.shape[1], 512), 0)
-    hot = (index == ids_ref[0]).astype(f32).astype(bf16)
-    for h in range(2):
-        piece = got[:, h].reshape(512, 256).astype(bf16)
-        term = nn(hot, piece)
-
-        @pl.when(k == 0)
-        def _():
-            total[h] = term
-
-        @pl.when(k > 0)
-        def _():
-            total[h] += term
-
-    @pl.when(k == 6)
-    def _():
-        for h in range(2):
-            o_ref[:, h * 256 : (h + 1) * 256] = total[h].astype(bf16)
-
-
-def collect(ids, got):
-    flat = got.reshape(1024, 7 * 256)
-    return pl.pallas_call(
-        collect_kernel,
-        grid=(7,),
-        out_shape=jax.ShapeDtypeStruct((2048, 512), bf16),
-        in_specs=[
-            pl.BlockSpec((1, 1, 512), lambda k: (k, 0, 0)),
-            pl.BlockSpec((1024, 256), lambda k: (0, k)),
-        ],
-        out_specs=pl.BlockSpec((2048, 512), lambda k: (0, 0)),
-        scratch_shapes=[pltpu.VMEM((2, 2048, 256), f32)],
-        compiler_params=params(),
-    )(ids, flat)
+        in_specs=[vmem] * 10,
+        out_specs=(vmem,) * 2,
+        scratch_shapes=[
+            pltpu.VMEM((8, 256, 256), f32),
+            pltpu.VMEM((8, 7, 256, 128), bf16),
+            pltpu.VMEM((7, 16 * n, 128), f32),
+            pltpu.VMEM((2048, 128), f32),
+            pltpu.VMEM((2, n, 16, 896), bf16),
+            pltpu.VMEM((2, n, 16, 896), bf16),
+            pltpu.VMEM((896, 256), bf16),
+            pltpu.VMEM((2048, 256), f32),
+            pltpu.VMEM((2, planes, 512, 256), bf16),
+            pltpu.VMEM((2, planes, 512, 256), bf16),
+            pltpu.VMEM((2, n, 16, 128), bf16),
+            pltpu.VMEM((2, n, 16, 128), bf16),
+            pltpu.SemaphoreType.DMA((2,)),
+            pltpu.SemaphoreType.DMA((2, 4)),
+        ]
+        + [pltpu.SemaphoreType.DMA((2,))] * 4,
+        compiler_params=params(cid, 60),
+    )(ids, x, own, far, beta, lse, alpha, ownf, gotf, srcf)
 
 
 def shards(
@@ -628,7 +658,10 @@
     )
     spin = lax.rem(jnp.arange(n) - me + n, n)
     table = near[spin][:, :56]
-    ids_row = table.reshape(n, 7, 8).transpose(1, 0, 2).reshape(7, 1, n * 8)
+    message = jnp.arange(n)
+    away = 8 * (message % 8) + message // 8
+    ids_row = near[(n - away) % n][:, :56].reshape(4, 16, 7, 8).transpose(0, 2, 1, 3)
+    ids_row = ids_row.reshape(4, 1, 896)
     owner_of = (table // 8) % 64
     slot_of = (table // 512) * 8 + table % 8
     here = owner_of == me
@@ -650,19 +683,10 @@
     beta, lse, alpha, got_feats = rounds(
         inv, asked, posn, source_points, own_points, far_points, logw, owned_logw, packed, 3
     )
-    far_feats = gather_rows(got_feats, 128)
-    moved_source, diag, parts = transport(
-        source_points, own_points, far_points, beta, lse, alpha, own_feats, far_feats, source_feats
+    moved_source, moved_target = back(
+        ids_row, source_points, own_points, far_points, beta, lse, alpha,
+        own_feats, got_feats, source_feats, 4,
     )
-    got_parts = exchange(scatter_rows(parts), 4)
-    sums = collect(ids_row, got_parts)
-    planes = spread(sums.reshape(4, 512, 512), 5)
-    summed = jnp.sum(planes.astype(f32), axis=0).astype(bf16)
-    final = exchange(
-        summed.reshape(64, 8, 2, 256).transpose(0, 2, 1, 3).reshape(64, 16, 256), 6
-    )
-    far_sum = final.reshape(64, 2, 8, 2, 128).transpose(2, 1, 3, 0, 4).reshape(2048, 128)
-    moved_target = (far_sum.astype(f32) + diag.astype(f32)).astype(bf16)
     return moved_source, moved_target
 
 

time: 426 us -> 346 us (0.81)
  Pallas kernels: 397 us -> 325 us
  local copies, waits for them, and re-layouts: 21.9 us -> 16.7 us
    pallas_call x7 -> x1, Pallas kernels: 198 us -> 126 us  [back(): pl.pallas_call(back_kernel, out_shape=(jax.ShapeDtypeStruct((2048, 128),...]
    unnamed x36 -> x16, local copies, waits for them, and re-layouts: 11 us -> 7.78 us
where the time goes in v3:
time: 346 us
  Pallas kernels  325 us (94%)
  local copies, waits for them, and re-layouts  16.7 us (5%)
    pallas_call x1, Pallas kernels, back(): pl.pallas_call(back_kernel, out_shape=(jax.ShapeDtypeStruct((2048, 128),...  126 us
    pallas_call x1, Pallas kernels, rounds(): pl.pallas_call(rounds_kernel, out_shape=(jax.ShapeDtypeStruct((pairs, blo...  115 us
    pallas_call x1, Pallas kernels, front(): pl.pallas_call(front_kernel, out_shape=(jax.ShapeDtypeStruct((8, 7, 256,...  84.4 us
    unnamed x16, local copies, waits for them, and re-layouts  7.78 us

profile of v3, /device:TPU:1, one launch (start us, length us, event | category | flops | bytes accessed | tf_op | source)
XLA Modules:
  0.0 345.9 jit_solution(13140065903945832456)
XLA Ops:
  0.6 0.9 fusion.13
  1.7 1.0 constant_dynamic-slice_fusion.1
  2.7 0.3 copy.45.own_ref
  3.0 0.5 copy.48
  3.5 0.2 reshape.209.points_ref
  3.8 0.3 copy.49
  4.2 84.4 %shard_map.95 = (bf16[8,7,256,64]{3,2,1,0:T(8,128)(2,1)S(1)}, bf16[64,16,1792]{2,1,0:T(8,128)(2,1)}, s32[64,128]{1,0:T(8,128)S(1)}) custom-call(s32[1,128]{1,0:T(1,128)S(1)} %pad.4.ids_ref, bf16[64,16,128]{2,1,0:T(8,128)(2,1)S(1)} %reshape.209.points_ref, bf16[64,16,256]{2,1,0:T(8,128)(2,1)S(1)} %bitcast.27), custom_call_target="tpu_custom_call" | custom-call | tf_op jit(solution)/shard_map/pallas_call | solution.py:188
  88.6 1.8 copy-done.1
  90.3 0.5 fusion.25
  90.9 0.6 gather_fusion
  91.8 0.8 reshape.234.ids_ref
  92.6 2.0 copy.42.x_ref
  94.5 0.8 copy.37
  95.6 0.6 select_reduce_fusion.2.inv
  96.2 0.6 pad_clamp_fusion
  96.8 0.6 gather_fusion.1
  97.5 0.2 reduce_window_sum.11
  98.0 0.7 reshape.215.asked
  98.7 2.1 copy.40.logw_ref
  100.8 0.6 reshape.217.logwt_ref
  101.4 115.0 %shard_map.96 = (f32[64,256]{1,0:T(8,128)}, f32[64,256]{1,0:T(8,128)}, f32[2048,1]{1,0:T(8,128)}, bf16[64,16,1792]{2,1,0:T(8,128)(2,1)}) custom-call(s32[128]{0:T(128)} %select_reduce_fusion.2.inv, s32[128]{0:T(128)} %reshape.215.asked, s32[56]{0:T(128)} %copy-done.5, bf16[2048,64]{1,0:T(8,128)(2,1)} %copy.42.x_ref, bf16[2048,64]{1,0:T(8,128)(2,1)} %copy-done.2, ...), custom_call_target="tpu_custom_call" | custom-call | tf_op jit(solution)/shard_map/pallas_call | solution.py:377
  216.5 125.7 %shard_map.97 = (bf16[2048,128]{1,0:T(8,128)(2,1)}, bf16[2048,128]{1,0:T(8,128)(2,1)}) custom-call(s32[4,1,896]{2,1,0:T(1,128)} %reshape.234.ids_ref, bf16[2048,64]{1,0:T(8,128)(2,1)} %copy.42.x_ref, bf16[2048,64]{1,0:T(8,128)(2,1)} %copy-done.2, bf16[8,7,256,64]{3,2,1,0:T(8,128)(2,1)} %copy-done.1, f32[64,256]{1,0:T(8,128)} %get-tuple-element.12.beta_ref, ...), custom_call_target="tpu_custom_call" | custom-call | tf_op jit(solution)/shard_map/pallas_call | solution.py:610
  342.2 1.9 copy.52
  344.1 1.9 copy.53
  (27 shorter events, 1.2 us)
Async XLA Ops:
  0.6 3.1 copy-start
  2.9 97.8 %copy-start.2 = (bf16[2048,64]{1,0:T(8,128)(2,1)}, bf16[2048,64]{1,0:T(8,128)(2,1)S(1)}, u32[]{:S(2)}) copy-start(bf16[2048,64]{1,0:T(8,128)(2,1)S(1)} %copy.45.own_ref) | copy-start | bytes 786436
  3.5 97.3 %copy-start.4 = (f32[8192]{0:T(1024)S(1)}, f32[8192]{0:T(1024)}, u32[]{:S(2)}) copy-start(f32[8192]{0:T(1024)} %param.11) | copy-start | bytes 98308
  3.8 212.6 %copy-start.3 = (bf16[2048,128]{1,0:T(8,128)(2,1)}, bf16[2048,128]{1,0:T(8,128)(2,1)S(1)}, u32[]{:S(2)}) copy-start(bf16[2048,128]{1,0:T(8,128)(2,1)S(1)} %constant_dynamic-slice_fusion.ownf_ref) | copy-start | bytes 1572868
  88.5 1.8 copy-start.1
  95.6 5.8 %copy-start.5 = (s32[56]{0:T(128)}, s32[56]{0:T(128)S(1)}, u32[]{:S(2)}) copy-start(s32[56]{0:T(128)S(1)} %get-tuple-element.24.posn) | copy-start | bytes 676

commit v4 on v3

v4 whole, which is shorter than its diff:
```python
import functools
import jax
import jax.numpy as jnp
from jax import lax
from jax.experimental import pallas as pl
from jax.experimental.pallas import tpu as pltpu
from jax.sharding import PartitionSpec as P

LOWEST = -1e30
CROSS = 0.3125
SQUARE = 0.15625
MESH = pl.DeviceIdType.MESH
MIB = 2**20
f32 = jnp.float32
bf16 = jnp.bfloat16


def params(cid=None, vmem=48):
    if cid is None:
        return pltpu.CompilerParams(vmem_limit_bytes=vmem * MIB)
    return pltpu.CompilerParams(
        collective_id=cid, has_side_effects=True, vmem_limit_bytes=vmem * MIB
    )


def nt(a, b):
    return lax.dot_general(a, b, (((1,), (1,)), ((), ())), preferred_element_type=f32)


def tn(a, b):
    return lax.dot_general(a, b, (((0,), (0,)), ((), ())), preferred_element_type=f32)


def nn(a, b):
    return jnp.dot(a, b, preferred_element_type=f32)


def greet_signal(axes):
    bar = pltpu.get_barrier_semaphore()
    for name in axes:
        n = lax.axis_size(name)
        me = lax.axis_index(name)

        @pl.loop(1, n)
        def _(s):
            pl.semaphore_signal(
                bar, inc=1, device_id={name: lax.rem(me + s, n)}, device_id_type=MESH
            )


def greet_wait(axes):
    total = sum(lax.axis_size(name) - 1 for name in axes)
    pl.semaphore_wait(pltpu.get_barrier_semaphore(), total)


def remote(src, dst, send, recv, axis, to):
    return pltpu.make_async_remote_copy(
        src_ref=src,
        dst_ref=dst,
        send_sem=send,
        recv_sem=recv,
        device_id={axis: to},
        device_id_type=MESH,
    )


def send_all(src, dst, send, recv, axis):
    n = lax.axis_size(axis)
    me = lax.axis_index(axis)

    @pl.loop(1, n)
    def _(s):
        to = lax.rem(me + s, n)
        remote(src(to), dst, send, recv, axis, to).start()


def messages(ref, count, send, recv, axis):
    part = ref.at[pl.ds(0, count)]
    n = lax.axis_size(axis)
    return remote(part, part, send, recv, axis, lax.rem(lax.axis_index(axis) + 1, n))


def wait_all(ref, send, recv, axis):
    every = messages(ref, lax.axis_size(axis) - 1, send, recv, axis)
    every.wait_send()
    every.wait_recv()


def away(m):
    return 8 * lax.rem(m, 8) + m // 8


def message(s):
    return 8 * lax.rem(s, 8) + s // 8


def squares_row(t):
    wide = t.astype(f32)
    square = wide * wide
    high = square.astype(bf16)
    low = (square - high.astype(f32)).astype(bf16)
    ones = jnp.ones((8, t.shape[1]), bf16)
    return SQUARE * (nt(ones, high) + nt(ones, low))[0:1]


def whole_kernel(
    inv, posn, msg_ref, x_hbm, ownp_hbm, logw_ref, logwt_ref, srcf_hbm, tfeats_hbm,
    moved_ref, out_ref,
    x_ref, own_ref, srcf_ref, ownf_ref, stripe_p, stripe_f, logw_col, alpha_ref,
    ids_all, ids_wide, ids_lane, asked, table_p, table_f, halves_p, halves_f, out_p, in_p,
    far_ref, packed_ref, got_ref, scores, beta_ref, lse_ref,
    padded, out1, in1, own, upper, outx, inx, both, out2, in2,
    farf, wide, diag, out_h, in_h, pieces, total, out_x, in_x, out_f, in_f,
    local, send_i, recv_i, send_p, recv_p, send_t, recv_t, send_f, recv_f,
    send1, recv1, send3, recv3, send_s, recv_s,
    sendx_p, recvx_p, sendx_f, recvx_f, send2, recv2,
    send_m, recv_m, send_x, recv_x, send_o, recv_o,
):
    n = lax.axis_size("blk")
    me = lax.axis_index("blk")
    plane = lax.axis_index("grp")
    pairs, block = beta_ref.shape
    rows = pairs // 8
    held = own.shape[0]
    planes = table_p.shape[0]
    mine = pl.ds(pl.multiple_of(plane * 2048, 2048), 2048)
    copies = [
        pltpu.make_async_copy(src, dst, local.at[i])
        for i, (src, dst) in enumerate(
            [
                (ownp_hbm, own_ref),
                (tfeats_hbm.at[mine], ownf_ref),
                (x_hbm, x_ref),
                (srcf_hbm, srcf_ref),
            ]
        )
    ]
    for copy in copies:
        copy.start()
    greet_signal(["blk", "grp"])

    copies[0].wait()
    for s in range(8):
        for h in range(2):
            at = 256 * s + 128 * h
            pair = [own_ref[at + 64 * c : at + 64 * c + 64, :].astype(f32) for c in range(2)]
            wide[0, pl.ds(h * 8 + s, n, stride=16), :] = jnp.concatenate(pair, axis=1)
    stripe_p[...] = wide[0].reshape(n, 16, 128).astype(bf16)
    copies[1].wait()
    for c in range(2):
        for s in range(8):
            for h in range(2):
                at = 256 * s + 128 * h + 64 * c
                wide[1 + c, pl.ds(h * 8 + s, n, stride=16), :] = ownf_ref[at : at + 64, :].astype(f32)
        stripe_f[:, :, 128 * c : 128 * c + 128] = wide[1 + c].reshape(n, 16, 128).astype(bf16)
    greet_wait(["blk", "grp"])

    @pl.loop(1, n)
    def _(s):
        to = lax.rem(me + s, n)
        remote(stripe_p.at[to], table_p.at[plane, me], send_p, recv_p, "blk", to).start()
        remote(msg_ref.at[to], ids_all.at[message(s)], send_i, recv_i, "blk", to).start()

    @pl.loop(1, n)
    def _(s):
        to = lax.rem(me + s, n)
        remote(stripe_f.at[to], table_f.at[plane, me], send_s, recv_s, "blk", to).start()

    ids_all[0] = msg_ref[me]
    table_p[plane, me] = stripe_p[me]
    table_f[plane, me] = stripe_f[me]
    turned = jnp.transpose(logw_ref[...])
    for r in range(rows):
        logw_col[block * r : block * (r + 1), :] = turned[:, r : r + 1]
    padded[pl.ds(pairs, 8), :] = jnp.full((8, block), LOWEST, f32)
    copies[2].wait()
    copies[3].wait()
    wait_all(stripe_p, send_p, recv_p, "blk")
    send_all(lambda to: table_p.at[plane], table_p.at[plane], sendx_p, recvx_p, "grp")
    wait_all(ids_all, send_i, recv_i, "blk")
    scalars = pltpu.make_async_copy(ids_all, asked, local.at[0])
    scalars.start()
    ids = ids_all[...].reshape(n, 128).astype(f32)
    turned = jnp.transpose(ids)
    for m in range(n):
        ids_wide[m] = jnp.broadcast_to(turned[0:56, m : m + 1], (56, 128))
    spot = lax.broadcasted_iota(jnp.int32, (16, 128), 1) // 8
    row = lax.broadcasted_iota(jnp.int32, (16, 128), 0)
    for group in range(4):
        some = ids[16 * group : 16 * group + 16]
        for k in range(7):
            moved = pltpu.roll(some, (128 - 8 * k) % 128, 1)
            moved = pltpu.roll(moved, 0, 1, stride=8, stride_axis=0)
            ids_lane[group, :, 128 * k : 128 * k + 128] = jnp.sum(
                jnp.where(spot == row, moved, 0.0), axis=0, keepdims=True
            ).astype(jnp.int32)
    scalars.wait()
    wait_all(stripe_f, send_s, recv_s, "blk")
    send_all(lambda to: table_f.at[plane], table_f.at[plane], sendx_f, recvx_f, "grp")

    def halve(table, halves):
        width = halves.shape[2]

        @pl.loop(0, planes)
        def _(p):
            for start in range(0, n, 16):
                piece = table[p, pl.ds(start, 16)].astype(f32)
                for h in range(2):
                    at = pl.ds(p * (8 * n) + start * 8, 128)
                    halves[h, at, :] = piece[:, 8 * h : 8 * h + 8].reshape(128, width).astype(bf16)

    def pack(halves, out, then):
        width = halves.shape[2]

        @pl.loop(0, n // 4)
        def _(g):
            ids = ids_wide[pl.ds(4 * g, 4)].reshape(224, 128)[:, 0:1]
            index = lax.broadcasted_iota(jnp.int32, (224, halves.shape[1]), 1)
            hot = (index == ids.astype(jnp.int32)).astype(f32).astype(bf16)
            low = nn(hot, halves[0])
            high = nn(hot, halves[1])
            for d in range(4):
                for k in range(7):
                    at = (d * 7 + k) * 8
                    two = jnp.concatenate([low[at : at + 8], high[at : at + 8]], axis=0)
                    out[4 * g + d, :, k * width : (k + 1) * width] = two.astype(bf16)
                then(4 * g + d)

    def send_points(m):
        @pl.when(m > 0)
        def _():
            to = lax.rem(me + n - away(m), n)
            remote(out_p.at[m], in_p.at[me], send_t, recv_t, "blk", to).start()

    wait_all(table_p, sendx_p, recvx_p, "grp")
    halve(table_p, halves_p)
    pack(halves_p, out_p, send_points)
    in_p[me] = out_p[0]
    wait_all(table_f, sendx_f, recvx_f, "grp")
    halve(table_f, halves_f)
    pack(halves_f, packed_ref, lambda m: None)
    got_ref[me] = packed_ref[0]
    wait_all(in_p, send_t, recv_t, "blk")
    for k in range(7):
        wide[k] = in_p[:, :, 128 * k : 128 * (k + 1)].astype(f32).reshape(n * 16, 128)
        for r in range(8):
            for h in range(2):
                got = wide[k, pl.ds(h * 8 + r, n, stride=16), :].astype(bf16)
                far_ref[r, k, 2 * h * 64 : (2 * h + 1) * 64, :] = got[:, 0:64]
                far_ref[r, k, (2 * h + 1) * 64 : (2 * h + 2) * 64, :] = got[:, 64:128]

    def bulk(chunk):
        @pl.loop(0, n // 8)
        def _(j):
            m = 8 * chunk + j

            @pl.when(m > 0)
            def _():
                to = lax.rem(me + n - away(m), n)
                remote(packed_ref.at[m], got_ref.at[me], send_f, recv_f, "blk", to).start()

    def compute(first, chunks):
        @pl.loop(0, rows)
        def _(r):
            for i, chunk in enumerate(chunks):

                @pl.when(r == i * (rows // len(chunks)))
                def _():
                    bulk(chunk)

            at = pl.ds(pl.multiple_of(r * block, block), block)
            x = x_ref[at, :]
            top = None
            for k in range(8):
                t = own_ref[at, :] if k == 0 else far_ref[r, k - 1]
                bias = -squares_row(t) if first else beta_ref[pl.ds(8 * r + k, 1), :]
                z = nt(x, t) * CROSS + bias
                scores[k] = z
                top = z if top is None else jnp.maximum(top, z)
            peak = jnp.max(top, axis=1, keepdims=True)
            weight = None
            for k in range(8):
                e = jnp.exp(scores[k] - peak)
                weight = e if weight is None else weight + e
            alpha = logw_col[at, :] - peak - jnp.log(jnp.sum(weight, axis=1, keepdims=True))
            alpha_ref[at, :] = alpha
            for k in range(8):
                t = own_ref[at, :] if k == 0 else far_ref[r, k - 1]
                v = nt(x, t) * CROSS + alpha
                top = jnp.max(v, axis=0, keepdims=True)
                padded[pl.ds(8 * r + k, 1), :] = top + jnp.log(
                    jnp.sum(jnp.exp(v - top), axis=0, keepdims=True)
                )

    def potentials(turn, chunks):
        @pl.loop(0, n)
        def _(s):
            to = lax.rem(me + s, n)
            out1[to, 0:1, :] = padded[pl.ds(inv[2 * to], 1), :]
            out1[to, 1:2, :] = padded[pl.ds(inv[2 * to + 1], 1), :]

            @pl.when(s > 0)
            def _():
                remote(out1.at[to], in1.at[message(s)], send1, recv1, "blk", to).start()

        for chunk in chunks[0]:
            bulk(chunk)
        in1[0] = out1[me]
        own[...] = jnp.full(own.shape, LOWEST, f32)
        for r in range(rows):
            own[pl.ds(plane * rows + r, 1), :] = padded[pl.ds(8 * r, 1), :]
        wait_all(in1, send1, recv1, "blk")
        index = lax.broadcasted_iota(jnp.int32, own.shape, 0)

        def highest(m, best):
            for c in range(2):
                value = in1[m, c : c + 1, :]
                best = jnp.maximum(best, jnp.where(index == asked[m, 0, 56 + c], value, LOWEST))
            return best

        upper[pl.ds(0, held), :] = lax.fori_loop(0, n, highest, own[...])
        upper[pl.ds(held, 8), :] = jnp.zeros((8, block), f32)

        def add(m, so_far):
            for c in range(2):
                slot = asked[m, 0, 56 + c]
                value = jnp.exp(in1[m, c : c + 1, :] - upper[pl.ds(slot, 1), :])
                so_far = so_far + jnp.where(index == slot, value, 0.0)
            return so_far

        top = upper[pl.ds(0, held), :]
        first = jnp.where(own[...] > 0.5 * LOWEST, jnp.exp(own[...] - top), 0.0)
        summed = lax.fori_loop(0, n, add, first)
        part = jnp.where(summed > 0.0, top + jnp.log(jnp.where(summed > 0.0, summed, 1.0)), LOWEST)
        outx[...] = part
        here = inx.at[turn]
        here[plane] = part
        send_all(lambda to: outx, here.at[plane], send2.at[turn], recv2.at[turn], "grp")
        wait_all(here, send2.at[turn], recv2.at[turn], "grp")
        top = inx[turn, 0]
        for p in range(1, planes):
            top = jnp.maximum(top, inx[turn, p])
        summed = jnp.exp(inx[turn, 0] - top)
        for p in range(1, planes):
            summed = summed + jnp.exp(inx[turn, p] - top)
        lse = top + jnp.log(summed)
        both[0, pl.ds(0, held), :] = logwt_ref[...] - lse
        both[1, pl.ds(0, held), :] = lse
        both[:, pl.ds(held, 8), :] = jnp.zeros((2, 8, block), f32)

        @pl.loop(0, n)
        def _(m):
            for c in range(2):
                slot = asked[m, 0, 56 + c]
                out2[m, 2 * c : 2 * c + 1, :] = both[0, pl.ds(slot, 1), :]
                out2[m, 2 * c + 1 : 2 * c + 2, :] = both[1, pl.ds(slot, 1), :]

            @pl.when(m > 0)
            def _():
                to = lax.rem(me + n - away(m), n)
                remote(out2.at[m], in2.at[me], send3, recv3, "blk", to).start()

        for chunk in chunks[1]:
            bulk(chunk)
        in2[me] = out2[0]
        wait_all(in2, send3, recv3, "blk")
        for r in range(rows):
            beta_ref[8 * r : 8 * r + 1, :] = both[0, pl.ds(plane * rows + r, 1), :]
            lse_ref[8 * r : 8 * r + 1, :] = both[1, pl.ds(plane * rows + r, 1), :]
            for k in range(7):
                where = posn[8 * k + r]
                owner = where // 2
                rank = where % 2
                row = 8 * r + k + 1
                beta_ref[row : row + 1, :] = in2[owner, pl.ds(2 * rank, 1), :]
                lse_ref[row : row + 1, :] = in2[owner, pl.ds(2 * rank + 1, 1), :]

    compute(True, [0, 1])
    potentials(0, [[2], [3]])
    compute(False, [4, 5])
    potentials(1, [[6], [7]])

    def parts(h):
        @pl.loop(0, rows)
        def _(r):
            at = pl.ds(pl.multiple_of(r * block, block), block)
            x = x_ref[at, :]
            alpha = alpha_ref[at, :]
            srcf = srcf_ref[at, :]
            half = pl.ds(pl.multiple_of(r * 256 + 128 * h, 128), 128)
            for k in range(8):
                t = own_ref[half, :] if k == 0 else far_ref[r, k - 1, 128 * h : 128 * h + 128, :]
                shift = lse_ref[pl.ds(8 * r + k, 1), :][:, 128 * h : 128 * h + 128]
                w = jnp.exp(nt(x, t) * CROSS + alpha - shift).astype(bf16)
                part = tn(w, srcf).astype(bf16).astype(f32)
                if k == 0:
                    diag[half, :] = part
                else:
                    for c in range(2):
                        wide[k - 1, pl.ds(c * 8 + r, n, stride=16), :] = part[64 * c : 64 * c + 64]

        for k in range(7):
            out_h[h, :, :, 128 * k : 128 * (k + 1)] = wide[k].reshape(n, 16, 128).astype(bf16)
        for chunk in range(8):

            @pl.loop(0, n // 8)
            def _(j):
                s = 8 * j + chunk

                @pl.when(s > 0)
                def _():
                    to = lax.rem(me + s, n)
                    remote(
                        out_h.at[h, to],
                        in_h.at[h, 8 * chunk + j],
                        send_m.at[h],
                        recv_m.at[h, chunk // 2],
                        "blk",
                        to,
                    ).start()

        in_h[h, 0] = out_h[h, me]

    def move_rows():
        wait_all(got_ref, send_f, recv_f, "blk")
        for k in range(7):
            for c in range(2):
                lanes = 128 * (2 * k + c)
                buffer = (2 * k + c) % 7
                wide[buffer] = got_ref[:, :, lanes : lanes + 128].astype(f32).reshape(16 * n, 128)
                for r in range(8):
                    for h in range(2):
                        got = wide[buffer, pl.ds(h * 8 + r, n, stride=16), :]
                        farf[r, k, 64 * (2 * h + c) : 64 * (2 * h + c + 1), :] = got.astype(bf16)

        @pl.loop(0, rows)
        def _(r):
            at = pl.ds(pl.multiple_of(r * block, block), block)
            x = x_ref[at, :]
            top = None
            for k in range(8):
                t = own_ref[at, :] if k == 0 else far_ref[r, k - 1]
                z = nt(x, t) * CROSS + beta_ref[pl.ds(8 * r + k, 1), :]
                scores[k] = z
                top = z if top is None else jnp.maximum(top, z)
            peak = jnp.max(top, axis=1, keepdims=True)
            weight = None
            mixed = None
            for k in range(8):
                e = jnp.exp(scores[k] - peak)
                weight = e if weight is None else weight + e
                feats = ownf_ref[at, :] if k == 0 else farf[r, k - 1]
                term = nn(e.astype(bf16), feats)
                mixed = term if mixed is None else mixed + term
            moved_ref[at, :] = (mixed / jnp.sum(weight, axis=1, keepdims=True)).astype(bf16)

    def collect(h, group):
        count = 16 - (1 if group == 0 else 0)
        messages(in_h.at[h], count, send_m.at[h], recv_m.at[h, group], "blk").wait_recv()

        @pl.loop(0, 8)
        def _(pair):
            one = in_h[h, 16 * group + 2 * pair].astype(f32)
            two = in_h[h, 16 * group + 2 * pair + 1].astype(f32)
            for k in range(7):
                for c in range(2):
                    lanes = slice(128 * k, 128 * (k + 1))
                    joined = jnp.concatenate(
                        [one[8 * c : 8 * c + 8, lanes], two[8 * c : 8 * c + 8, lanes]], axis=0
                    )
                    at = pl.ds(pl.multiple_of(128 * k + 16 * pair, 16), 16)
                    pieces[at, 128 * c : 128 * (c + 1)] = joined.astype(bf16)

        @pl.loop(0, 8)
        def _(i):
            at = pl.ds(pl.multiple_of(256 * i, 256), 256)
            index = lax.broadcasted_iota(jnp.int32, (256, 896), 0) + 256 * i
            hot = (index == ids_lane[group]).astype(f32).astype(bf16)
            term = nn(hot, pieces[...])
            if group == 0:
                total[at, :] = term
            else:
                total[at, :] += term

    def spread(h):
        for p in range(planes):
            out_x[h, p] = total[512 * p : 512 * (p + 1), :].astype(bf16)
        in_x[h, plane] = out_x[h, plane]
        send_all(
            lambda to: out_x.at[h, to], in_x.at[h, plane], send_x.at[h], recv_x.at[h], "grp"
        )

    def finish(h):
        wait_all(in_x.at[h], send_x.at[h], recv_x.at[h], "grp")
        added = in_x[h, 0].astype(f32)
        for p in range(1, planes):
            added = added + in_x[h, p].astype(f32)
        joined = jnp.concatenate(
            [added[:, 128 * c : 128 * (c + 1)].reshape(n, 8, 128) for c in range(2)], axis=1
        )
        out_f[h] = joined.astype(bf16)
        send_all(lambda to: out_f.at[h, to], in_f.at[h, me], send_o.at[h], recv_o.at[h], "blk")
        in_f[h, me] = out_f[h, me]

    def deliver(h):
        wait_all(in_f.at[h], send_o.at[h], recv_o.at[h], "blk")
        wide[h] = in_f[h].astype(f32).reshape(16 * n, 128)
        for s in range(8):
            for c in range(2):
                at = 256 * s + 64 * (2 * h + c)
                got = wide[h, pl.ds(c * 8 + s, n, stride=16), :]
                out_ref[at : at + 64, :] = (got + diag[at : at + 64, :]).astype(bf16)

    parts(0)
    parts(1)
    move_rows()
    for group in range(4):
        collect(0, group)
    spread(0)
    collect(1, 0)
    collect(1, 1)
    finish(0)
    collect(1, 2)
    collect(1, 3)
    spread(1)
    finish(1)
    deliver(0)
    deliver(1)
    for h in range(2):
        messages(out_h.at[h], n - 1, send_m.at[h], recv_m.at[h, 0], "blk").wait_send()


def whole(inv, posn, msg, x, ownp, logw, logwt, srcf, tfeats, cid):
    n = lax.axis_size("blk")
    planes = lax.axis_size("grp")
    pairs, block = 64, 256
    held = logwt.shape[0]
    smem = pl.BlockSpec(memory_space=pltpu.SMEM)
    vmem = pl.BlockSpec(memory_space=pltpu.VMEM)
    hbm = pl.BlockSpec(memory_space=pl.ANY)
    scratch = [
        ((2048, 64), bf16),
        ((2048, 64), bf16),
        ((2048, 128), bf16),
        ((2048, 128), bf16),
        ((n, 16, 128), bf16),
        ((n, 16, 256), bf16),
        ((2048, 1), f32),
        ((2048, 1), f32),
        ((n, 1, 128), jnp.int32),
        ((n, 56, 128), f32),
        ((4, 1, 896), jnp.int32),
        None,
        ((planes, n, 16, 128), bf16),
        ((planes, n, 16, 256), bf16),
        ((2, planes * 8 * n, 128), bf16),
        ((2, planes * 8 * n, 256), bf16),
        ((n, 16, 7 * 128), bf16),
        ((n, 16, 7 * 128), bf16),
        ((8, 7, 256, 64), bf16),
        ((n, 16, 7 * 256), bf16),
        ((n, 16, 7 * 256), bf16),
        ((8, block, block), f32),
        ((pairs, block), f32),
        ((pairs, block), f32),
        ((pairs + 8, block), f32),
        ((n, 2, block), f32),
        ((n, 2, block), f32),
        ((held, block), f32),
        ((held + 8, block), f32),
        ((held, block), f32),
        ((2, planes, held, block), f32),
        ((2, held + 8, block), f32),
        ((n, 4, block), f32),
        ((n, 4, block), f32),
        ((8, 7, 256, 128), bf16),
        ((7, 16 * n, 128), f32),
        ((2048, 128), f32),
        ((2, n, 16, 896), bf16),
        ((2, n, 16, 896), bf16),
        ((896, 256), bf16),
        ((planes * 8 * n, 256), f32),
        ((2, planes, 8 * n, 256), bf16),
        ((2, planes, 8 * n, 256), bf16),
        ((2, n, 16, 128), bf16),
        ((2, n, 16, 128), bf16),
    ]
    dma = pltpu.SemaphoreType.DMA
    return pl.pallas_call(
        whole_kernel,
        out_shape=(
            jax.ShapeDtypeStruct((2048, 128), bf16),
            jax.ShapeDtypeStruct((2048, 128), bf16),
        ),
        in_specs=[smem, smem, vmem, hbm, hbm, vmem, vmem, hbm, hbm],
        out_specs=(vmem,) * 2,
        scratch_shapes=[
            pltpu.SMEM((n, 1, 128), jnp.int32) if item is None else pltpu.VMEM(*item)
            for item in scratch
        ]
        + [dma((4,))]
        + [dma] * 14
        + [dma] * 4
        + [dma((2,))] * 2
        + [dma((2,)), dma((2, 4))]
        + [dma((2,))] * 4,
        compiler_params=params(cid, 62),
    )(inv, posn, msg, x, ownp, logw, logwt, srcf, tfeats)


def shards(
    source_points, target_points, source_logw, target_logw,
    source_feats, target_feats, pair_owner, pair_slot,
):
    n = lax.axis_size("blk")
    plane = lax.axis_index("grp")
    own_points = lax.dynamic_slice_in_dim(target_points, plane * 2048, 2048, 0)
    owners = pair_owner.T.reshape(56)
    slots = pair_slot.T.reshape(56)
    ids = (slots // 8) * (8 * n) + owners * 8 + slots % 8
    earlier = jnp.tril(jnp.ones((56, 56), bool), -1) & (owners[:, None] == owners[None, :])
    posn = owners * 2 + jnp.sum(earlier.astype(jnp.int32), axis=1)
    order = jnp.arange(56, dtype=jnp.int32)
    row_of = (order % 8) * 8 + order // 8 + 1
    at = posn[None, :] == jnp.arange(2 * n, dtype=jnp.int32)[:, None]
    inv = jnp.min(jnp.where(at, row_of[None, :], 64), axis=1)
    asked = jnp.min(jnp.where(at, slots[None, :], 32), axis=1).reshape(n, 2)
    msg = jnp.concatenate(
        [jnp.broadcast_to(ids[None], (n, 56)), asked, jnp.zeros((n, 70), jnp.int32)], axis=1
    ).reshape(n, 1, 128)
    return whole(
        inv, posn, msg, source_points, own_points, source_logw.reshape(8, 256),
        target_logw.reshape(32, 256), source_feats, target_feats, 0,
    )


def solution(mesh):
    return jax.shard_map(
        shards,
        mesh=mesh,
        in_specs=(
            P(("blk", "grp"), None),
            P("blk", None),
            P(("blk", "grp")),
            P("blk"),
            P(("blk", "grp"), None),
            P("blk", None),
            P(("blk", "grp"), None),
            P(("blk", "grp"), None),
        ),
        out_specs=(P(("blk", "grp"), None), P(("blk", "grp"), None)),
        check_vma=False,
    )
```

time: 346 us -> 315 us (0.910)
  Pallas kernels: 325 us -> 300 us
  local copies, waits for them, and re-layouts: 16.7 us -> 11.4 us
    pallas_call x3 -> x1, Pallas kernels: 325 us -> 300 us  [whole(): pl.pallas_call(whole_kernel, out_shape=(jax.ShapeDtypeStruct((2048, 128),...]
    unnamed x16 -> x8, local copies, waits for them, and re-layouts: 7.78 us -> 6.71 us
where the time goes in v4:
time: 315 us; the launch traced here: 313 us
  Pallas kernels  300 us (95%)
  local copies, waits for them, and re-layouts  11.4 us (4%)
    pallas_call x1, Pallas kernels, whole(): pl.pallas_call(whole_kernel, out_shape=(jax.ShapeDtypeStruct((2048, 128),...  300 us
    unnamed x8, local copies, waits for them, and re-layouts  6.71 us

profile of v4, /device:TPU:1, one launch (start us, length us, event | category | flops | bytes accessed | tf_op | source)
XLA Modules:
  0.0 313.4 jit_solution(12277855923903221502)
XLA Ops:
  0.6 0.0 copy-start
  0.7 0.1 pad.2.clone
  0.7 0.8 copy.18
  1.6 0.1 reshape.112
  1.7 0.2 convert_reduce_fusion
  1.8 0.8 copy.19
  2.6 0.1 reshape.113
  2.7 0.0 copy-start.1
  2.7 0.7 select_reduce_fusion
  3.4 1.3 reshape.116.logw_ref
  4.7 0.1 reshape.114
  4.9 0.7 add_add_fusion
  5.5 1.4 reshape.117.logwt_ref
  6.9 0.0 copy-done
  6.9 1.0 copy.22.ownp_hbm
  8.0 2.0 copy.21.x_hbm
  9.9 0.0 copy-done.1
  9.9 299.8 %shard_map.95 = (bf16[2048,128]{1,0:T(8,128)(2,1)}, bf16[2048,128]{1,0:T(8,128)(2,1)}) custom-call(s32[128]{0:T(128)} %get-tuple-element.3.inv, s32[56]{0:T(128)} %copy-done.1, s32[64,1,128]{2,1,0:T(1,128)} %bitcast.3, bf16[2048,64]{1,0:T(8,128)(2,1)} %copy.21.x_hbm, bf16[2048,64]{1,0:T(8,128)(2,1)} %copy.22.ownp_hbm, f32[8,256]{1,0:T(8,128)} %reshape.116.logw_ref, ...), custom_call_target="tpu_custom_call" | custom-call | tf_op jit(solution)/shard_map/pallas_call | solution.py:589
  309.7 1.9 copy.25
  311.5 1.9 copy.26
  (5 shorter events, 0.0 us)
Async XLA Ops:
  0.6 6.3 %copy-start = (bf16[8192,64]{0,1:T(8,128)(2,1)S(1)}, bf16[8192,64]{0,1:T(8,128)(2,1)}, u32[]{:S(2)}) copy-start(bf16[8192,64]{0,1:T(8,128)(2,1)} %param.9) | copy-start | bytes 3145732
  2.7 7.2 %copy-start.1 = (s32[56]{0:T(128)}, s32[56]{0:T(128)S(1)}, u32[]{:S(2)}) copy-start(s32[56]{0:T(128)S(1)} %get-tuple-element.5.posn) | copy-start | bytes 676

commit v5 on v4

--- a/solution.py
+++ b/solution.py
@@ -11,6 +11,7 @@
 SQUARE = 0.15625
 MESH = pl.DeviceIdType.MESH
 MIB = 2**20
+SCHEDULE = ((3, 10, 6), (3, 10, 6))
 f32 = jnp.float32
 bf16 = jnp.bfloat16
 
@@ -87,11 +88,33 @@
 
 
 def away(m):
-    return 8 * lax.rem(m, 8) + m // 8
+    place = lax.rem(m, 8)
+    return 8 * (2 * lax.rem(place, 4) + place // 4) + m // 8
+
+
+def holder(m, me):
+    z, yc = me // 8, lax.rem(me, 8)
+    return 8 * lax.rem(z + 8 + along(m, yc), 8) + lax.rem(yc + m // 4, 8)
+
+
+def sender(m, me):
+    z, yc = me // 8, lax.rem(lax.rem(me, 8) + 8 - m // 4, 8)
+    return 8 * lax.rem(z + 8 - along(m, yc), 8) + yc
+
+
+def along(m, yc):
+    turn = lax.rem(m, 4)
+    two = (turn // 2) * (1 - turn // 3)
+    return turn - 4 * (turn // 3) - 4 * two * lax.rem(yc, 2)
+
+
+def stripe(device):
+    return 8 * lax.rem(device // 8, 4) + lax.rem(device, 8)
 
 
 def message(s):
-    return 8 * lax.rem(s, 8) + s // 8
+    z = s // 8
+    return 8 * lax.rem(s, 8) + z // 2 + 4 * lax.rem(z, 2)
 
 
 def squares_row(t):
@@ -106,8 +129,8 @@
 def whole_kernel(
     inv, posn, msg_ref, x_hbm, ownp_hbm, logw_ref, logwt_ref, srcf_hbm, tfeats_hbm,
     moved_ref, out_ref,
-    x_ref, own_ref, srcf_ref, ownf_ref, stripe_p, stripe_f, logw_col, alpha_ref,
-    ids_all, ids_wide, ids_lane, asked, table_p, table_f, halves_p, halves_f, out_p, in_p,
+    turned_x, turned_own, logwt, x_ref, own_ref, srcf_ref, ownf_ref, stripe_p, stripe_f, logw_col, alpha_ref,
+    ids_all, ids_sel, ids_wide, ids_lane, asked, table_p, table_f, halves_p, halves_f, out_p, in_p,
     far_ref, packed_ref, got_ref, scores, beta_ref, lse_ref,
     padded, out1, in1, own, upper, outx, inx, both, out2, in2,
     farf, wide, diag, out_h, in_h, pieces, total, out_x, in_x, out_f, in_f,
@@ -128,9 +151,9 @@
         pltpu.make_async_copy(src, dst, local.at[i])
         for i, (src, dst) in enumerate(
             [
-                (ownp_hbm, own_ref),
+                (ownp_hbm.at[:, mine], turned_own),
                 (tfeats_hbm.at[mine], ownf_ref),
-                (x_hbm, x_ref),
+                (x_hbm, turned_x),
                 (srcf_hbm, srcf_ref),
             ]
         )
@@ -140,6 +163,8 @@
     greet_signal(["blk", "grp"])
 
     copies[0].wait()
+    for i in range(0, 2048, 256):
+        own_ref[i : i + 256, :] = jnp.transpose(turned_own[:, i : i + 256].astype(f32)).astype(bf16)
     for s in range(8):
         for h in range(2):
             at = 256 * s + 128 * h
@@ -170,10 +195,14 @@
     table_p[plane, me] = stripe_p[me]
     table_f[plane, me] = stripe_f[me]
     turned = jnp.transpose(logw_ref[...])
-    for r in range(rows):
-        logw_col[block * r : block * (r + 1), :] = turned[:, r : r + 1]
+    for i in range(16):
+        logw_col[128 * i : 128 * (i + 1), :] = turned[:, i : i + 1]
+    for i in range(2):
+        logwt[:, 128 * i : 128 * (i + 1)] = logwt_ref[pl.ds(i, held, stride=2), :]
     padded[pl.ds(pairs, 8), :] = jnp.full((8, block), LOWEST, f32)
     copies[2].wait()
+    for i in range(0, 2048, 256):
+        x_ref[i : i + 256, :] = jnp.transpose(turned_x[:, i : i + 256].astype(f32)).astype(bf16)
     copies[3].wait()
     wait_all(stripe_p, send_p, recv_p, "blk")
     send_all(lambda to: table_p.at[plane], table_p.at[plane], sendx_p, recvx_p, "grp")
@@ -186,8 +215,13 @@
         ids_wide[m] = jnp.broadcast_to(turned[0:56, m : m + 1], (56, 128))
     spot = lax.broadcasted_iota(jnp.int32, (16, 128), 1) // 8
     row = lax.broadcasted_iota(jnp.int32, (16, 128), 0)
-    for group in range(4):
-        some = ids[16 * group : 16 * group + 16]
+
+    @pl.loop(0, n // 2)
+    def _(m):
+        ids_sel[m] = ids_all[message(lax.rem(me + n - sender(m, me), n))]
+
+    for group in range(2):
+        some = ids_sel[16 * group : 16 * group + 16].reshape(16, 128).astype(f32)
         for k in range(7):
             moved = pltpu.roll(some, (128 - 8 * k) % 128, 1)
             moved = pltpu.roll(moved, 0, 1, stride=8, stride_axis=0)
@@ -249,24 +283,22 @@
                 far_ref[r, k, 2 * h * 64 : (2 * h + 1) * 64, :] = got[:, 0:64]
                 far_ref[r, k, (2 * h + 1) * 64 : (2 * h + 2) * 64, :] = got[:, 64:128]
 
-    def bulk(chunk):
-        @pl.loop(0, n // 8)
+    def bulk(first, count):
+        @pl.loop(0, count)
         def _(j):
-            m = 8 * chunk + j
+            m = first + j
 
             @pl.when(m > 0)
             def _():
                 to = lax.rem(me + n - away(m), n)
                 remote(packed_ref.at[m], got_ref.at[me], send_f, recv_f, "blk", to).start()
 
-    def compute(first, chunks):
+    def compute(first, start, count):
         @pl.loop(0, rows)
         def _(r):
-            for i, chunk in enumerate(chunks):
-
-                @pl.when(r == i * (rows // len(chunks)))
-                def _():
-                    bulk(chunk)
+            @pl.when(lax.rem(r, 2) == 0)
+            def _():
+                bulk(start + (r // 2) * count, count)
 
             at = pl.ds(pl.multiple_of(r * block, block), block)
             x = x_ref[at, :]
@@ -292,7 +324,7 @@
                     jnp.sum(jnp.exp(v - top), axis=0, keepdims=True)
                 )
 
-    def potentials(turn, chunks):
+    def potentials(turn, start, counts):
         @pl.loop(0, n)
         def _(s):
             to = lax.rem(me + s, n)
@@ -303,8 +335,7 @@
             def _():
                 remote(out1.at[to], in1.at[message(s)], send1, recv1, "blk", to).start()
 
-        for chunk in chunks[0]:
-            bulk(chunk)
+        bulk(start, counts[0])
         in1[0] = out1[me]
         own[...] = jnp.full(own.shape, LOWEST, f32)
         for r in range(rows):
@@ -344,7 +375,7 @@
         for p in range(1, planes):
             summed = summed + jnp.exp(inx[turn, p] - top)
         lse = top + jnp.log(summed)
-        both[0, pl.ds(0, held), :] = logwt_ref[...] - lse
+        both[0, pl.ds(0, held), :] = logwt[...] - lse
         both[1, pl.ds(0, held), :] = lse
         both[:, pl.ds(held, 8), :] = jnp.zeros((2, 8, block), f32)
 
@@ -360,8 +391,7 @@
                 to = lax.rem(me + n - away(m), n)
                 remote(out2.at[m], in2.at[me], send3, recv3, "blk", to).start()
 
-        for chunk in chunks[1]:
-            bulk(chunk)
+        bulk(start + counts[0], counts[1])
         in2[me] = out2[0]
         wait_all(in2, send3, recv3, "blk")
         for r in range(rows):
@@ -375,10 +405,16 @@
                 beta_ref[row : row + 1, :] = in2[owner, pl.ds(2 * rank, 1), :]
                 lse_ref[row : row + 1, :] = in2[owner, pl.ds(2 * rank + 1, 1), :]
 
-    compute(True, [0, 1])
-    potentials(0, [[2], [3]])
-    compute(False, [4, 5])
-    potentials(1, [[6], [7]])
+    sent = 0
+    for turn in range(2):
+        per_two, after_ask, after_answer = SCHEDULE[turn]
+        compute(turn == 0, sent, per_two)
+        sent += 4 * per_two
+        potentials(turn, sent, (after_ask, after_answer))
+        sent += after_ask + after_answer
+    bulk(sent, n - sent)
+
+    few = n // 2
 
     def parts(h):
         @pl.loop(0, rows)
@@ -396,30 +432,30 @@
                 if k == 0:
                     diag[half, :] = part
                 else:
-                    for c in range(2):
-                        wide[k - 1, pl.ds(c * 8 + r, n, stride=16), :] = part[64 * c : 64 * c + 64]
+                    for d in range(2):
+                        for c in range(2):
+                            at = 64 * d + 32 * c
+                            to = pl.ds(512 * d + 8 * c + r, few, stride=16)
+                            wide[k - 1, to, :] = part[at : at + 32]
 
         for k in range(7):
-            out_h[h, :, :, 128 * k : 128 * (k + 1)] = wide[k].reshape(n, 16, 128).astype(bf16)
-        for chunk in range(8):
-
-            @pl.loop(0, n // 8)
-            def _(j):
-                s = 8 * j + chunk
-
-                @pl.when(s > 0)
-                def _():
-                    to = lax.rem(me + s, n)
-                    remote(
-                        out_h.at[h, to],
-                        in_h.at[h, 8 * chunk + j],
-                        send_m.at[h],
-                        recv_m.at[h, chunk // 2],
-                        "blk",
-                        to,
-                    ).start()
-
-        in_h[h, 0] = out_h[h, me]
+            for d in range(2):
+                lanes = 128 * (7 * d + k)
+                value = wide[k, 512 * d : 512 * (d + 1), :].reshape(few, 16, 128)
+                out_h[h, :, :, lanes : lanes + 128] = value.astype(bf16)
+        @pl.loop(1, few)
+        def _(m):
+            to = holder(m, me)
+            remote(
+                out_h.at[h, stripe(to)],
+                in_h.at[h, m],
+                send_m.at[h],
+                recv_m.at[h, m // 16],
+                "blk",
+                to,
+            ).start()
+
+        in_h[h, 0] = out_h[h, stripe(me)]
 
     def move_rows():
         wait_all(got_ref, send_f, recv_f, "blk")
@@ -463,13 +499,14 @@
             one = in_h[h, 16 * group + 2 * pair].astype(f32)
             two = in_h[h, 16 * group + 2 * pair + 1].astype(f32)
             for k in range(7):
-                for c in range(2):
-                    lanes = slice(128 * k, 128 * (k + 1))
-                    joined = jnp.concatenate(
-                        [one[8 * c : 8 * c + 8, lanes], two[8 * c : 8 * c + 8, lanes]], axis=0
-                    )
-                    at = pl.ds(pl.multiple_of(128 * k + 16 * pair, 16), 16)
-                    pieces[at, 128 * c : 128 * (c + 1)] = joined.astype(bf16)
+                for d in range(2):
+                    for c in range(2):
+                        lanes = slice(128 * (7 * d + k), 128 * (7 * d + k + 1))
+                        joined = jnp.concatenate(
+                            [one[8 * c : 8 * c + 8, lanes], two[8 * c : 8 * c + 8, lanes]], axis=0
+                        )
+                        at = pl.ds(pl.multiple_of(128 * k + 16 * pair, 16), 16)
+                        pieces[at, 128 * (2 * d + c) : 128 * (2 * d + c + 1)] = joined.astype(bf16)
 
         @pl.loop(0, 8)
         def _(i):
@@ -484,61 +521,68 @@
 
     def spread(h):
         for p in range(planes):
-            out_x[h, p] = total[512 * p : 512 * (p + 1), :].astype(bf16)
-        in_x[h, plane] = out_x[h, plane]
-        send_all(
-            lambda to: out_x.at[h, to], in_x.at[h, plane], send_x.at[h], recv_x.at[h], "grp"
-        )
+            out_x[p] = total[512 * p : 512 * (p + 1), :].astype(bf16)
+        in_x[h, plane] = out_x[plane]
+        send_all(lambda to: out_x.at[to], in_x.at[h, plane], send_x.at[h], recv_x.at[h], "grp")
 
     def finish(h):
         wait_all(in_x.at[h], send_x.at[h], recv_x.at[h], "grp")
         added = in_x[h, 0].astype(f32)
         for p in range(1, planes):
             added = added + in_x[h, p].astype(f32)
-        joined = jnp.concatenate(
-            [added[:, 128 * c : 128 * (c + 1)].reshape(n, 8, 128) for c in range(2)], axis=1
-        )
-        out_f[h] = joined.astype(bf16)
+        for d in range(2):
+            joined = jnp.concatenate(
+                [
+                    added[:, 128 * (2 * d + c) : 128 * (2 * d + c + 1)].reshape(n, 8, 128)
+                    for c in range(2)
+                ],
+                axis=1,
+            )
+            out_f[h, :, :, 128 * d : 128 * (d + 1)] = joined.astype(bf16)
         send_all(lambda to: out_f.at[h, to], in_f.at[h, me], send_o.at[h], recv_o.at[h], "blk")
         in_f[h, me] = out_f[h, me]
 
     def deliver(h):
         wait_all(in_f.at[h], send_o.at[h], recv_o.at[h], "blk")
-        wide[h] = in_f[h].astype(f32).reshape(16 * n, 128)
-        for s in range(8):
-            for c in range(2):
-                at = 256 * s + 64 * (2 * h + c)
-                got = wide[h, pl.ds(c * 8 + s, n, stride=16), :]
-                out_ref[at : at + 64, :] = (got + diag[at : at + 64, :]).astype(bf16)
+        for d in range(2):
+            lanes = slice(128 * d, 128 * (d + 1))
+            added = in_f[h, 0:few, :, lanes].astype(f32) + in_f[h, few:n, :, lanes].astype(f32)
+            wide[h, 512 * d : 512 * (d + 1), :] = added.reshape(16 * few, 128)
+            for s in range(8):
+                for c in range(2):
+                    at = 256 * s + 128 * h + 64 * d + 32 * c
+                    got = wide[h, pl.ds(512 * d + 8 * c + s, few, stride=16), :]
+                    out_ref[at : at + 32, :] = (got + diag[at : at + 32, :]).astype(bf16)
 
     parts(0)
     parts(1)
     move_rows()
-    for group in range(4):
-        collect(0, group)
+    collect(0, 0)
+    collect(0, 1)
     spread(0)
     collect(1, 0)
     collect(1, 1)
     finish(0)
-    collect(1, 2)
-    collect(1, 3)
     spread(1)
     finish(1)
     deliver(0)
     deliver(1)
     for h in range(2):
-        messages(out_h.at[h], n - 1, send_m.at[h], recv_m.at[h, 0], "blk").wait_send()
+        messages(out_h.at[h], few - 1, send_m.at[h], recv_m.at[h, 0], "blk").wait_send()
 
 
 def whole(inv, posn, msg, x, ownp, logw, logwt, srcf, tfeats, cid):
     n = lax.axis_size("blk")
     planes = lax.axis_size("grp")
     pairs, block = 64, 256
-    held = logwt.shape[0]
+    held = 32
     smem = pl.BlockSpec(memory_space=pltpu.SMEM)
     vmem = pl.BlockSpec(memory_space=pltpu.VMEM)
     hbm = pl.BlockSpec(memory_space=pl.ANY)
     scratch = [
+        ((64, 2048), bf16),
+        ((64, 2048), bf16),
+        ((held, block), f32),
         ((2048, 64), bf16),
         ((2048, 64), bf16),
         ((2048, 128), bf16),
@@ -548,8 +592,9 @@
         ((2048, 1), f32),
         ((2048, 1), f32),
         ((n, 1, 128), jnp.int32),
+        ((n // 2, 1, 128), jnp.int32),
         ((n, 56, 128), f32),
-        ((4, 1, 896), jnp.int32),
+        ((2, 1, 896), jnp.int32),
         None,
         ((planes, n, 16, 128), bf16),
         ((planes, n, 16, 256), bf16),
@@ -576,14 +621,14 @@
         ((8, 7, 256, 128), bf16),
         ((7, 16 * n, 128), f32),
         ((2048, 128), f32),
-        ((2, n, 16, 896), bf16),
-        ((2, n, 16, 896), bf16),
-        ((896, 256), bf16),
-        ((planes * 8 * n, 256), f32),
-        ((2, planes, 8 * n, 256), bf16),
-        ((2, planes, 8 * n, 256), bf16),
-        ((2, n, 16, 128), bf16),
-        ((2, n, 16, 128), bf16),
+        ((2, n // 2, 16, 1792), bf16),
+        ((2, n // 2, 16, 1792), bf16),
+        ((896, 512), bf16),
+        ((planes * 8 * n, 512), f32),
+        ((planes, 8 * n, 512), bf16),
+        ((2, planes, 8 * n, 512), bf16),
+        ((2, n, 16, 256), bf16),
+        ((2, n, 16, 256), bf16),
     ]
     dma = pltpu.SemaphoreType.DMA
     return pl.pallas_call(
@@ -602,7 +647,7 @@
         + [dma] * 14
         + [dma] * 4
         + [dma((2,))] * 2
-        + [dma((2,)), dma((2, 4))]
+        + [dma((2,)), dma((2, 2))]
         + [dma((2,))] * 4,
         compiler_params=params(cid, 62),
     )(inv, posn, msg, x, ownp, logw, logwt, srcf, tfeats)
@@ -613,8 +658,6 @@
     source_feats, target_feats, pair_owner, pair_slot,
 ):
     n = lax.axis_size("blk")
-    plane = lax.axis_index("grp")
-    own_points = lax.dynamic_slice_in_dim(target_points, plane * 2048, 2048, 0)
     owners = pair_owner.T.reshape(56)
     slots = pair_slot.T.reshape(56)
     ids = (slots // 8) * (8 * n) + owners * 8 + slots % 8
@@ -629,8 +672,8 @@
         [jnp.broadcast_to(ids[None], (n, 56)), asked, jnp.zeros((n, 70), jnp.int32)], axis=1
     ).reshape(n, 1, 128)
     return whole(
-        inv, posn, msg, source_points, own_points, source_logw.reshape(8, 256),
-        target_logw.reshape(32, 256), source_feats, target_feats, 0,
+        inv, posn, msg, source_points.T, target_points.T, source_logw.reshape(16, 128),
+        target_logw.reshape(64, 128), source_feats, target_feats, 0,
     )
 
 

time: 315 us -> 298 us (0.946)
  Pallas kernels: 300 us -> 289 us
  local copies, waits for them, and re-layouts: 11.4 us -> 5.65 us
    pallas_call x1, Pallas kernels: 300 us -> 289 us  [whole(): pl.pallas_call(whole_kernel, out_shape=(jax.ShapeDtypeStruct((2048, 128),...]
    unnamed x8 -> x4, local copies, waits for them, and re-layouts: 6.71 us -> 3.74 us
where the time goes in v5:
time: 298 us; the launch traced here: 297 us
  Pallas kernels  289 us (97%)
  local copies, waits for them, and re-layouts  5.65 us (2%)
    pallas_call x1, Pallas kernels, whole(): pl.pallas_call(whole_kernel, out_shape=(jax.ShapeDtypeStruct((2048, 128),...  289 us

profile of v5, /device:TPU:1, one launch (start us, length us, event | category | flops | bytes accessed | tf_op | source)
XLA Modules:
  0.0 297.3 jit_solution(9957941548685069987)
XLA Ops:
  0.6 0.1 pad.2.clone
  0.7 0.8 copy.14
  1.5 0.1 reshape.112
  1.6 0.2 convert_reduce_fusion
  1.7 0.8 copy.15
  2.5 0.1 reshape.113
  2.6 0.0 copy-start
  2.6 0.6 select_reduce_fusion
  3.3 0.1 reshape.114
  3.4 0.7 add_add_fusion
  4.1 0.0 copy-done
  4.1 289.4 %shard_map.95 = (bf16[2048,128]{1,0:T(8,128)(2,1)}, bf16[2048,128]{1,0:T(8,128)(2,1)}) custom-call(s32[128]{0:T(128)} %get-tuple-element.3.inv, s32[56]{0:T(128)} %copy-done, s32[64,1,128]{2,1,0:T(1,128)} %bitcast.9, bf16[64,2048]{1,0:T(8,128)(2,1)} %bitcast.8, bf16[64,8192]{1,0:T(8,128)(2,1)} %bitcast.7, f32[16,128]{1,0:T(8,128)} %bitcast.11, ...), custom_call_target="tpu_custom_call" | custom-call | tf_op jit(solution)/shard_map/pallas_call | solution.py:634
  293.5 1.9 copy.18
  295.4 1.9 copy.19
  (4 shorter events, 0.0 us)
Async XLA Ops:
  2.6 1.5 copy-start

commit v6 on v5

--- a/solution.py
+++ b/solution.py
@@ -11,7 +11,7 @@
 SQUARE = 0.15625
 MESH = pl.DeviceIdType.MESH
 MIB = 2**20
-SCHEDULE = ((3, 10, 6), (3, 10, 6))
+SCHEDULE = ((3, 10, 8), (3, 10, 8))
 f32 = jnp.float32
 bf16 = jnp.bfloat16
 
@@ -412,7 +412,6 @@
         sent += 4 * per_two
         potentials(turn, sent, (after_ask, after_answer))
         sent += after_ask + after_answer
-    bulk(sent, n - sent)
 
     few = n // 2
 
@@ -440,22 +439,24 @@
 
         for k in range(7):
             for d in range(2):
-                lanes = 128 * (7 * d + k)
+                lanes = 128 * k
                 value = wide[k, 512 * d : 512 * (d + 1), :].reshape(few, 16, 128)
-                out_h[h, :, :, lanes : lanes + 128] = value.astype(bf16)
-        @pl.loop(1, few)
-        def _(m):
-            to = holder(m, me)
-            remote(
-                out_h.at[h, stripe(to)],
-                in_h.at[h, m],
-                send_m.at[h],
-                recv_m.at[h, m // 16],
-                "blk",
-                to,
-            ).start()
-
-        in_h[h, 0] = out_h[h, stripe(me)]
+                out_h[2 * h + d, :, :, lanes : lanes + 128] = value.astype(bf16)
+        for q in (2 * h, 2 * h + 1):
+
+            @pl.loop(1, few)
+            def _(m):
+                to = holder(m, me)
+                remote(
+                    out_h.at[q, stripe(to)],
+                    in_h.at[q, m],
+                    send_m.at[q],
+                    recv_m.at[q, m // 16],
+                    "blk",
+                    to,
+                ).start()
+
+            in_h[q, 0] = out_h[q, stripe(me)]
 
     def move_rows():
         wait_all(got_ref, send_f, recv_f, "blk")
@@ -490,85 +491,84 @@
                 mixed = term if mixed is None else mixed + term
             moved_ref[at, :] = (mixed / jnp.sum(weight, axis=1, keepdims=True)).astype(bf16)
 
-    def collect(h, group):
-        count = 16 - (1 if group == 0 else 0)
-        messages(in_h.at[h], count, send_m.at[h], recv_m.at[h, group], "blk").wait_recv()
-
-        @pl.loop(0, 8)
-        def _(pair):
-            one = in_h[h, 16 * group + 2 * pair].astype(f32)
-            two = in_h[h, 16 * group + 2 * pair + 1].astype(f32)
-            for k in range(7):
-                for d in range(2):
+    def collect(q):
+        for group in range(2):
+            count = 16 - (1 if group == 0 else 0)
+            messages(in_h.at[q], count, send_m.at[q], recv_m.at[q, group], "blk").wait_recv()
+
+            @pl.loop(0, 8)
+            def _(pair):
+                one = in_h[q, 16 * group + 2 * pair].astype(f32)
+                two = in_h[q, 16 * group + 2 * pair + 1].astype(f32)
+                for k in range(7):
                     for c in range(2):
-                        lanes = slice(128 * (7 * d + k), 128 * (7 * d + k + 1))
+                        lanes = slice(128 * k, 128 * (k + 1))
                         joined = jnp.concatenate(
                             [one[8 * c : 8 * c + 8, lanes], two[8 * c : 8 * c + 8, lanes]], axis=0
                         )
                         at = pl.ds(pl.multiple_of(128 * k + 16 * pair, 16), 16)
-                        pieces[at, 128 * (2 * d + c) : 128 * (2 * d + c + 1)] = joined.astype(bf16)
-
-        @pl.loop(0, 8)
-        def _(i):
-            at = pl.ds(pl.multiple_of(256 * i, 256), 256)
-            index = lax.broadcasted_iota(jnp.int32, (256, 896), 0) + 256 * i
-            hot = (index == ids_lane[group]).astype(f32).astype(bf16)
-            term = nn(hot, pieces[...])
-            if group == 0:
-                total[at, :] = term
-            else:
-                total[at, :] += term
-
-    def spread(h):
+                        pieces[at, 128 * c : 128 * (c + 1)] = joined.astype(bf16)
+
+            @pl.loop(0, 8)
+            def _(i):
+                at = pl.ds(pl.multiple_of(256 * i, 256), 256)
+                index = lax.broadcasted_iota(jnp.int32, (256, 896), 0) + 256 * i
+                hot = (index == ids_lane[group]).astype(f32).astype(bf16)
+                term = nn(hot, pieces[...])
+                if group == 0:
+                    total[at, :] = term
+                else:
+                    total[at, :] += term
+
+    def spread(q):
+        out = out_x.at[q % 2]
         for p in range(planes):
-            out_x[p] = total[512 * p : 512 * (p + 1), :].astype(bf16)
-        in_x[h, plane] = out_x[plane]
-        send_all(lambda to: out_x.at[to], in_x.at[h, plane], send_x.at[h], recv_x.at[h], "grp")
-
-    def finish(h):
-        wait_all(in_x.at[h], send_x.at[h], recv_x.at[h], "grp")
-        added = in_x[h, 0].astype(f32)
+            out[p] = total[512 * p : 512 * (p + 1), :].astype(bf16)
+        in_x[q, plane] = out[plane]
+        send_all(lambda to: out.at[to], in_x.at[q, plane], send_x.at[q], recv_x.at[q], "grp")
+
+    def finish(q):
+        wait_all(in_x.at[q], send_x.at[q], recv_x.at[q], "grp")
+        added = in_x[q, 0].astype(f32)
         for p in range(1, planes):
-            added = added + in_x[h, p].astype(f32)
-        for d in range(2):
-            joined = jnp.concatenate(
-                [
-                    added[:, 128 * (2 * d + c) : 128 * (2 * d + c + 1)].reshape(n, 8, 128)
-                    for c in range(2)
-                ],
-                axis=1,
-            )
-            out_f[h, :, :, 128 * d : 128 * (d + 1)] = joined.astype(bf16)
-        send_all(lambda to: out_f.at[h, to], in_f.at[h, me], send_o.at[h], recv_o.at[h], "blk")
-        in_f[h, me] = out_f[h, me]
-
-    def deliver(h):
-        wait_all(in_f.at[h], send_o.at[h], recv_o.at[h], "blk")
-        for d in range(2):
-            lanes = slice(128 * d, 128 * (d + 1))
-            added = in_f[h, 0:few, :, lanes].astype(f32) + in_f[h, few:n, :, lanes].astype(f32)
-            wide[h, 512 * d : 512 * (d + 1), :] = added.reshape(16 * few, 128)
-            for s in range(8):
-                for c in range(2):
-                    at = 256 * s + 128 * h + 64 * d + 32 * c
-                    got = wide[h, pl.ds(512 * d + 8 * c + s, few, stride=16), :]
-                    out_ref[at : at + 32, :] = (got + diag[at : at + 32, :]).astype(bf16)
+            added = added + in_x[q, p].astype(f32)
+        joined = jnp.concatenate(
+            [added[:, 128 * c : 128 * (c + 1)].reshape(n, 8, 128) for c in range(2)], axis=1
+        )
+        out_f[q] = joined.astype(bf16)
+        send_all(lambda to: out_f.at[q, to], in_f.at[q, me], send_o.at[q], recv_o.at[q], "blk")
+        in_f[q, me] = out_f[q, me]
+
+    def deliver(q):
+        wait_all(in_f.at[q], send_o.at[q], recv_o.at[q], "blk")
+        added = in_f[q, 0:few].astype(f32) + in_f[q, few:n].astype(f32)
+        wide[q, 0:512, :] = added.reshape(16 * few, 128)
+        for s in range(8):
+            for c in range(2):
+                at = 256 * s + 64 * q + 32 * c
+                got = wide[q, pl.ds(8 * c + s, few, stride=16), :]
+                out_ref[at : at + 32, :] = (got + diag[at : at + 32, :]).astype(bf16)
 
     parts(0)
     parts(1)
+    bulk(sent, n - sent)
+    collect(0)
+    spread(0)
+    collect(1)
+    spread(1)
+    finish(0)
+    collect(2)
+    spread(2)
+    finish(1)
+    collect(3)
+    spread(3)
     move_rows()
-    collect(0, 0)
-    collect(0, 1)
-    spread(0)
-    collect(1, 0)
-    collect(1, 1)
-    finish(0)
-    spread(1)
-    finish(1)
-    deliver(0)
-    deliver(1)
-    for h in range(2):
-        messages(out_h.at[h], few - 1, send_m.at[h], recv_m.at[h, 0], "blk").wait_send()
+    finish(2)
+    finish(3)
+    for q in range(4):
+        deliver(q)
+    for q in range(4):
+        messages(out_h.at[q], few - 1, send_m.at[q], recv_m.at[q, 0], "blk").wait_send()
 
 
 def whole(inv, posn, msg, x, ownp, logw, logwt, srcf, tfeats, cid):
@@ -621,14 +621,14 @@
         ((8, 7, 256, 128), bf16),
         ((7, 16 * n, 128), f32),
         ((2048, 128), f32),
-        ((2, n // 2, 16, 1792), bf16),
-        ((2, n // 2, 16, 1792), bf16),
-        ((896, 512), bf16),
-        ((planes * 8 * n, 512), f32),
-        ((planes, 8 * n, 512), bf16),
-        ((2, planes, 8 * n, 512), bf16),
-        ((2, n, 16, 256), bf16),
-        ((2, n, 16, 256), bf16),
+        ((4, n // 2, 16, 896), bf16),
+        ((4, n // 2, 16, 896), bf16),
+        ((896, 256), bf16),
+        ((planes * 8 * n, 256), f32),
+        ((2, planes, 8 * n, 256), bf16),
+        ((4, planes, 8 * n, 256), bf16),
+        ((4, n, 16, 128), bf16),
+        ((4, n, 16, 128), bf16),
     ]
     dma = pltpu.SemaphoreType.DMA
     return pl.pallas_call(
@@ -647,8 +647,8 @@
         + [dma] * 14
         + [dma] * 4
         + [dma((2,))] * 2
-        + [dma((2,)), dma((2, 2))]
-        + [dma((2,))] * 4,
+        + [dma((4,)), dma((4, 2))]
+        + [dma((4,))] * 4,
         compiler_params=params(cid, 62),
     )(inv, posn, msg, x, ownp, logw, logwt, srcf, tfeats)
 

time: 298 us -> 274 us (0.919)
  Pallas kernels: 289 us -> 265 us
    pallas_call x1, Pallas kernels: 289 us -> 265 us  [whole(): pl.pallas_call(whole_kernel, out_shape=(jax.ShapeDtypeStruct((2048, 128),...]
where the time goes in v6:
time: 274 us; the launch traced here: 273 us
  Pallas kernels  265 us (97%)
  local copies, waits for them, and re-layouts  5.65 us (2%)
    pallas_call x1, Pallas kernels, whole(): pl.pallas_call(whole_kernel, out_shape=(jax.ShapeDtypeStruct((2048, 128),...  265 us

profile of v6, /device:TPU:1, one launch (start us, length us, event | category | flops | bytes accessed | tf_op | source)
XLA Modules:
  0.0 273.2 jit_solution(7360392946260627257)
XLA Ops:
  0.6 0.1 pad.2.clone
  0.7 0.8 copy.14
  1.5 0.1 reshape.112
  1.6 0.2 convert_reduce_fusion
  1.7 0.8 copy.15
  2.5 0.1 reshape.113
  2.6 0.0 copy-start
  2.6 0.6 select_reduce_fusion
  3.3 0.1 reshape.114
  3.4 0.7 add_add_fusion
  4.1 0.0 copy-done
  4.1 265.4 %shard_map.95 = (bf16[2048,128]{1,0:T(8,128)(2,1)}, bf16[2048,128]{1,0:T(8,128)(2,1)}) custom-call(s32[128]{0:T(128)} %get-tuple-element.3.inv, s32[56]{0:T(128)} %copy-done, s32[64,1,128]{2,1,0:T(1,128)} %bitcast.9, bf16[64,2048]{1,0:T(8,128)(2,1)} %bitcast.8, bf16[64,8192]{1,0:T(8,128)(2,1)} %bitcast.7, f32[16,128]{1,0:T(8,128)} %bitcast.11, ...), custom_call_target="tpu_custom_call" | custom-call | tf_op jit(solution)/shard_map/pallas_call | solution.py:634
  269.5 1.9 copy.18
  271.3 1.9 copy.19
  (4 shorter events, 0.0 us)
Async XLA Ops:
  2.6 1.5 copy-start

commit v7 on v6

--- a/solution.py
+++ b/solution.py
@@ -132,7 +132,7 @@
     turned_x, turned_own, logwt, x_ref, own_ref, srcf_ref, ownf_ref, stripe_p, stripe_f, logw_col, alpha_ref,
     ids_all, ids_sel, ids_wide, ids_lane, asked, table_p, table_f, halves_p, halves_f, out_p, in_p,
     far_ref, packed_ref, got_ref, scores, beta_ref, lse_ref,
-    padded, out1, in1, own, upper, outx, inx, both, out2, in2,
+    padded, out1, in1, own, upper, outx, inx, both, out2, in2, out3, in3,
     farf, wide, diag, out_h, in_h, pieces, total, out_x, in_x, out_f, in_f,
     local, send_i, recv_i, send_p, recv_p, send_t, recv_t, send_f, recv_f,
     send1, recv1, send3, recv3, send_s, recv_s,
@@ -325,6 +325,8 @@
                 )
 
     def potentials(turn, start, counts):
+        answer, answers = (out3, in3) if turn == 0 else (out2, in2)
+
         @pl.loop(0, n)
         def _(s):
             to = lax.rem(me + s, n)
@@ -383,17 +385,18 @@
         def _(m):
             for c in range(2):
                 slot = asked[m, 0, 56 + c]
-                out2[m, 2 * c : 2 * c + 1, :] = both[0, pl.ds(slot, 1), :]
-                out2[m, 2 * c + 1 : 2 * c + 2, :] = both[1, pl.ds(slot, 1), :]
+                answer[m, c : c + 1, :] = both[0, pl.ds(slot, 1), :]
+                if turn == 1:
+                    answer[m, c + 2 : c + 3, :] = both[1, pl.ds(slot, 1), :]
 
             @pl.when(m > 0)
             def _():
                 to = lax.rem(me + n - away(m), n)
-                remote(out2.at[m], in2.at[me], send3, recv3, "blk", to).start()
+                remote(answer.at[m], answers.at[me], send3, recv3, "blk", to).start()
 
         bulk(start + counts[0], counts[1])
-        in2[me] = out2[0]
-        wait_all(in2, send3, recv3, "blk")
+        answers[me] = answer[0]
+        wait_all(answers, send3, recv3, "blk")
         for r in range(rows):
             beta_ref[8 * r : 8 * r + 1, :] = both[0, pl.ds(plane * rows + r, 1), :]
             lse_ref[8 * r : 8 * r + 1, :] = both[1, pl.ds(plane * rows + r, 1), :]
@@ -402,8 +405,9 @@
                 owner = where // 2
                 rank = where % 2
                 row = 8 * r + k + 1
-                beta_ref[row : row + 1, :] = in2[owner, pl.ds(2 * rank, 1), :]
-                lse_ref[row : row + 1, :] = in2[owner, pl.ds(2 * rank + 1, 1), :]
+                beta_ref[row : row + 1, :] = answers[owner, pl.ds(rank, 1), :]
+                if turn == 1:
+                    lse_ref[row : row + 1, :] = answers[owner, pl.ds(rank + 2, 1), :]
 
     sent = 0
     for turn in range(2):
@@ -618,6 +622,8 @@
         ((2, held + 8, block), f32),
         ((n, 4, block), f32),
         ((n, 4, block), f32),
+        ((n, 2, block), f32),
+        ((n, 2, block), f32),
         ((8, 7, 256, 128), bf16),
         ((7, 16 * n, 128), f32),
         ((2048, 128), f32),

time: 274 us -> 274 us (level)
  no operation moved by 1% of the time
where the time goes in v7:
time: 274 us; the launch traced here: 273 us
  Pallas kernels  265 us (97%)
  local copies, waits for them, and re-layouts  5.65 us (2%)
    pallas_call x1, Pallas kernels, whole(): pl.pallas_call(whole_kernel, out_shape=(jax.ShapeDtypeStruct((2048, 128),...  265 us

profile of v7, /device:TPU:1, one launch (start us, length us, event | category | flops | bytes accessed | tf_op | source)
XLA Modules:
  0.0 273.3 jit_solution(13934277119771474535)
XLA Ops:
  0.6 0.1 pad.2.clone
  0.7 0.8 copy.14
  1.5 0.1 reshape.112
  1.6 0.2 convert_reduce_fusion
  1.7 0.8 copy.15
  2.5 0.1 reshape.113
  2.6 0.0 copy-start
  2.6 0.6 select_reduce_fusion
  3.3 0.1 reshape.114
  3.4 0.7 add_add_fusion
  4.1 0.0 copy-done
  4.1 265.4 %shard_map.95 = (bf16[2048,128]{1,0:T(8,128)(2,1)}, bf16[2048,128]{1,0:T(8,128)(2,1)}) custom-call(s32[128]{0:T(128)} %get-tuple-element.3.inv, s32[56]{0:T(128)} %copy-done, s32[64,1,128]{2,1,0:T(1,128)} %bitcast.9, bf16[64,2048]{1,0:T(8,128)(2,1)} %bitcast.8, bf16[64,8192]{1,0:T(8,128)(2,1)} %bitcast.7, f32[16,128]{1,0:T(8,128)} %bitcast.11, ...), custom_call_target="tpu_custom_call" | custom-call | tf_op jit(solution)/shard_map/pallas_call | solution.py:640
  269.5 1.9 copy.18
  271.4 1.9 copy.19
  (4 shorter events, 0.0 us)
Async XLA Ops:
  2.6 1.5 copy-start
